TPU v7x, 768 devices: a whole 4x8x12 slice. The times are simulated.
768 devices in a mesh: replica: 4 (over x_lo, core), shard: 192 (over z, x_hi, y).
Axes of the slice: x: 4 (x_hi: 2, x_lo: 2; x = x_hi * 2 + x_lo), y: 8, z: 12, core: 2. Of those that a mesh axis runs over, the one named last changes fastest.
Arguments:
- activations: bfloat16 [4, 49152, 2, 192], P('replica', 'shard'), may hold values from -0.02734375 to 0.02734375
- out_grads: bfloat16 [4, 49152, 2, 4096], P('replica', 'shard'), may hold values from -6 to 6
- momentum: float32 [4, 192, 64, 128], P('replica', 'shard'), may hold values from -6 to 6
- band_idx: int32 [192, 2, 32], P('shard'), may hold values from 0 to 4095, as said below
Outputs:
- new_momentum: float32 [4, 192, 64, 128], P('replica', 'shard')
- update: float32 [192, 64, 128], P('shard')
Inputs may be any that keep to these rules, and one draw needn't show every extreme that they name: `band_idx`: for each group and layer the 32 entries are distinct indices u * 64 + v of coefficients of the group's transform.
All inputs are finite; a program needn't handle non-finite values.
Results may differ from a plain program's by a relative error of at most 0.0003.
Values sent between devices are 32-bit elements; how exact they have to be, the bound alone decides.
No kernel may reach another device: no remote copies, remote signals or barrier semaphores. Data moves between devices by JAX's collectives and lax.ppermute only.
A program may use at most 64 MiB of HBM per device.

v0:
```python
import jax
import jax.numpy as jnp
from jax import lax
from jax.sharding import PartitionSpec as P

MOMENTUM_DECAY = 0.999
DECODE_GAIN = 8.0


def dct_table(length):
    freq = jnp.arange(length, dtype=jnp.float32)[:, None]
    places = jnp.arange(length, dtype=jnp.float32)[None, :]
    scales = jnp.where(freq == 0, jnp.sqrt(1.0 / length), jnp.sqrt(2.0 / length)).astype(
        jnp.float32
    )
    return scales * jnp.cos(jnp.pi * (2.0 * places + 1.0) * freq / (2.0 * length))


def forward(tiles, matrix, layer_count):
    side = matrix.shape[0]
    left = jnp.einsum("ux,qxy->quy", matrix, tiles, precision=lax.Precision.HIGHEST)
    left = left.reshape(left.shape[0], side, layer_count, side)
    both = jnp.einsum("quly,vy->qulv", left, matrix, precision=lax.Precision.HIGHEST)
    return both.reshape(tiles.shape)


def inverse(coeffs, matrix, layer_count):
    side = matrix.shape[0]
    left = jnp.einsum("ux,quy->qxy", matrix, coeffs, precision=lax.Precision.HIGHEST)
    left = left.reshape(left.shape[0], side, layer_count, side)
    both = jnp.einsum("qxlv,vy->qxly", left, matrix, precision=lax.Precision.HIGHEST)
    return both.reshape(coeffs.shape)


def flat_positions(band_idx, side, layer_count):
    rows_u = band_idx // side
    cols_v = band_idx % side
    layer_ids = jnp.arange(layer_count, dtype=jnp.int32)[None, :, None]
    places = rows_u * (layer_count * side) + layer_ids * side + cols_v
    return places.reshape(band_idx.shape[0], -1)


def place_band(values, positions, total):
    group_ids = jnp.arange(positions.shape[0], dtype=jnp.int32)[:, None]
    empty = jnp.zeros((positions.shape[0], total), jnp.float32)
    return empty.at[group_ids, positions].set(values)


def local(activations, out_grads, momentum, band_idx):
    act_rows = activations[0]
    grad_out = out_grads[0]
    own_momentum = momentum[0]
    group_side = own_momentum.shape[1]
    layer_count = own_momentum.shape[2] // group_side
    row_blocks = act_rows.shape[2] // group_side
    col_blocks = grad_out.shape[2] // group_side
    owned = own_momentum.shape[0]
    pieces = []
    for layer_idx in range(layer_count):
        whole = jnp.dot(
            act_rows[:, layer_idx, :].T,
            grad_out[:, layer_idx, :],
            preferred_element_type=jnp.float32,
        )
        whole = whole.reshape(row_blocks, group_side, col_blocks, group_side).transpose(0, 2, 1, 3)
        pieces.append(whole.reshape(row_blocks * col_blocks, group_side, group_side))
    partial_value = jnp.concatenate(pieces, axis=2)
    gradient = lax.psum_scatter(partial_value, "shard", scatter_dimension=0, tiled=True)
    momentum_pre = MOMENTUM_DECAY * own_momentum + gradient
    matrix = dct_table(group_side)
    positions = flat_positions(band_idx, group_side, layer_count)
    total = group_side * layer_count * group_side
    coeffs = forward(momentum_pre, matrix, layer_count)
    band_vals = jnp.take_along_axis(coeffs.reshape(owned, total), positions, axis=1)
    placed = place_band(band_vals, positions, total).reshape(coeffs.shape)
    new_momentum = momentum_pre - inverse(placed, matrix, layer_count)
    every_band = lax.all_gather(band_vals[None], "replica", axis=0, tiled=True)
    mean_band = jnp.sum(every_band, axis=0) / lax.axis_size("replica")
    placed_mean = place_band(mean_band, positions, total).reshape(coeffs.shape)
    update = DECODE_GAIN * inverse(placed_mean, matrix, layer_count)
    return (new_momentum[None], update)


def solution(mesh):
    return jax.shard_map(
        local,
        mesh=mesh,
        in_specs=(
            P("replica", "shard", None, None),
            P("replica", "shard", None, None),
            P("replica", "shard", None, None),
            P("shard", None, None),
        ),
        out_specs=(P("replica", "shard", None, None), P("shard", None, None)),
        check_vma=False,
    )
```

profile of v0, /device:TPU:1, one launch (start us, length us, event | category | flops | bytes accessed | tf_op | source)
XLA Modules:
  0.0 1139.8 jit_solution(2158125471167956870)
XLA Ops:
  7.2 5.1 copy.38
  12.3 1.6 slice_bitcast_fusion.1
  13.9 4.1 copy.21
  18.0 2.5 copy.22
  20.5 2.7 fusion.45
  23.3 1.0 fusion.46
  24.3 4.3 pad_maximum_fusion
  28.7 0.6 copy-done.3
  29.8 932.0 %reduce-scatter.2.cloned.1.call-done = f32[1,64,128]{2,1,0:T(8,128)} async-done(((f32[192,64,128]{2,1,0:T(8,128)}), f32[1,64,128]{2,1,0:T(8,128)}) %reduce-scatter.2.cloned.1.call-update) | async-done | bytes 32784 | tf_op jit(solution)/shard_map/reduce_scatter | solution.py:68
  961.8 1.0 convolution_bitcast_fusion.2
  962.8 0.1 reshape.332
  962.9 0.3 fusion.3
  963.3 0.1 reshape.340
  963.4 0.8 gather_fusion
  964.2 0.8 scatter_custom_fusion
  965.1 0.4 convolution_bitcast_fusion.1
  965.5 0.3 fusion.1
  965.9 0.1 reshape.336
  966.0 163.1 %all_gather.3 = f32[4,1,64]{2,1,0:T(1,128)S(1)} all-gather(f32[1,1,64]{2,1,0:T(1,128)S(1)} %and_select_fusion), channel_id=1, replica_groups=mesh['replica'=4,'shard'=192] {'replica'}, dimensions={0}, use_global_device_ids=true | all-gather | bytes 1280 | tf_op jit(solution)/shard_map/all_gather | solution.py:77
  1129.2 0.8 scatter_custom_fusion.1
  1130.0 0.4 convolution_bitcast_fusion
  1130.5 0.3 convolution_multiply_fusion
  1130.9 0.7 mul.178
  1131.6 1.4 subtract_bitcast_fusion
  (31 shorter events, 0.9 us)
Async XLA Ops:
  7.2 954.6 %reduce-scatter.2.cloned.1.call-start = ((), (), s32[]{:S(2)}) async-start(), calls=%async_computation.1 | async-start | bytes 6324224 | tf_op jit(solution)/shard_map/reduce_scatter | solution.py:68
  13.9 4.1 copy-start.1
  20.5 2.7 copy-start
  28.6 0.7 copy-start.3
  28.6 933.1 %copy-start.2 = (f32[1,1,64,128]{3,2,1,0:T(8,128)S(1)}, f32[1,1,64,128]{3,2,1,0:T(8,128)}, u32[]{:S(2)}) copy-start(f32[1,1,64,128]{3,2,1,0:T(8,128)} %param.6) | copy-start | bytes 98308
Sparse Core Ops, SparseCore 0:
  28.8 932.9 reduce-scatter.1
where the time goes:
time: 1140 us
  waiting for transfers between devices  932 us (82%)
  blocking collectives  163 us (14%)
  local copies, waits for them, and re-layouts  18.1 us (2%)
  between operations  14.2 us (1%)
    reduce_scatter x1, waiting for transfers between devices, local(): lax.psum_scatter(partial_value, 'shard', scatter_dimension=0, tiled=True)  932 us
    all_gather x1, blocking collectives, local(): every_band = lax.all_gather(band_vals[None], 'replica', axis=0, tiled=True)  163 us
  transfers between devices with their start and end apart: 1, of which 1 were waited for; matrix products, arithmetic and copies ran while one was open for 0% of the time, Pallas kernels for 0%

commit v1 on v0

v1 whole, which is shorter than its diff:
```python
import functools

import jax
import jax.numpy as jnp
import numpy as np
from jax import lax
from jax.experimental import pallas as pl
from jax.experimental.pallas import tpu as pltpu
from jax.sharding import PartitionSpec as P

MOMENTUM_DECAY = 0.999
DECODE_GAIN = 8.0
SIDE = 64
LAYERS = 2
WIDE = SIDE * LAYERS
BAND = 32
REPLICAS = 4
CHUNK = 512
HIGHEST = lax.Precision.HIGHEST


def flat(x_lo, core, z, x_hi, y):
    return ((x_lo * 2 + core) * 12 + z % 12) * 16 + x_hi * 8 + y % 8


def stage_groups():
    first, second, third = [], [], []
    for x_lo in range(2):
        for core in range(2):
            for x_hi in range(2):
                for z in range(core, 12 + core, 2):
                    for y in range(core, 8 + core, 2):
                        pz = sorted((z % 12, (z + 1) % 12), key=lambda v: v % 2)
                        py = sorted((y % 8, (y + 1) % 8), key=lambda v: v % 2)
                        first.append([flat(x_lo, core, a, x_hi, b) for a in pz for b in py])
            for z0 in range(2):
                for y0 in range(2):
                    for m in range(core, 6 + core, 2):
                        for n in range(core, 4 + core, 2):
                            pz = sorted((m % 6, (m + 1) % 6), key=lambda v: v % 2)
                            py = sorted((n % 4, (n + 1) % 4), key=lambda v: v % 2)
                            second.append(
                                [
                                    flat(x_lo, core, 2 * a + z0, h, 2 * b + y0)
                                    for h in range(2)
                                    for a in pz
                                    for b in py
                                ]
                            )
            for x_hi in range(2):
                for z in range(4):
                    for y in range(4):
                        third.append(
                            [flat(x_lo, core, 4 * a + z, x_hi, 4 * b + y) for a in range(3) for b in range(2)]
                        )
    return first, second, third


def dct_matrix():
    u = np.arange(SIDE, dtype=np.float64)[:, None]
    x = np.arange(SIDE, dtype=np.float64)[None, :]
    scale = np.where(u == 0, np.sqrt(1.0 / SIDE), np.sqrt(2.0 / SIDE))
    return (scale * np.cos(np.pi * (2.0 * x + 1.0) * u / (2.0 * SIDE))).astype(np.float32)


def terms_kernel(act_ref, grad_ref, out_ref, left_ref):
    tokens = grad_ref.shape[1]
    rows = act_ref.shape[1]

    @pl.when(pl.program_id(0) == 0)
    def _():
        token = lax.broadcasted_iota(jnp.int32, (tokens, tokens * LAYERS), 0)
        place = lax.broadcasted_iota(jnp.int32, (tokens, tokens * LAYERS), 1)
        for layer in range(LAYERS):
            spread = (place == token * LAYERS + layer).astype(jnp.float32).astype(act_ref.dtype)
            left_ref[layer * rows : (layer + 1) * rows] = jnp.dot(
                act_ref[layer], spread, preferred_element_type=jnp.float32
            ).astype(act_ref.dtype)

    rhs = grad_ref[0].reshape(tokens * LAYERS, CHUNK)
    both = jnp.dot(left_ref[...], rhs, preferred_element_type=jnp.float32)
    low = lax.broadcasted_iota(jnp.int32, (SIDE, WIDE), 1) < SIDE
    for a in range(rows // SIDE):
        for pair in range(CHUNK // WIDE):
            cols = slice(pair * WIDE, (pair + 1) * WIDE)
            one = both[a * SIDE : (a + 1) * SIDE, cols]
            two = both[rows + a * SIDE : rows + (a + 1) * SIDE, cols]
            even = jnp.where(low, one, pltpu.roll(two, SIDE, 1))
            odd = jnp.where(low, pltpu.roll(one, SIDE, 1), two)
            out_ref[0, 0, 0, 0, pair % 2, a, pair // 2] = even
            out_ref[0, 1, 0, 0, pair % 2, a, pair // 2] = odd


def gradient_terms(acts, grads):
    tokens, cols = grads.shape[1], grads.shape[3]
    rows = acts.shape[3]
    shape = (2, 2, 2, 2, 2, rows // SIDE, 2, SIDE, WIDE)
    return pl.pallas_call(
        terms_kernel,
        grid=(cols // CHUNK,),
        in_specs=[
            pl.BlockSpec((LAYERS, rows, tokens), lambda c: (0, 0, 0)),
            pl.BlockSpec((1, tokens, LAYERS, CHUNK), lambda c: (0, 0, 0, c)),
        ],
        out_specs=pl.BlockSpec(
            (1, 2, 1, 1, 2, rows // SIDE, 2, SIDE, WIDE),
            lambda c: ((c // 2) % 2, 0, c % 2, c // 4, 0, 0, 0, 0, 0),
        ),
        out_shape=jax.ShapeDtypeStruct(shape, jnp.float32),
        scratch_shapes=[pltpu.VMEM((LAYERS * rows, tokens * LAYERS), acts.dtype)],
        name="terms",
    )(acts[0].transpose(1, 2, 0), grads)


def dot(a, b, dims):
    return lax.dot_general(a, b, (dims, ((), ())), precision=HIGHEST, preferred_element_type=jnp.float32)


def one_hots(idx_ref):
    places = lax.broadcasted_iota(jnp.int32, (BAND, SIDE), 1)
    rows, cols = [], []
    for layer in range(LAYERS):
        idx = idx_ref[layer]
        rows.append((idx // SIDE == places).astype(jnp.float32))
        cols.append((idx % SIDE == places).astype(jnp.float32))
    masks = [dot(r, c, ((0,), (0,))) for r, c in zip(rows, cols)]
    return jnp.concatenate(masks, axis=1)


def encode_kernel(parts_ref, mom_ref, idx_ref, left_ref, wide_ref, new_ref, sent_ref):
    gradient = parts_ref[0]
    for k in range(1, parts_ref.shape[0]):
        gradient = gradient + parts_ref[k]
    pre = MOMENTUM_DECAY * mom_ref[0, 0] + gradient
    mask = one_hots(idx_ref)
    coeffs = dot(dot(left_ref[...], pre, ((1,), (0,))), wide_ref[...], ((1,), (1,)))
    kept = coeffs * mask
    for k in range(REPLICAS):
        sent_ref[k] = kept
    back = dot(dot(left_ref[...], kept, ((0,), (0,))), wide_ref[...], ((1,), (0,)))
    new_ref[0, 0] = pre - back


def decode_kernel(every_ref, left_ref, wide_ref, out_ref):
    mean = ((every_ref[0] + every_ref[1]) + (every_ref[2] + every_ref[3])) / REPLICAS
    back = dot(dot(left_ref[...], mean, ((0,), (0,))), wide_ref[...], ((1,), (0,)))
    out_ref[0] = DECODE_GAIN * back


def matrices():
    side = dct_matrix()
    return jnp.asarray(side), jnp.asarray(np.kron(np.eye(LAYERS, dtype=np.float32), side))


def encode(parts, momentum, band_idx):
    return pl.pallas_call(
        encode_kernel,
        out_shape=(
            jax.ShapeDtypeStruct((1, 1, SIDE, WIDE), jnp.float32),
            jax.ShapeDtypeStruct((REPLICAS, SIDE, WIDE), jnp.float32),
        ),
        name="encode",
    )(parts, momentum, band_idx.reshape(LAYERS, BAND, 1), *matrices())


def decode(every):
    return pl.pallas_call(
        decode_kernel,
        out_shape=jax.ShapeDtypeStruct((1, SIDE, WIDE), jnp.float32),
        name="decode",
    )(every, *matrices())


def local(acts, grads, momentum, band_idx):
    first, second, third = stage_groups()
    axes = ("replica", "shard")
    exchange = functools.partial(lax.all_to_all, axis_name=axes, split_axis=0, concat_axis=0, tiled=True)
    terms = gradient_terms(acts, grads).reshape(4, 48, SIDE, WIDE)
    terms = exchange(terms, axis_index_groups=first)
    terms = jnp.sum(terms, axis=0).reshape(8, 6, SIDE, WIDE)
    terms = exchange(terms, axis_index_groups=second)
    terms = jnp.sum(terms, axis=0)
    terms = exchange(terms, axis_index_groups=third)
    new_momentum, sent = encode(terms, momentum, band_idx)
    every = lax.all_to_all(sent, "replica", split_axis=0, concat_axis=0, tiled=True)
    update = decode(every)
    return (new_momentum, update)


def solution(mesh):
    return jax.shard_map(
        local,
        mesh=mesh,
        in_specs=(
            P("replica", "shard", None, None),
            P("replica", "shard", None, None),
            P("replica", "shard", None, None),
            P("shard", None, None),
        ),
        out_specs=(P("replica", "shard", None, None), P("shard", None, None)),
        check_vma=False,
    )
```

time: 1140 us -> 142 us (0.12)
  waiting for transfers between devices: 932 us -> 16.4 us
  blocking collectives: 163 us -> 98.7 us
  local copies, waits for them, and re-layouts: 18.1 us -> 1.39 us
  Pallas kernels: 0 us -> 13.9 us
  between operations: 14.2 us -> 0.65 us
    reduce_scatter x1 -> x0, waiting for transfers between devices: 932 us -> none  [local(): lax.psum_scatter(partial_value, 'shard', scatter_dimension=0, tiled=True)]
    all_gather x1 -> x0, blocking collectives: 163 us -> none  [local(): every_band = lax.all_gather(band_vals[None], 'replica', axis=0, tiled=True)]
    all_to_all x0 -> x3, blocking collectives: none -> 98.7 us  [the longest x1 57.4 us: local(): terms = exchange(terms, axis_index_groups=first)]
    all_to_all x0 -> x1, waiting for transfers between devices: none -> 16.4 us  [local(): terms = exchange(terms, axis_index_groups=third)]
    pallas_call x0 -> x3, Pallas kernels: none -> 13.9 us  [the longest x1 9.28 us: gradient_terms(): pl.pallas_call(terms_kernel, grid=(cols // CHUNK,), in_specs=[pl.BlockSpe...]
  transfers between devices with their start and end apart: 1 -> 1, of which waited for: 1 -> 1; matrix products, arithmetic and copies ran while one was open for 0% -> 1% of each run, Pallas kernels for 0% -> 0%
where the time goes in v1:
time: 142 us; the launch traced here: 141 us
  blocking collectives  98.7 us (70%)
  waiting for transfers between devices  16.4 us (12%)
  Pallas kernels  13.9 us (10%)
  starting transfers between devices  5.83 us (4%)
  other arithmetic  4.39 us (3%)
    all_to_all x1, blocking collectives, local(): terms = exchange(terms, axis_index_groups=first)  57.4 us
    all_to_all x1, blocking collectives, local(): terms = exchange(terms, axis_index_groups=second)  33.3 us
    all_to_all x1, waiting for transfers between devices, local(): terms = exchange(terms, axis_index_groups=third)  16.4 us
    pallas_call x1, Pallas kernels, gradient_terms(): pl.pallas_call(terms_kernel, grid=(cols // CHUNK,), in_specs=[pl.BlockSpe...  9.28 us
    all_to_all x1, blocking collectives, local(): lax.all_to_all(sent, 'replica', split_axis=0, concat_axis=0, tiled=True)  8.08 us
    all_to_all x1, starting transfers between devices, local(): terms = exchange(terms, axis_index_groups=third)  5.83 us
    reduce_sum x1, other arithmetic, local(): terms = jnp.sum(terms, axis=0).reshape(8, 6, SIDE, WIDE)  3.62 us
  transfers between devices with their start and end apart: 1, of which 1 were waited for; matrix products, arithmetic and copies ran while one was open for 1% of the time, Pallas kernels for 0%

profile of v1, /device:TPU:1, one launch (start us, length us, event | category | flops | bytes accessed | tf_op | source)
XLA Modules:
  0.0 141.3 jit_solution(11360231670651830474)
XLA Ops:
  0.6 9.3 %terms.1 = f32[2,2,2,2,2,3,2,64,128]{8,7,6,5,4,3,2,1,0:T(8,128)} custom-call(bf16[2,192,256]{2,1,0:T(8,128)(2,1)} %bitcast.8, bf16[1,256,2,4096]{3,2,1,0:T(2,128)(2,1)} %grad_ref.1), custom_call_target="tpu_custom_call" | custom-call | tf_op jit(solution)/shard_map/terms/pallas_call | solution.py:98
  9.9 57.4 %all_to_all.20 = f32[4,48,64,128]{3,2,1,0:T(8,128)} all-to-all(f32[4,48,64,128]{3,2,1,0:T(8,128)} %bitcast.6), channel_id=1, replica_groups={{0,1,16,17},{2,3,18,19},{4,5,20,21},{6,7,22,23},{32,33,48,49},{34,35,50..., dimensions={0} | all-to-all | bytes 12582912 | tf_op jit(solution)/shard_map/all_to_all | solution.py:179
  67.3 3.6 %reduce_sum.18 = f32[48,64,128]{2,1,0:T(8,128)S(1)} reduce(f32[4,48,64,128]{3,2,1,0:T(8,128)} %all_to_all.20, f32[]{:T(128)} %constant.2.clone.1), dimensions={0}, to_apply=%region_0.0 | reduce | flops 1179648 | bytes 7864324 | tf_op jit(solution)/shard_map/reduce_sum | solution.py:180
  70.9 0.0 copy-start.1
  70.9 33.3 %all_to_all.21 = f32[8,6,64,128]{3,2,1,0:T(8,128)S(1)} all-to-all(f32[8,6,64,128]{3,2,1,0:T(8,128)S(1)} %bitcast.7), channel_id=1, replica_groups={{0,2,32,34,8,10,40,42},{4,6,36,38,12,14,44,46},{64,66,96,98,72,74,104,1..., dimensions={0} | all-to-all | bytes 3145728 | tf_op jit(solution)/shard_map/all_to_all | solution.py:181
  104.2 0.8 reduce_sum.19
  105.0 5.8 %all-to-all-start.2 = ((f32[6,64,128]{2,1,0:T(8,128)}), f32[6,64,128]{2,1,0:T(8,128)S(1)}, u32[]{:S(2)}, u32[]{:S(2)}) async-start(f32[6,64,128]{2,1,0:T(8,128)} %reduce_sum.19), calls=%async_computation.2 | async-start | bytes 393216 | tf_op jit(solution)/shard_map/all_to_all | solution.py:183
  110.8 0.0 copy-done.1
  110.8 0.7 copy.11.idx_ref
  111.5 16.4 %all-to-all-done.2.parts_ref = f32[6,64,128]{2,1,0:T(8,128)S(1)} async-done(((f32[6,64,128]{2,1,0:T(8,128)}), f32[6,64,128]{2,1,0:T(8,128)S(1)}, u32[]{:S(2)}, u32[]{:S(2)}) %all-to-all-start.2) | async-done | bytes 196640 | tf_op jit(solution)/shard_map/all_to_all | solution.py:183
  127.9 0.0 copy-start
  127.9 0.7 copy-done
  128.6 2.6 %encode.1 = (f32[1,1,64,128]{3,2,1,0:T(8,128)}, f32[4,64,128]{2,1,0:T(8,128)}) custom-call(f32[6,64,128]{2,1,0:T(8,128)} %copy-done, f32[1,1,64,128]{3,2,1,0:T(8,128)} %mom_ref.1, s32[2,32,1]{2,1,0:T(8,128)} %copy.11.idx_ref, f32[64,64]{1,0:T(8,128)} %constant.6.clone.left_ref, f32[128,128]{1,0:T(8,128)} %constant.7.clone.wide_ref), custom_call_target="tpu_custom_call" | custom-call | tf_op jit(solution)/shard_map/encode/pallas_call | solution.py:156
  131.2 8.1 %all_to_all.22.every_ref = f32[4,64,128]{2,1,0:T(8,128)} all-to-all(f32[4,64,128]{2,1,0:T(8,128)} %get-tuple-element.5), channel_id=1, replica_groups=mesh['replica'=4,'shard'=192] {'replica'}, dimensions={0} | all-to-all | bytes 262144 | tf_op jit(solution)/shard_map/all_to_all | solution.py:185
  139.3 2.0 %decode.1 = f32[1,64,128]{2,1,0:T(8,128)} custom-call(f32[4,64,128]{2,1,0:T(8,128)} %all_to_all.22.every_ref, f32[64,64]{1,0:T(8,128)} %constant.6.clone.left_ref, f32[128,128]{1,0:T(8,128)} %constant.7.clone.wide_ref), custom_call_target="tpu_custom_call" | custom-call | tf_op jit(solution)/shard_map/decode/pallas_call | solution.py:167
Async XLA Ops:
  70.9 39.9 %copy-start.1 = (s32[1,2,32]{2,1,0:T(2,128)S(1)}, s32[1,2,32]{2,1,0:T(2,128)}, u32[]{:S(2)}) copy-start(s32[1,2,32]{2,1,0:T(2,128)} %param.11) | copy-start | bytes 772
  105.0 23.0 %all-to-all-start.2 = ((f32[6,64,128]{2,1,0:T(8,128)}), f32[6,64,128]{2,1,0:T(8,128)S(1)}, u32[]{:S(2)}, u32[]{:S(2)}) async-start(f32[6,64,128]{2,1,0:T(8,128)} %reduce_sum.19), calls=%async_computation.2 | async-start | bytes 393216 | tf_op jit(solution)/shard_map/all_to_all | solution.py:183
  127.9 0.7 copy-start

commit v2 on v1

--- a/solution.py
+++ b/solution.py
@@ -19,20 +19,41 @@
 HIGHEST = lax.Precision.HIGHEST
 
 
+Z, Y = 12, 8
+
+
 def flat(x_lo, core, z, x_hi, y):
-    return ((x_lo * 2 + core) * 12 + z % 12) * 16 + x_hi * 8 + y % 8
+    return ((x_lo * 2 + core) * Z + z % Z) * 16 + x_hi * 8 + y % Y
+
+
+def partner(at, core, size):
+    return (((at + size - core) ^ 1) + core) % size
+
+
+def pairs(across_z, across_y):
+    return [
+        (
+            flat(x_lo, core, z, x_hi, y),
+            flat(
+                x_lo,
+                core,
+                partner(z, core, Z) if across_z else z,
+                x_hi,
+                partner(y, core, Y) if across_y else y,
+            ),
+        )
+        for x_lo in range(2)
+        for core in range(2)
+        for z in range(Z)
+        for x_hi in range(2)
+        for y in range(Y)
+    ]
 
 
 def stage_groups():
-    first, second, third = [], [], []
+    second, third = [], []
     for x_lo in range(2):
         for core in range(2):
-            for x_hi in range(2):
-                for z in range(core, 12 + core, 2):
-                    for y in range(core, 8 + core, 2):
-                        pz = sorted((z % 12, (z + 1) % 12), key=lambda v: v % 2)
-                        py = sorted((y % 8, (y + 1) % 8), key=lambda v: v % 2)
-                        first.append([flat(x_lo, core, a, x_hi, b) for a in pz for b in py])
             for z0 in range(2):
                 for y0 in range(2):
                     for m in range(core, 6 + core, 2):
@@ -53,7 +74,7 @@
                         third.append(
                             [flat(x_lo, core, 4 * a + z, x_hi, 4 * b + y) for a in range(3) for b in range(2)]
                         )
-    return first, second, third
+    return second, third
 
 
 def dct_matrix():
@@ -63,7 +84,11 @@
     return (scale * np.cos(np.pi * (2.0 * x + 1.0) * u / (2.0 * SIDE))).astype(np.float32)
 
 
-def terms_kernel(act_ref, grad_ref, out_ref, left_ref):
+def parities(place_ref):
+    return (place_ref[0] >> 4) & 1, place_ref[0] & 1
+
+
+def terms_kernel(place_ref, act_ref, grad_ref, other_ref, own_ref, left_ref):
     tokens = grad_ref.shape[1]
     rows = act_ref.shape[1]
 
@@ -80,36 +105,51 @@
     rhs = grad_ref[0].reshape(tokens * LAYERS, CHUNK)
     both = jnp.dot(left_ref[...], rhs, preferred_element_type=jnp.float32)
     low = lax.broadcasted_iota(jnp.int32, (SIDE, WIDE), 1) < SIDE
-    for a in range(rows // SIDE):
-        for pair in range(CHUNK // WIDE):
-            cols = slice(pair * WIDE, (pair + 1) * WIDE)
-            one = both[a * SIDE : (a + 1) * SIDE, cols]
-            two = both[rows + a * SIDE : rows + (a + 1) * SIDE, cols]
-            even = jnp.where(low, one, pltpu.roll(two, SIDE, 1))
-            odd = jnp.where(low, pltpu.roll(one, SIDE, 1), two)
-            out_ref[0, 0, 0, 0, pair % 2, a, pair // 2] = even
-            out_ref[0, 1, 0, 0, pair % 2, a, pair // 2] = odd
-
-
-def gradient_terms(acts, grads):
+
+    def write(even_ref, odd_ref):
+        for a in range(rows // SIDE):
+            for pair in range(CHUNK // WIDE):
+                cols = slice(pair * WIDE, (pair + 1) * WIDE)
+                one = both[a * SIDE : (a + 1) * SIDE, cols]
+                two = both[rows + a * SIDE : rows + (a + 1) * SIDE, cols]
+                even_ref[0, 0, pair % 2, a, pair // 2] = jnp.where(low, one, pltpu.roll(two, SIDE, 1))
+                odd_ref[0, 0, pair % 2, a, pair // 2] = jnp.where(low, pltpu.roll(one, SIDE, 1), two)
+
+    @pl.when(parities(place_ref)[1] == 0)
+    def _():
+        write(own_ref, other_ref)
+
+    @pl.when(parities(place_ref)[1] == 1)
+    def _():
+        write(other_ref, own_ref)
+
+
+def gradient_terms(place, acts, grads, far):
     tokens, cols = grads.shape[1], grads.shape[3]
-    rows = acts.shape[3]
-    shape = (2, 2, 2, 2, 2, rows // SIDE, 2, SIDE, WIDE)
+    rows = acts.shape[1]
+    out = jax.ShapeDtypeStruct((2, 2, 2, rows // SIDE, 2, SIDE, WIDE), jnp.float32)
+    out_spec = pl.BlockSpec(
+        (1, 1, 2, rows // SIDE, 2, SIDE, WIDE), lambda c, place: (c % 2, c // 2, 0, 0, 0, 0, 0)
+    )
     return pl.pallas_call(
         terms_kernel,
-        grid=(cols // CHUNK,),
-        in_specs=[
-            pl.BlockSpec((LAYERS, rows, tokens), lambda c: (0, 0, 0)),
-            pl.BlockSpec((1, tokens, LAYERS, CHUNK), lambda c: (0, 0, 0, c)),
-        ],
-        out_specs=pl.BlockSpec(
-            (1, 2, 1, 1, 2, rows // SIDE, 2, SIDE, WIDE),
-            lambda c: ((c // 2) % 2, 0, c % 2, c // 4, 0, 0, 0, 0, 0),
+        grid_spec=pltpu.PrefetchScalarGridSpec(
+            num_scalar_prefetch=1,
+            grid=(cols // CHUNK // 2,),
+            in_specs=[
+                pl.BlockSpec((LAYERS, rows, tokens), lambda c, place: (0, 0, 0)),
+                pl.BlockSpec(
+                    (1, tokens, LAYERS, CHUNK),
+                    lambda c, place: (0, 0, 0, (c // 2) * 4 + (parities(place)[0] ^ far) * 2 + c % 2),
+                ),
+            ],
+            out_specs=[out_spec, out_spec],
+            scratch_shapes=[pltpu.VMEM((LAYERS * rows, tokens * LAYERS), acts.dtype)],
         ),
-        out_shape=jax.ShapeDtypeStruct(shape, jnp.float32),
-        scratch_shapes=[pltpu.VMEM((LAYERS * rows, tokens * LAYERS), acts.dtype)],
-        name="terms",
-    )(acts[0].transpose(1, 2, 0), grads)
+        out_shape=(out, out),
+        compiler_params=pltpu.CompilerParams(vmem_limit_bytes=16 * 2**20),
+        name="far" if far else "near",
+    )(place, acts, grads)
 
 
 def dot(a, b, dims):
@@ -159,6 +199,7 @@
             jax.ShapeDtypeStruct((1, 1, SIDE, WIDE), jnp.float32),
             jax.ShapeDtypeStruct((REPLICAS, SIDE, WIDE), jnp.float32),
         ),
+        compiler_params=pltpu.CompilerParams(vmem_limit_bytes=4 * 2**20),
         name="encode",
     )(parts, momentum, band_idx.reshape(LAYERS, BAND, 1), *matrices())
 
@@ -167,17 +208,23 @@
     return pl.pallas_call(
         decode_kernel,
         out_shape=jax.ShapeDtypeStruct((1, SIDE, WIDE), jnp.float32),
+        compiler_params=pltpu.CompilerParams(vmem_limit_bytes=4 * 2**20),
         name="decode",
     )(every, *matrices())
 
 
 def local(acts, grads, momentum, band_idx):
-    first, second, third = stage_groups()
+    second, third = stage_groups()
     axes = ("replica", "shard")
     exchange = functools.partial(lax.all_to_all, axis_name=axes, split_axis=0, concat_axis=0, tiled=True)
-    terms = gradient_terms(acts, grads).reshape(4, 48, SIDE, WIDE)
-    terms = exchange(terms, axis_index_groups=first)
-    terms = jnp.sum(terms, axis=0).reshape(8, 6, SIDE, WIDE)
+    place = lax.axis_index(axes)[None]
+    acts = acts[0].transpose(1, 2, 0)
+    diagonal, across_z = gradient_terms(place, acts, grads, 1)
+    across_y, own = gradient_terms(place, acts, grads, 0)
+    diagonal = lax.ppermute(diagonal, axes, pairs(True, True))
+    across_z = lax.ppermute(across_z, axes, pairs(True, False))
+    across_y = lax.ppermute(across_y, axes, pairs(False, True))
+    terms = ((own + across_y) + (across_z + diagonal)).reshape(8, 6, SIDE, WIDE)
     terms = exchange(terms, axis_index_groups=second)
     terms = jnp.sum(terms, axis=0)
     terms = exchange(terms, axis_index_groups=third)

time: 142 us -> 136 us (0.958)
  blocking collectives: 98.7 us -> 42 us
  waiting for transfers between devices: 16.4 us -> 51.1 us
  starting transfers between devices: 5.83 us -> 26.7 us
  Pallas kernels: 13.9 us -> 9.62 us
  other arithmetic: 4.39 us -> 1.6 us
  local copies, waits for them, and re-layouts: 1.39 us -> 3.21 us
    all_to_all x1 -> x0, blocking collectives: 57.4 us -> none  [local(): terms = exchange(terms, axis_index_groups=first)]
    ppermute x0 -> x3, waiting for transfers between devices: none -> 36.9 us  [the longest x1 19.9 us: local(): diagonal = lax.ppermute(diagonal, axes, pairs(True, True))]
    ppermute x0 -> x3, starting transfers between devices: none -> 22.4 us  [the longest x1 15.1 us: local(): across_z = lax.ppermute(across_z, axes, pairs(True, False))]
    reduce_sum x1 -> x0, other arithmetic: 3.62 us -> none  [local(): terms = jnp.sum(terms, axis=0).reshape(8, 6, SIDE, WIDE)]
    unnamed x4 -> x12, local copies, waits for them, and re-layouts: 0.68 us -> 3.12 us
    pallas_call x1 -> x2, Pallas kernels: 9.28 us -> 6.92 us  [gradient_terms(): pl.pallas_call(terms_kernel, grid_spec=pltpu.PrefetchScalarGridSpec(num_s...]
    all_to_all x1, waiting for transfers between devices: 16.4 us -> 14.2 us  [local(): terms = exchange(terms, axis_index_groups=third)]
    all_to_all x1, starting transfers between devices: 5.83 us -> 4.31 us  [local(): terms = exchange(terms, axis_index_groups=third)]
  transfers between devices with their start and end apart: 1 -> 4, of which waited for: 1 -> 4; matrix products, arithmetic and copies ran while one was open for 1% -> 0% of each run, Pallas kernels for 0% -> 3%
where the time goes in v2:
time: 136 us; the launch traced here: 135 us
  waiting for transfers between devices  51.1 us (38%)
  blocking collectives  42 us (31%)
  starting transfers between devices  26.7 us (20%)
  Pallas kernels  9.62 us (7%)
  local copies, waits for them, and re-layouts  3.21 us (2%)
  other arithmetic  1.6 us (1%)
    all_to_all x1, blocking collectives, local(): terms = exchange(terms, axis_index_groups=second)  32.7 us
    ppermute x1, waiting for transfers between devices, local(): diagonal = lax.ppermute(diagonal, axes, pairs(True, True))  19.9 us
    ppermute x1, starting transfers between devices, local(): across_z = lax.ppermute(across_z, axes, pairs(True, False))  15.1 us
    all_to_all x1, waiting for transfers between devices, local(): terms = exchange(terms, axis_index_groups=third)  14.2 us
    ppermute x1, waiting for transfers between devices, local(): across_y = lax.ppermute(across_y, axes, pairs(False, True))  9.89 us
    all_to_all x1, blocking collectives, local(): lax.all_to_all(sent, 'replica', split_axis=0, concat_axis=0, tiled=True)  9.28 us
    ppermute x1, waiting for transfers between devices, local(): across_z = lax.ppermute(across_z, axes, pairs(True, False))  7.14 us
    pallas_call x2, Pallas kernels, gradient_terms(): pl.pallas_call(terms_kernel, grid_spec=pltpu.PrefetchScalarGridSpec(num_s...  6.92 us
  transfers between devices with their start and end apart: 4, of which 4 were waited for; matrix products, arithmetic and copies ran while one was open for 0% of the time, Pallas kernels for 3%

profile of v2, /device:TPU:1, one launch (start us, length us, event | category | flops | bytes accessed | tf_op | source)
XLA Modules:
  0.0 135.0 jit_solution(16830386973389933372)
XLA Ops:
  0.6 0.0 copy-start
  0.7 2.2 %copy-done = bf16[1,256,2,4096]{3,2,1,0:T(2,128)(2,1)S(1)} copy-done((bf16[1,256,2,4096]{3,2,1,0:T(2,128)(2,1)S(1)}, bf16[1,256,2,4096]{3,2,1,0:T(2,128)(2,1)}, u32[]{:S(2)}) %copy-start) | copy-done | bytes 4194328
  2.8 0.9 copy-done.1
  3.8 3.4 %far.1 = (f32[2,2,2,3,2,64,128]{6,5,4,3,2,1,0:T(8,128)S(1)}, f32[2,2,2,3,2,64,128]{6,5,4,3,2,1,0:T(8,128)S(1)}) custom-call(s32[1]{0:T(128)} %bitcast.place_ref, bf16[2,192,256]{2,1,0:T(8,128)(2,1)S(1)} %bitcast.6, bf16[1,256,2,4096]{3,2,1,0:T(2,128)(2,1)S(1)} %copy-done), custom_call_target="tpu_custom_call" | custom-call | tf_op jit(solution)/shard_map/far/pallas_call | solution.py:134
  7.2 15.1 %collective-permute-start.1 = (f32[2,2,2,3,2,64,128]{6,5,4,3,2,1,0:T(8,128)S(1)}, f32[2,2,2,3,2,64,128]{6,5,4,3,2,1,0:T(8,128)S(1)}, u32[]{:S(2)}, u32[]{:S(2)}) collective-permute-start(f32[2,2,2,3,2,64,128]{6,5,4,3,2,1,0:T(8,128)S(1)} %get-tuple-element.10), channel_id=1, source_target_pairs={{0,16},{1,17},{2,18},{3,19},{4,20},{5,21},{6,22},{7,23},{8,24},{9,... | collective-permute-start | bytes 4718600 | tf_op jit(solution)/shard_map/ppermute | solution.py:225
  22.4 5.0 %collective-permute-start.2 = (f32[2,2,2,3,2,64,128]{6,5,4,3,2,1,0:T(8,128)S(1)}, f32[2,2,2,3,2,64,128]{6,5,4,3,2,1,0:T(8,128)S(1)}, u32[]{:S(2)}, u32[]{:S(2)}) collective-permute-start(f32[2,2,2,3,2,64,128]{6,5,4,3,2,1,0:T(8,128)S(1)} %get-tuple-element.11), channel_id=1, source_target_pairs={{0,17},{1,16},{2,19},{3,18},{4,21},{5,20},{6,23},{7,22},{8,25},{9,... | collective-permute-start | bytes 4718600 | tf_op jit(solution)/shard_map/ppermute | solution.py:224
  27.3 3.5 %near.1 = (f32[2,2,2,3,2,64,128]{6,5,4,3,2,1,0:T(8,128)S(1)}, f32[2,2,2,3,2,64,128]{6,5,4,3,2,1,0:T(8,128)S(1)}) custom-call(s32[1]{0:T(128)} %bitcast.place_ref, bf16[2,192,256]{2,1,0:T(8,128)(2,1)S(1)} %bitcast.7, bf16[1,256,2,4096]{3,2,1,0:T(2,128)(2,1)S(1)} %copy-done), custom_call_target="tpu_custom_call" | custom-call | tf_op jit(solution)/shard_map/near/pallas_call | solution.py:134
  30.8 2.3 %collective-permute-start = (f32[2,2,2,3,2,64,128]{6,5,4,3,2,1,0:T(8,128)S(1)}, f32[2,2,2,3,2,64,128]{6,5,4,3,2,1,0:T(8,128)S(1)}, u32[]{:S(2)}, u32[]{:S(2)}) collective-permute-start(f32[2,2,2,3,2,64,128]{6,5,4,3,2,1,0:T(8,128)S(1)} %get-tuple-element.9), channel_id=1, source_target_pairs={{0,1},{1,0},{2,3},{3,2},{4,5},{5,4},{6,7},{7,6},{8,9},{9,8},{10,11... | collective-permute-start | bytes 4718600 | tf_op jit(solution)/shard_map/ppermute | solution.py:226
  33.1 7.1 %collective-permute-done.1 = f32[2,2,2,3,2,64,128]{6,5,4,3,2,1,0:T(8,128)S(1)} collective-permute-done((f32[2,2,2,3,2,64,128]{6,5,4,3,2,1,0:T(8,128)S(1)}, f32[2,2,2,3,2,64,128]{6,5,4,3,2,1,0:T(8,128)S(1)}, u32[]{:S(2)}, u32[]{:S(2)}) %collective-permute-start.1) | collective-permute-done | bytes 1572896 | tf_op jit(solution)/shard_map/ppermute | solution.py:225
  40.3 19.9 %collective-permute-done.2 = f32[2,2,2,3,2,64,128]{6,5,4,3,2,1,0:T(8,128)S(1)} collective-permute-done((f32[2,2,2,3,2,64,128]{6,5,4,3,2,1,0:T(8,128)S(1)}, f32[2,2,2,3,2,64,128]{6,5,4,3,2,1,0:T(8,128)S(1)}, u32[]{:S(2)}, u32[]{:S(2)}) %collective-permute-start.2) | collective-permute-done | bytes 1572896 | tf_op jit(solution)/shard_map/ppermute | solution.py:224
  60.1 9.9 %collective-permute-done = f32[2,2,2,3,2,64,128]{6,5,4,3,2,1,0:T(8,128)S(1)} collective-permute-done((f32[2,2,2,3,2,64,128]{6,5,4,3,2,1,0:T(8,128)S(1)}, f32[2,2,2,3,2,64,128]{6,5,4,3,2,1,0:T(8,128)S(1)}, u32[]{:S(2)}, u32[]{:S(2)}) %collective-permute-start) | collective-permute-done | bytes 1572896 | tf_op jit(solution)/shard_map/ppermute | solution.py:226
  70.0 0.8 add_add_fusion
  70.9 32.7 %all_to_all.15 = f32[8,6,64,128]{3,2,1,0:T(8,128)S(1)} all-to-all(f32[8,6,64,128]{3,2,1,0:T(8,128)S(1)} %bitcast.8), channel_id=1, replica_groups={{0,2,32,34,8,10,40,42},{4,6,36,38,12,14,44,46},{64,66,96,98,72,74,104,1..., dimensions={0} | all-to-all | bytes 3145728 | tf_op jit(solution)/shard_map/all_to_all | solution.py:228
  103.6 0.8 reduce_sum.9
  104.3 4.3 %all-to-all-start.1 = ((f32[6,64,128]{2,1,0:T(8,128)}), f32[6,64,128]{2,1,0:T(8,128)S(1)}, u32[]{:S(2)}, u32[]{:S(2)}) async-start(f32[6,64,128]{2,1,0:T(8,128)} %reduce_sum.9), calls=%async_computation.1 | async-start | bytes 393216 | tf_op jit(solution)/shard_map/all_to_all | solution.py:230
  108.6 0.0 copy-done.5
  108.6 0.1 copy.10.idx_ref
  108.7 14.2 %all-to-all-done.1.parts_ref = f32[6,64,128]{2,1,0:T(8,128)S(1)} async-done(((f32[6,64,128]{2,1,0:T(8,128)}), f32[6,64,128]{2,1,0:T(8,128)S(1)}, u32[]{:S(2)}, u32[]{:S(2)}) %all-to-all-start.1) | async-done | bytes 196640 | tf_op jit(solution)/shard_map/all_to_all | solution.py:230
  123.0 0.0 copy-done.2
  123.0 0.0 copy-done.3
  123.0 0.0 copy-done.4
  123.0 1.7 %encode.1 = (f32[1,1,64,128]{3,2,1,0:T(8,128)}, f32[4,64,128]{2,1,0:T(8,128)S(1)}) custom-call(f32[6,64,128]{2,1,0:T(8,128)S(1)} %all-to-all-done.1.parts_ref, f32[1,1,64,128]{3,2,1,0:T(8,128)S(1)} %copy-done.4, s32[2,32,1]{2,1,0:T(8,128)S(1)} %copy.10.idx_ref, f32[64,64]{1,0:T(8,128)S(1)} %copy-done.3, f32[128,128]{1,0:T(8,128)S(1)} %copy-done.2), custom_call_target="tpu_custom_call" | custom-call | tf_op jit(solution)/shard_map/encode/pallas_call | solution.py:196
  124.6 9.3 %all_to_all.16.every_ref = f32[4,64,128]{2,1,0:T(8,128)S(1)} all-to-all(f32[4,64,128]{2,1,0:T(8,128)S(1)} %get-tuple-element.13), channel_id=1, replica_groups=mesh['replica'=4,'shard'=192] {'replica'}, dimensions={0} | all-to-all | bytes 262144 | tf_op jit(solution)/shard_map/all_to_all | solution.py:232
  133.9 1.0 decode.1
  (5 shorter events, 0.0 us)
Async XLA Ops:
  0.6 2.2 %copy-start = (bf16[1,256,2,4096]{3,2,1,0:T(2,128)(2,1)S(1)}, bf16[1,256,2,4096]{3,2,1,0:T(2,128)(2,1)}, u32[]{:S(2)}) copy-start(bf16[1,256,2,4096]{3,2,1,0:T(2,128)(2,1)} %grad_ref.3) | copy-start | bytes 12582916
  2.8 0.9 copy-start.1
  7.2 33.1 %collective-permute-start.1 = (f32[2,2,2,3,2,64,128]{6,5,4,3,2,1,0:T(8,128)S(1)}, f32[2,2,2,3,2,64,128]{6,5,4,3,2,1,0:T(8,128)S(1)}, u32[]{:S(2)}, u32[]{:S(2)}) collective-permute-start(f32[2,2,2,3,2,64,128]{6,5,4,3,2,1,0:T(8,128)S(1)} %get-tuple-element.10), channel_id=1, source_target_pairs={{0,16},{1,17},{2,18},{3,19},{4,20},{5,21},{6,22},{7,23},{8,24},{9,... | collective-permute-start | bytes 4718600 | tf_op jit(solution)/shard_map/ppermute | solution.py:225
  22.4 37.8 %collective-permute-start.2 = (f32[2,2,2,3,2,64,128]{6,5,4,3,2,1,0:T(8,128)S(1)}, f32[2,2,2,3,2,64,128]{6,5,4,3,2,1,0:T(8,128)S(1)}, u32[]{:S(2)}, u32[]{:S(2)}) collective-permute-start(f32[2,2,2,3,2,64,128]{6,5,4,3,2,1,0:T(8,128)S(1)} %get-tuple-element.11), channel_id=1, source_target_pairs={{0,17},{1,16},{2,19},{3,18},{4,21},{5,20},{6,23},{7,22},{8,25},{9,... | collective-permute-start | bytes 4718600 | tf_op jit(solution)/shard_map/ppermute | solution.py:224
  30.8 39.2 %collective-permute-start = (f32[2,2,2,3,2,64,128]{6,5,4,3,2,1,0:T(8,128)S(1)}, f32[2,2,2,3,2,64,128]{6,5,4,3,2,1,0:T(8,128)S(1)}, u32[]{:S(2)}, u32[]{:S(2)}) collective-permute-start(f32[2,2,2,3,2,64,128]{6,5,4,3,2,1,0:T(8,128)S(1)} %get-tuple-element.9), channel_id=1, source_target_pairs={{0,1},{1,0},{2,3},{3,2},{4,5},{5,4},{6,7},{7,6},{8,9},{9,8},{10,11... | collective-permute-start | bytes 4718600 | tf_op jit(solution)/shard_map/ppermute | solution.py:226
  103.5 5.1 %copy-start.5 = (s32[1,2,32]{2,1,0:T(2,128)S(1)}, s32[1,2,32]{2,1,0:T(2,128)}, u32[]{:S(2)}) copy-start(s32[1,2,32]{2,1,0:T(2,128)} %param.11) | copy-start | bytes 772
  103.5 19.4 %copy-start.2 = (f32[128,128]{1,0:T(8,128)S(1)}, f32[128,128]{1,0:T(8,128)}, u32[]{:S(2)}) copy-start(f32[128,128]{1,0:T(8,128)} %constant.15.clone.wide_ref) | copy-start | bytes 196612
  103.5 19.4 %copy-start.3 = (f32[64,64]{1,0:T(8,128)S(1)}, f32[64,64]{1,0:T(8,128)}, u32[]{:S(2)}) copy-start(f32[64,64]{1,0:T(8,128)} %constant.14.clone.left_ref) | copy-start | bytes 49156
  103.5 19.4 %copy-start.4 = (f32[1,1,64,128]{3,2,1,0:T(8,128)S(1)}, f32[1,1,64,128]{3,2,1,0:T(8,128)}, u32[]{:S(2)}) copy-start(f32[1,1,64,128]{3,2,1,0:T(8,128)} %mom_ref.1) | copy-start | bytes 98308
  104.3 18.6 %all-to-all-start.1 = ((f32[6,64,128]{2,1,0:T(8,128)}), f32[6,64,128]{2,1,0:T(8,128)S(1)}, u32[]{:S(2)}, u32[]{:S(2)}) async-start(f32[6,64,128]{2,1,0:T(8,128)} %reduce_sum.9), calls=%async_computation.1 | async-start | bytes 393216 | tf_op jit(solution)/shard_map/all_to_all | solution.py:230

commit v3 on v2

--- a/solution.py
+++ b/solution.py
@@ -88,11 +88,12 @@
     return (place_ref[0] >> 4) & 1, place_ref[0] & 1
 
 
-def terms_kernel(place_ref, act_ref, grad_ref, other_ref, own_ref, left_ref):
+def terms_kernel(colour, place_ref, act_ref, grad_ref, send_ref, keep_ref, left_ref):
     tokens = grad_ref.shape[1]
     rows = act_ref.shape[1]
-
-    @pl.when(pl.program_id(0) == 0)
+    _, y_own = parities(place_ref)
+
+    @pl.when((pl.program_id(0) == 0) & (pl.program_id(1) == 0))
     def _():
         token = lax.broadcasted_iota(jnp.int32, (tokens, tokens * LAYERS), 0)
         place = lax.broadcasted_iota(jnp.int32, (tokens, tokens * LAYERS), 1)
@@ -106,49 +107,51 @@
     both = jnp.dot(left_ref[...], rhs, preferred_element_type=jnp.float32)
     low = lax.broadcasted_iota(jnp.int32, (SIDE, WIDE), 1) < SIDE
 
-    def write(even_ref, odd_ref):
+    def write(even_ref, odd_ref, even_at, odd_at):
         for a in range(rows // SIDE):
             for pair in range(CHUNK // WIDE):
                 cols = slice(pair * WIDE, (pair + 1) * WIDE)
                 one = both[a * SIDE : (a + 1) * SIDE, cols]
                 two = both[rows + a * SIDE : rows + (a + 1) * SIDE, cols]
-                even_ref[0, 0, pair % 2, a, pair // 2] = jnp.where(low, one, pltpu.roll(two, SIDE, 1))
-                odd_ref[0, 0, pair % 2, a, pair // 2] = jnp.where(low, pltpu.roll(one, SIDE, 1), two)
-
-    @pl.when(parities(place_ref)[1] == 0)
-    def _():
-        write(own_ref, other_ref)
-
-    @pl.when(parities(place_ref)[1] == 1)
-    def _():
-        write(other_ref, own_ref)
-
-
-def gradient_terms(place, acts, grads, far):
-    tokens, cols = grads.shape[1], grads.shape[3]
+                even_ref[even_at, 0, pair % 2, a, pair // 2] = jnp.where(low, one, pltpu.roll(two, SIDE, 1))
+                odd_ref[odd_at, 0, pair % 2, a, pair // 2] = jnp.where(low, pltpu.roll(one, SIDE, 1), two)
+
+    if colour == 0:
+        pl.when(y_own == 0)(lambda: write(keep_ref, send_ref, 0, 0))
+        pl.when(y_own == 1)(lambda: write(send_ref, keep_ref, 0, 0))
+    else:
+        pl.when(pl.program_id(0) == 0)(lambda: write(send_ref, send_ref, 1 - y_own, y_own))
+        pl.when(pl.program_id(0) == 1)(lambda: write(keep_ref, keep_ref, 1 - y_own, y_own))
+
+
+def gradient_terms(place, acts, grads, colour):
+    tokens = grads.shape[1]
     rows = acts.shape[1]
     out = jax.ShapeDtypeStruct((2, 2, 2, rows // SIDE, 2, SIDE, WIDE), jnp.float32)
-    out_spec = pl.BlockSpec(
-        (1, 1, 2, rows // SIDE, 2, SIDE, WIDE), lambda c, place: (c % 2, c // 2, 0, 0, 0, 0, 0)
-    )
+    block = (2 if colour else 1, 1, 2, rows // SIDE, 2, SIDE, WIDE)
+    if colour == 0:
+        send_spec = keep_spec = pl.BlockSpec(block, lambda z, k, place: (z, k, 0, 0, 0, 0, 0))
+    else:
+        send_spec = pl.BlockSpec(block, lambda z, k, place: (0, jnp.where(z == 0, k, 1), 0, 0, 0, 0, 0))
+        keep_spec = pl.BlockSpec(block, lambda z, k, place: (0, jnp.where(z == 0, 0, k), 0, 0, 0, 0, 0))
     return pl.pallas_call(
-        terms_kernel,
+        functools.partial(terms_kernel, colour),
         grid_spec=pltpu.PrefetchScalarGridSpec(
             num_scalar_prefetch=1,
-            grid=(cols // CHUNK // 2,),
+            grid=(2, 2),
             in_specs=[
-                pl.BlockSpec((LAYERS, rows, tokens), lambda c, place: (0, 0, 0)),
+                pl.BlockSpec((LAYERS, rows, tokens), lambda z, k, place: (0, 0, 0)),
                 pl.BlockSpec(
                     (1, tokens, LAYERS, CHUNK),
-                    lambda c, place: (0, 0, 0, (c // 2) * 4 + (parities(place)[0] ^ far) * 2 + c % 2),
+                    lambda z, k, place: (0, 0, 0, k * 4 + (parities(place)[0] ^ 1 ^ z) * 2 + colour),
                 ),
             ],
-            out_specs=[out_spec, out_spec],
+            out_specs=[send_spec, keep_spec],
             scratch_shapes=[pltpu.VMEM((LAYERS * rows, tokens * LAYERS), acts.dtype)],
         ),
         out_shape=(out, out),
         compiler_params=pltpu.CompilerParams(vmem_limit_bytes=16 * 2**20),
-        name="far" if far else "near",
+        name=f"terms{colour}",
     )(place, acts, grads)
 
 
@@ -219,12 +222,16 @@
     exchange = functools.partial(lax.all_to_all, axis_name=axes, split_axis=0, concat_axis=0, tiled=True)
     place = lax.axis_index(axes)[None]
     acts = acts[0].transpose(1, 2, 0)
-    diagonal, across_z = gradient_terms(place, acts, grads, 1)
-    across_y, own = gradient_terms(place, acts, grads, 0)
-    diagonal = lax.ppermute(diagonal, axes, pairs(True, True))
-    across_z = lax.ppermute(across_z, axes, pairs(True, False))
-    across_y = lax.ppermute(across_y, axes, pairs(False, True))
-    terms = ((own + across_y) + (across_z + diagonal)).reshape(8, 6, SIDE, WIDE)
+    hop = functools.partial(lax.ppermute, axis_name=axes)
+    across_z, across_y = pairs(True, False), pairs(False, True)
+    ways = [(across_y, across_z), (across_z, across_y)]
+    sums = []
+    for colour in range(2):
+        send, keep = gradient_terms(place, acts, grads, colour)
+        got = hop(send, perm=ways[colour][0])
+        got, more = keep[1] + got[1], hop(keep[0] + got[0], perm=ways[colour][1])
+        sums.append(got + more)
+    terms = jnp.concatenate(sums).reshape(8, 6, SIDE, WIDE)
     terms = exchange(terms, axis_index_groups=second)
     terms = jnp.sum(terms, axis=0)
     terms = exchange(terms, axis_index_groups=third)

time: 136 us -> 129 us (0.949)
  waiting for transfers between devices: 51.1 us -> 28.5 us
  starting transfers between devices: 26.7 us -> 40.6 us
    ppermute x3 -> x4, waiting for transfers between devices: 36.9 us -> 15.5 us  [the longest x2 11.8 us: local(): got, more = (keep[1] + got[1], hop(keep[0] + got[0], perm=ways[colour][1]))]
    ppermute x3 -> x4, starting transfers between devices: 22.4 us -> 36.3 us  [the longest x2 20.4 us: local(): got = hop(send, perm=ways[colour][0])]
  transfers between devices with their start and end apart: 4 -> 5, of which waited for: 4 -> 4; matrix products, arithmetic and copies ran while one was open for 0% -> 0% of each run, Pallas kernels for 3% -> 3%
where the time goes in v3:
time: 129 us; the launch traced here: 127 us
  blocking collectives  42.9 us (33%)
  starting transfers between devices  40.6 us (31%)
  waiting for transfers between devices  28.5 us (22%)
  Pallas kernels  9.86 us (8%)
  local copies, waits for them, and re-layouts  3.21 us (2%)
  other arithmetic  1.5 us (1%)
    all_to_all x1, blocking collectives, local(): terms = exchange(terms, axis_index_groups=second)  33 us
    ppermute x2, starting transfers between devices, local(): got = hop(send, perm=ways[colour][0])  20.4 us
    ppermute x2, starting transfers between devices, local(): got, more = (keep[1] + got[1], hop(keep[0] + got[0], perm=ways[colour][1]))  15.9 us
    all_to_all x1, waiting for transfers between devices, local(): terms = exchange(terms, axis_index_groups=third)  13 us
    ppermute x2, waiting for transfers between devices, local(): got, more = (keep[1] + got[1], hop(keep[0] + got[0], perm=ways[colour][1]))  11.8 us
    all_to_all x1, blocking collectives, local(): lax.all_to_all(sent, 'replica', split_axis=0, concat_axis=0, tiled=True)  9.96 us
    pallas_call x2, Pallas kernels, gradient_terms(): pl.pallas_call(functools.partial(terms_kernel, colour), grid_spec=pltpu.P...  7.16 us
    all_to_all x1, starting transfers between devices, local(): terms = exchange(terms, axis_index_groups=third)  4.3 us
  transfers between devices with their start and end apart: 5, of which 4 were waited for; matrix products, arithmetic and copies ran while one was open for 0% of the time, Pallas kernels for 3%

profile of v3, /device:TPU:1, one launch (start us, length us, event | category | flops | bytes accessed | tf_op | source)
XLA Modules:
  0.0 127.4 jit_solution(1444633677188327988)
XLA Ops:
  0.7 2.2 %copy-done = bf16[1,256,2,4096]{3,2,1,0:T(2,128)(2,1)S(1)} copy-done((bf16[1,256,2,4096]{3,2,1,0:T(2,128)(2,1)S(1)}, bf16[1,256,2,4096]{3,2,1,0:T(2,128)(2,1)}, u32[]{:S(2)}) %copy-start) | copy-done | bytes 4194328
  2.8 0.9 copy-done.1
  3.8 3.4 %terms0.1 = (f32[2,2,2,3,2,64,128]{6,5,4,3,2,1,0:T(8,128)S(1)}, f32[2,2,2,3,2,64,128]{6,5,4,3,2,1,0:T(8,128)S(1)}) custom-call(s32[1]{0:T(128)} %bitcast.place_ref, bf16[2,192,256]{2,1,0:T(8,128)(2,1)S(1)} %bitcast.18, bf16[1,256,2,4096]{3,2,1,0:T(2,128)(2,1)S(1)} %copy-done), custom_call_target="tpu_custom_call" | custom-call | tf_op jit(solution)/shard_map/terms0/pallas_call | solution.py:137
  7.2 6.1 %collective-permute-start = (f32[2,2,2,3,2,64,128]{6,5,4,3,2,1,0:T(8,128)S(1)}, f32[2,2,2,3,2,64,128]{6,5,4,3,2,1,0:T(8,128)S(1)}, u32[]{:S(2)}, u32[]{:S(2)}) collective-permute-start(f32[2,2,2,3,2,64,128]{6,5,4,3,2,1,0:T(8,128)S(1)} %get-tuple-element.9), channel_id=1, source_target_pairs={{0,1},{1,0},{2,3},{3,2},{4,5},{5,4},{6,7},{7,6},{8,9},{9,8},{10,11... | collective-permute-start | bytes 4718600 | tf_op jit(solution)/shard_map/ppermute | solution.py:231
  13.2 3.8 %terms1.1 = (f32[2,2,2,3,2,64,128]{6,5,4,3,2,1,0:T(8,128)S(1)}, f32[2,2,2,3,2,64,128]{6,5,4,3,2,1,0:T(8,128)S(1)}) custom-call(s32[1]{0:T(128)} %bitcast.place_ref, bf16[2,192,256]{2,1,0:T(8,128)(2,1)S(1)} %bitcast.19, bf16[1,256,2,4096]{3,2,1,0:T(2,128)(2,1)S(1)} %copy-done), custom_call_target="tpu_custom_call" | custom-call | tf_op jit(solution)/shard_map/terms1/pallas_call | solution.py:137
  17.0 14.3 %collective-permute-start.2 = (f32[2,2,2,3,2,64,128]{6,5,4,3,2,1,0:T(8,128)S(1)}, f32[2,2,2,3,2,64,128]{6,5,4,3,2,1,0:T(8,128)S(1)}, u32[]{:S(2)}, u32[]{:S(2)}) collective-permute-start(f32[2,2,2,3,2,64,128]{6,5,4,3,2,1,0:T(8,128)S(1)} %get-tuple-element.11), channel_id=1, source_target_pairs={{0,16},{1,17},{2,18},{3,19},{4,20},{5,21},{6,22},{7,23},{8,24},{9,... | collective-permute-start | bytes 4718600 | tf_op jit(solution)/shard_map/ppermute | solution.py:231
  31.3 0.1 fusion.3
  31.5 14.0 %collective-permute-start.1 = (f32[2,2,3,2,64,128]{5,4,3,2,1,0:T(8,128)S(1)}, f32[2,2,3,2,64,128]{5,4,3,2,1,0:T(8,128)S(1)}, u32[]{:S(2)}, u32[]{:S(2)}) collective-permute-start(f32[2,2,3,2,64,128]{5,4,3,2,1,0:T(8,128)S(1)} %fusion.3), channel_id=1, source_target_pairs={{0,16},{1,17},{2,18},{3,19},{4,20},{5,21},{6,22},{7,23},{8,24},{9,... | collective-permute-start | bytes 2359304 | tf_op jit(solution)/shard_map/ppermute | solution.py:232
  45.5 3.7 %collective-permute-done.2 = f32[2,2,2,3,2,64,128]{6,5,4,3,2,1,0:T(8,128)S(1)} collective-permute-done((f32[2,2,2,3,2,64,128]{6,5,4,3,2,1,0:T(8,128)S(1)}, f32[2,2,2,3,2,64,128]{6,5,4,3,2,1,0:T(8,128)S(1)}, u32[]{:S(2)}, u32[]{:S(2)}) %collective-permute-start.2) | collective-permute-done | bytes 1572896 | tf_op jit(solution)/shard_map/ppermute | solution.py:231
  49.1 0.1 fusion
  49.2 1.9 %collective-permute-start.3 = (f32[2,2,3,2,64,128]{5,4,3,2,1,0:T(8,128)S(1)}, f32[2,2,3,2,64,128]{5,4,3,2,1,0:T(8,128)S(1)}, u32[]{:S(2)}, u32[]{:S(2)}) collective-permute-start(f32[2,2,3,2,64,128]{5,4,3,2,1,0:T(8,128)S(1)} %fusion), channel_id=1, source_target_pairs={{0,1},{1,0},{2,3},{3,2},{4,5},{5,4},{6,7},{7,6},{8,9},{9,8},{10,11... | collective-permute-start | bytes 2359304 | tf_op jit(solution)/shard_map/ppermute | solution.py:232
  51.2 6.4 %collective-permute-done.1 = f32[2,2,3,2,64,128]{5,4,3,2,1,0:T(8,128)S(1)} collective-permute-done((f32[2,2,3,2,64,128]{5,4,3,2,1,0:T(8,128)S(1)}, f32[2,2,3,2,64,128]{5,4,3,2,1,0:T(8,128)S(1)}, u32[]{:S(2)}, u32[]{:S(2)}) %collective-permute-start.1) | collective-permute-done | bytes 786464 | tf_op jit(solution)/shard_map/ppermute | solution.py:232
  57.6 0.2 fusion.5
  57.7 5.4 %collective-permute-done.3 = f32[2,2,3,2,64,128]{5,4,3,2,1,0:T(8,128)S(1)} collective-permute-done((f32[2,2,3,2,64,128]{5,4,3,2,1,0:T(8,128)S(1)}, f32[2,2,3,2,64,128]{5,4,3,2,1,0:T(8,128)S(1)}, u32[]{:S(2)}, u32[]{:S(2)}) %collective-permute-start.3) | collective-permute-done | bytes 786464 | tf_op jit(solution)/shard_map/ppermute | solution.py:232
  63.2 0.2 fusion.2
  63.4 0.2 pad_maximum_fusion
  63.5 33.0 %all_to_all.15 = f32[8,6,64,128]{3,2,1,0:T(8,128)S(1)} all-to-all(f32[8,6,64,128]{3,2,1,0:T(8,128)S(1)} %bitcast.20), channel_id=1, replica_groups={{0,2,32,34,8,10,40,42},{4,6,36,38,12,14,44,46},{64,66,96,98,72,74,104,1..., dimensions={0} | all-to-all | bytes 3145728 | tf_op jit(solution)/shard_map/all_to_all | solution.py:235
  96.5 0.8 reduce_sum.9
  97.3 4.3 %all-to-all-start.1 = ((f32[6,64,128]{2,1,0:T(8,128)}), f32[6,64,128]{2,1,0:T(8,128)S(1)}, u32[]{:S(2)}, u32[]{:S(2)}) async-start(f32[6,64,128]{2,1,0:T(8,128)} %reduce_sum.9), calls=%async_computation.1 | async-start | bytes 393216 | tf_op jit(solution)/shard_map/all_to_all | solution.py:237
  101.6 0.1 copy.10.idx_ref
  101.7 13.0 %all-to-all-done.1.parts_ref = f32[6,64,128]{2,1,0:T(8,128)S(1)} async-done(((f32[6,64,128]{2,1,0:T(8,128)}), f32[6,64,128]{2,1,0:T(8,128)S(1)}, u32[]{:S(2)}, u32[]{:S(2)}) %all-to-all-start.1) | async-done | bytes 196640 | tf_op jit(solution)/shard_map/all_to_all | solution.py:237
  114.7 1.7 %encode.1 = (f32[1,1,64,128]{3,2,1,0:T(8,128)}, f32[4,64,128]{2,1,0:T(8,128)S(1)}) custom-call(f32[6,64,128]{2,1,0:T(8,128)S(1)} %all-to-all-done.1.parts_ref, f32[1,1,64,128]{3,2,1,0:T(8,128)S(1)} %copy-done.4, s32[2,32,1]{2,1,0:T(8,128)S(1)} %copy.10.idx_ref, f32[64,64]{1,0:T(8,128)S(1)} %copy-done.3, f32[128,128]{1,0:T(8,128)S(1)} %copy-done.2), custom_call_target="tpu_custom_call" | custom-call | tf_op jit(solution)/shard_map/encode/pallas_call | solution.py:199
  116.4 10.0 %all_to_all.16.every_ref = f32[4,64,128]{2,1,0:T(8,128)S(1)} all-to-all(f32[4,64,128]{2,1,0:T(8,128)S(1)} %get-tuple-element.13), channel_id=1, replica_groups=mesh['replica'=4,'shard'=192] {'replica'}, dimensions={0} | all-to-all | bytes 262144 | tf_op jit(solution)/shard_map/all_to_all | solution.py:239
  126.3 1.0 decode.1
  (11 shorter events, 0.0 us)
Async XLA Ops:
  0.6 2.2 %copy-start = (bf16[1,256,2,4096]{3,2,1,0:T(2,128)(2,1)S(1)}, bf16[1,256,2,4096]{3,2,1,0:T(2,128)(2,1)}, u32[]{:S(2)}) copy-start(bf16[1,256,2,4096]{3,2,1,0:T(2,128)(2,1)} %grad_ref.3) | copy-start | bytes 12582916
  2.8 0.9 copy-start.1
  7.2 24.2 %collective-permute-start = (f32[2,2,2,3,2,64,128]{6,5,4,3,2,1,0:T(8,128)S(1)}, f32[2,2,2,3,2,64,128]{6,5,4,3,2,1,0:T(8,128)S(1)}, u32[]{:S(2)}, u32[]{:S(2)}) collective-permute-start(f32[2,2,2,3,2,64,128]{6,5,4,3,2,1,0:T(8,128)S(1)} %get-tuple-element.9), channel_id=1, source_target_pairs={{0,1},{1,0},{2,3},{3,2},{4,5},{5,4},{6,7},{7,6},{8,9},{9,8},{10,11... | collective-permute-start | bytes 4718600 | tf_op jit(solution)/shard_map/ppermute | solution.py:231
  17.0 32.1 %collective-permute-start.2 = (f32[2,2,2,3,2,64,128]{6,5,4,3,2,1,0:T(8,128)S(1)}, f32[2,2,2,3,2,64,128]{6,5,4,3,2,1,0:T(8,128)S(1)}, u32[]{:S(2)}, u32[]{:S(2)}) collective-permute-start(f32[2,2,2,3,2,64,128]{6,5,4,3,2,1,0:T(8,128)S(1)} %get-tuple-element.11), channel_id=1, source_target_pairs={{0,16},{1,17},{2,18},{3,19},{4,20},{5,21},{6,22},{7,23},{8,24},{9,... | collective-permute-start | bytes 4718600 | tf_op jit(solution)/shard_map/ppermute | solution.py:231
  31.5 26.1 %collective-permute-start.1 = (f32[2,2,3,2,64,128]{5,4,3,2,1,0:T(8,128)S(1)}, f32[2,2,3,2,64,128]{5,4,3,2,1,0:T(8,128)S(1)}, u32[]{:S(2)}, u32[]{:S(2)}) collective-permute-start(f32[2,2,3,2,64,128]{5,4,3,2,1,0:T(8,128)S(1)} %fusion.3), channel_id=1, source_target_pairs={{0,16},{1,17},{2,18},{3,19},{4,20},{5,21},{6,22},{7,23},{8,24},{9,... | collective-permute-start | bytes 2359304 | tf_op jit(solution)/shard_map/ppermute | solution.py:232
  49.2 13.9 %collective-permute-start.3 = (f32[2,2,3,2,64,128]{5,4,3,2,1,0:T(8,128)S(1)}, f32[2,2,3,2,64,128]{5,4,3,2,1,0:T(8,128)S(1)}, u32[]{:S(2)}, u32[]{:S(2)}) collective-permute-start(f32[2,2,3,2,64,128]{5,4,3,2,1,0:T(8,128)S(1)} %fusion), channel_id=1, source_target_pairs={{0,1},{1,0},{2,3},{3,2},{4,5},{5,4},{6,7},{7,6},{8,9},{9,8},{10,11... | collective-permute-start | bytes 2359304 | tf_op jit(solution)/shard_map/ppermute | solution.py:232
  96.5 5.1 %copy-start.5 = (s32[1,2,32]{2,1,0:T(2,128)S(1)}, s32[1,2,32]{2,1,0:T(2,128)}, u32[]{:S(2)}) copy-start(s32[1,2,32]{2,1,0:T(2,128)} %param.11) | copy-start | bytes 772
  96.5 18.2 %copy-start.2 = (f32[128,128]{1,0:T(8,128)S(1)}, f32[128,128]{1,0:T(8,128)}, u32[]{:S(2)}) copy-start(f32[128,128]{1,0:T(8,128)} %constant.15.clone.wide_ref) | copy-start | bytes 196612
  96.5 18.2 %copy-start.3 = (f32[64,64]{1,0:T(8,128)S(1)}, f32[64,64]{1,0:T(8,128)}, u32[]{:S(2)}) copy-start(f32[64,64]{1,0:T(8,128)} %constant.14.clone.left_ref) | copy-start | bytes 49156
  96.5 18.2 %copy-start.4 = (f32[1,1,64,128]{3,2,1,0:T(8,128)S(1)}, f32[1,1,64,128]{3,2,1,0:T(8,128)}, u32[]{:S(2)}) copy-start(f32[1,1,64,128]{3,2,1,0:T(8,128)} %mom_ref.1) | copy-start | bytes 98308
  97.3 17.4 %all-to-all-start.1 = ((f32[6,64,128]{2,1,0:T(8,128)}), f32[6,64,128]{2,1,0:T(8,128)S(1)}, u32[]{:S(2)}, u32[]{:S(2)}) async-start(f32[6,64,128]{2,1,0:T(8,128)} %reduce_sum.9), calls=%async_computation.1 | async-start | bytes 393216 | tf_op jit(solution)/shard_map/all_to_all | solution.py:237

commit v4 on v2

--- a/solution.py
+++ b/solution.py
@@ -16,6 +16,7 @@
 BAND = 32
 REPLICAS = 4
 CHUNK = 512
+FIRST_VMEM = 50
 HIGHEST = lax.Precision.HIGHEST
 
 
@@ -88,20 +89,25 @@
     return (place_ref[0] >> 4) & 1, place_ref[0] & 1
 
 
-def terms_kernel(place_ref, act_ref, grad_ref, other_ref, own_ref, left_ref):
+def left_kernel_part(act_ref, left_ref):
+    rows, tokens = act_ref.shape[1:]
+    token = lax.broadcasted_iota(jnp.int32, (tokens, tokens * LAYERS), 0)
+    place = lax.broadcasted_iota(jnp.int32, (tokens, tokens * LAYERS), 1)
+    for layer in range(LAYERS):
+        spread = (place == token * LAYERS + layer).astype(jnp.float32).astype(act_ref.dtype)
+        left_ref[layer * rows : (layer + 1) * rows] = jnp.dot(
+            act_ref[layer], spread, preferred_element_type=jnp.float32
+        ).astype(act_ref.dtype)
+
+
+def terms_kernel(first, place_ref, in_ref, grad_ref, other_ref, own_ref, *made_ref):
     tokens = grad_ref.shape[1]
-    rows = act_ref.shape[1]
-
-    @pl.when(pl.program_id(0) == 0)
-    def _():
-        token = lax.broadcasted_iota(jnp.int32, (tokens, tokens * LAYERS), 0)
-        place = lax.broadcasted_iota(jnp.int32, (tokens, tokens * LAYERS), 1)
-        for layer in range(LAYERS):
-            spread = (place == token * LAYERS + layer).astype(jnp.float32).astype(act_ref.dtype)
-            left_ref[layer * rows : (layer + 1) * rows] = jnp.dot(
-                act_ref[layer], spread, preferred_element_type=jnp.float32
-            ).astype(act_ref.dtype)
-
+    if first:
+        left_ref = made_ref[0]
+        pl.when(pl.program_id(0) == 0)(lambda: left_kernel_part(in_ref, left_ref))
+    else:
+        left_ref = in_ref
+    rows = left_ref.shape[0] // LAYERS
     rhs = grad_ref[0].reshape(tokens * LAYERS, CHUNK)
     both = jnp.dot(left_ref[...], rhs, preferred_element_type=jnp.float32)
     low = lax.broadcasted_iota(jnp.int32, (SIDE, WIDE), 1) < SIDE
@@ -112,44 +118,41 @@
                 cols = slice(pair * WIDE, (pair + 1) * WIDE)
                 one = both[a * SIDE : (a + 1) * SIDE, cols]
                 two = both[rows + a * SIDE : rows + (a + 1) * SIDE, cols]
-                even_ref[0, 0, pair % 2, a, pair // 2] = jnp.where(low, one, pltpu.roll(two, SIDE, 1))
-                odd_ref[0, 0, pair % 2, a, pair // 2] = jnp.where(low, pltpu.roll(one, SIDE, 1), two)
-
-    @pl.when(parities(place_ref)[1] == 0)
-    def _():
-        write(own_ref, other_ref)
-
-    @pl.when(parities(place_ref)[1] == 1)
-    def _():
-        write(other_ref, own_ref)
-
-
-def gradient_terms(place, acts, grads, far):
-    tokens, cols = grads.shape[1], grads.shape[3]
-    rows = acts.shape[1]
-    out = jax.ShapeDtypeStruct((2, 2, 2, rows // SIDE, 2, SIDE, WIDE), jnp.float32)
-    out_spec = pl.BlockSpec(
-        (1, 1, 2, rows // SIDE, 2, SIDE, WIDE), lambda c, place: (c % 2, c // 2, 0, 0, 0, 0, 0)
-    )
+                even_ref[0, pair % 2, a, pair // 2] = jnp.where(low, one, pltpu.roll(two, SIDE, 1))
+                odd_ref[0, pair % 2, a, pair // 2] = jnp.where(low, pltpu.roll(one, SIDE, 1), two)
+
+    _, y_own = parities(place_ref)
+    pl.when(y_own == 0)(lambda: write(own_ref, other_ref))
+    pl.when(y_own == 1)(lambda: write(other_ref, own_ref))
+
+
+def gradient_terms(place, acts_or_left, grads, colour, far):
+    first = acts_or_left.ndim == 3
+    tokens = grads.shape[1]
+    rows = acts_or_left.shape[1] if first else acts_or_left.shape[0] // LAYERS
+    blocks = (2, 2, rows // SIDE, 2, SIDE, WIDE)
+    out = jax.ShapeDtypeStruct(blocks, jnp.float32)
+    out_spec = pl.BlockSpec((1,) + blocks[1:], lambda k, place: (k, 0, 0, 0, 0, 0))
+    left = (LAYERS * rows, tokens * LAYERS)
+    left_spec = pl.BlockSpec(left, lambda k, place: (0, 0))
     return pl.pallas_call(
-        terms_kernel,
+        functools.partial(terms_kernel, first),
         grid_spec=pltpu.PrefetchScalarGridSpec(
             num_scalar_prefetch=1,
-            grid=(cols // CHUNK // 2,),
+            grid=(2,),
             in_specs=[
-                pl.BlockSpec((LAYERS, rows, tokens), lambda c, place: (0, 0, 0)),
+                pl.BlockSpec(acts_or_left.shape, lambda k, place: (0, 0, 0)) if first else left_spec,
                 pl.BlockSpec(
                     (1, tokens, LAYERS, CHUNK),
-                    lambda c, place: (0, 0, 0, (c // 2) * 4 + (parities(place)[0] ^ far) * 2 + c % 2),
+                    lambda k, place: (0, 0, 0, k * 4 + (parities(place)[0] ^ far) * 2 + colour),
                 ),
             ],
-            out_specs=[out_spec, out_spec],
-            scratch_shapes=[pltpu.VMEM((LAYERS * rows, tokens * LAYERS), acts.dtype)],
+            out_specs=[out_spec, out_spec] + [left_spec] * first,
         ),
-        out_shape=(out, out),
-        compiler_params=pltpu.CompilerParams(vmem_limit_bytes=16 * 2**20),
-        name="far" if far else "near",
-    )(place, acts, grads)
+        out_shape=[out, out] + [jax.ShapeDtypeStruct(left, acts_or_left.dtype)] * first,
+        compiler_params=pltpu.CompilerParams(vmem_limit_bytes=(FIRST_VMEM if first else 40) * 2**20),
+        name=f"terms{colour}{far}",
+    )(place, acts_or_left, grads)
 
 
 def dot(a, b, dims):
@@ -157,13 +160,13 @@
 
 
 def one_hots(idx_ref):
-    places = lax.broadcasted_iota(jnp.int32, (BAND, SIDE), 1)
-    rows, cols = [], []
+    places = lax.broadcasted_iota(jnp.int32, (SIDE, BAND), 0)
+    masks = []
     for layer in range(LAYERS):
-        idx = idx_ref[layer]
-        rows.append((idx // SIDE == places).astype(jnp.float32))
-        cols.append((idx % SIDE == places).astype(jnp.float32))
-    masks = [dot(r, c, ((0,), (0,))) for r, c in zip(rows, cols)]
+        idx = idx_ref[0, layer : layer + 1, :]
+        rows = (idx // SIDE == places).astype(jnp.float32)
+        cols = (idx % SIDE == places).astype(jnp.float32)
+        masks.append(dot(rows, cols, ((1,), (1,))))
     return jnp.concatenate(masks, axis=1)
 
 
@@ -201,7 +204,7 @@
         ),
         compiler_params=pltpu.CompilerParams(vmem_limit_bytes=4 * 2**20),
         name="encode",
-    )(parts, momentum, band_idx.reshape(LAYERS, BAND, 1), *matrices())
+    )(parts, momentum, band_idx, *matrices())
 
 
 def decode(every):
@@ -219,12 +222,17 @@
     exchange = functools.partial(lax.all_to_all, axis_name=axes, split_axis=0, concat_axis=0, tiled=True)
     place = lax.axis_index(axes)[None]
     acts = acts[0].transpose(1, 2, 0)
-    diagonal, across_z = gradient_terms(place, acts, grads, 1)
-    across_y, own = gradient_terms(place, acts, grads, 0)
-    diagonal = lax.ppermute(diagonal, axes, pairs(True, True))
-    across_z = lax.ppermute(across_z, axes, pairs(True, False))
-    across_y = lax.ppermute(across_y, axes, pairs(False, True))
-    terms = ((own + across_y) + (across_z + diagonal)).reshape(8, 6, SIDE, WIDE)
+    hop = functools.partial(lax.ppermute, axis_name=axes)
+    across_z, across_y = pairs(True, False), pairs(False, True)
+    far0_other, far0_own, left = gradient_terms(place, acts, grads, 0, 1)
+    far1_other, far1_own = gradient_terms(place, left, grads, 1, 1)
+    near0_other, near0_own = gradient_terms(place, left, grads, 0, 0)
+    near1_other, near1_own = gradient_terms(place, left, grads, 1, 0)
+    far0 = far0_own + hop(far0_other, perm=across_y)
+    other1 = near1_other + hop(far1_other, perm=across_z)
+    sum0 = near0_own + hop(near0_other, perm=across_y) + hop(far0, perm=across_z)
+    sum1 = near1_own + hop(far1_own, perm=across_z) + hop(other1, perm=across_y)
+    terms = jnp.concatenate([sum0, sum1]).reshape(8, 6, SIDE, WIDE)
     terms = exchange(terms, axis_index_groups=second)
     terms = jnp.sum(terms, axis=0)
     terms = exchange(terms, axis_index_groups=third)

time: 136 us -> 121 us (0.89)
  waiting for transfers between devices: 51.1 us -> 9.91 us
  blocking collectives: 42 us -> 63.5 us
  starting transfers between devices: 26.7 us -> 34.1 us
  local copies, waits for them, and re-layouts: 3.21 us -> 0.94 us
    ppermute x3 -> x6, waiting for transfers between devices: 36.9 us -> 9.91 us  [the longest x1 8.22 us: local(): hop(near0_other, perm=across_y)]
    all_to_all x0 -> x1, blocking collectives: none -> 21.7 us  [local(): terms = exchange(terms, axis_index_groups=third)]
    all_to_all x1 -> x0, waiting for transfers between devices: 14.2 us -> none  [local(): terms = exchange(terms, axis_index_groups=third)]
    ppermute x3 -> x6, starting transfers between devices: 22.4 us -> 34.1 us  [the longest x1 15.1 us: local(): other1 = near1_other + hop(far1_other, perm=across_z)]
    all_to_all x1 -> x0, starting transfers between devices: 4.31 us -> none  [local(): terms = exchange(terms, axis_index_groups=third)]
    unnamed x12, local copies, waits for them, and re-layouts: 3.12 us -> 0.94 us
    all_to_all x1, blocking collectives: 9.28 us -> 7.17 us  [local(): lax.all_to_all(sent, 'replica', split_axis=0, concat_axis=0, tiled=True)]
    all_to_all x1, blocking collectives: 32.7 us -> 34.6 us  [local(): terms = exchange(terms, axis_index_groups=second)]
  transfers between devices with their start and end apart: 4 -> 6, of which waited for: 4 -> 3; matrix products, arithmetic and copies ran while one was open for 0% -> 0% of each run, Pallas kernels for 3% -> 3%
where the time goes in v4:
time: 121 us; the launch traced here: 120 us
  blocking collectives  63.5 us (52%)
  starting transfers between devices  34.1 us (28%)
  Pallas kernels  10 us (8%)
  waiting for transfers between devices  9.91 us (8%)
    all_to_all x1, blocking collectives, local(): terms = exchange(terms, axis_index_groups=second)  34.6 us
    all_to_all x1, blocking collectives, local(): terms = exchange(terms, axis_index_groups=third)  21.7 us
    ppermute x1, starting transfers between devices, local(): other1 = near1_other + hop(far1_other, perm=across_z)  15.1 us
    ppermute x1, waiting for transfers between devices, local(): hop(near0_other, perm=across_y)  8.22 us
    pallas_call x4, Pallas kernels, gradient_terms(): pl.pallas_call(functools.partial(terms_kernel, first), grid_spec=pltpu.Pr...  7.44 us
    all_to_all x1, blocking collectives, local(): lax.all_to_all(sent, 'replica', split_axis=0, concat_axis=0, tiled=True)  7.17 us
    ppermute x2, starting transfers between devices, local(): sum1 = near1_own + hop(far1_own, perm=across_z) + hop(other1, perm=across_y)  7.16 us
    ppermute x1, starting transfers between devices, local(): far0 = far0_own + hop(far0_other, perm=across_y)  5.24 us
  transfers between devices with their start and end apart: 6, of which 3 were waited for; matrix products, arithmetic and copies ran while one was open for 0% of the time, Pallas kernels for 3%

profile of v4, /device:TPU:1, one launch (start us, length us, event | category | flops | bytes accessed | tf_op | source)
XLA Modules:
  0.0 120.1 jit_solution(2731528203902567211)
XLA Ops:
  0.7 0.9 copy-done.2
  1.6 2.7 %terms01.1 = (f32[2,2,3,2,64,128]{5,4,3,2,1,0:T(8,128)S(1)}, f32[2,2,3,2,64,128]{5,4,3,2,1,0:T(8,128)S(1)}, bf16[384,512]{1,0:T(8,128)(2,1)S(1)}) custom-call(s32[1]{0:T(128)} %bitcast.place_ref, bf16[2,192,256]{2,1,0:T(8,128)(2,1)S(1)} %bitcast.5, bf16[1,256,2,4096]{3,2,1,0:T(2,128)(2,1)} %grad_ref.7), custom_call_target="tpu_custom_call" | custom-call | tf_op jit(solution)/shard_map/terms01/pallas_call | solution.py:138
  4.3 1.6 %terms11.1 = (f32[2,2,3,2,64,128]{5,4,3,2,1,0:T(8,128)S(1)}, f32[2,2,3,2,64,128]{5,4,3,2,1,0:T(8,128)S(1)}) custom-call(s32[1]{0:T(128)} %bitcast.place_ref, bf16[384,512]{1,0:T(8,128)(2,1)S(1)} %get-tuple-element.13.in_ref, bf16[1,256,2,4096]{3,2,1,0:T(2,128)(2,1)S(1)} %copy-done), custom_call_target="tpu_custom_call" | custom-call | tf_op jit(solution)/shard_map/terms11/pallas_call | solution.py:138
  5.9 15.1 %collective-permute-start.4 = (f32[2,2,3,2,64,128]{5,4,3,2,1,0:T(8,128)S(1)}, f32[2,2,3,2,64,128]{5,4,3,2,1,0:T(8,128)S(1)}, u32[]{:S(2)}, u32[]{:S(2)}) collective-permute-start(f32[2,2,3,2,64,128]{5,4,3,2,1,0:T(8,128)S(1)} %get-tuple-element.21), channel_id=1, source_target_pairs={{0,16},{1,17},{2,18},{3,19},{4,20},{5,21},{6,22},{7,23},{8,24},{9,... | collective-permute-start | bytes 2359304 | tf_op jit(solution)/shard_map/ppermute | solution.py:232
  21.0 5.2 %collective-permute-start.1 = (f32[2,2,3,2,64,128]{5,4,3,2,1,0:T(8,128)S(1)}, f32[2,2,3,2,64,128]{5,4,3,2,1,0:T(8,128)S(1)}, u32[]{:S(2)}, u32[]{:S(2)}) collective-permute-start(f32[2,2,3,2,64,128]{5,4,3,2,1,0:T(8,128)S(1)} %get-tuple-element.17), channel_id=1, source_target_pairs={{0,1},{1,0},{2,3},{3,2},{4,5},{5,4},{6,7},{7,6},{8,9},{9,8},{10,11... | collective-permute-start | bytes 2359304 | tf_op jit(solution)/shard_map/ppermute | solution.py:231
  26.3 1.9 %collective-permute-start.3 = (f32[2,2,3,2,64,128]{5,4,3,2,1,0:T(8,128)S(1)}, f32[2,2,3,2,64,128]{5,4,3,2,1,0:T(8,128)S(1)}, u32[]{:S(2)}, u32[]{:S(2)}) collective-permute-start(f32[2,2,3,2,64,128]{5,4,3,2,1,0:T(8,128)S(1)} %get-tuple-element.19), channel_id=1, source_target_pairs={{0,16},{1,17},{2,18},{3,19},{4,20},{5,21},{6,22},{7,23},{8,24},{9,... | collective-permute-start | bytes 2359304 | tf_op jit(solution)/shard_map/ppermute | solution.py:234
  28.2 1.6 %terms10.1 = (f32[2,2,3,2,64,128]{5,4,3,2,1,0:T(8,128)S(1)}, f32[2,2,3,2,64,128]{5,4,3,2,1,0:T(8,128)S(1)}) custom-call(s32[1]{0:T(128)} %bitcast.place_ref, bf16[384,512]{1,0:T(8,128)(2,1)S(1)} %get-tuple-element.13.in_ref, bf16[1,256,2,4096]{3,2,1,0:T(2,128)(2,1)S(1)} %copy-done), custom_call_target="tpu_custom_call" | custom-call | tf_op jit(solution)/shard_map/terms10/pallas_call | solution.py:138
  29.8 0.6 collective-permute-done.4
  30.4 0.1 add.26
  30.5 5.2 %collective-permute-start.5 = (f32[2,2,3,2,64,128]{5,4,3,2,1,0:T(8,128)S(1)}, f32[2,2,3,2,64,128]{5,4,3,2,1,0:T(8,128)S(1)}, u32[]{:S(2)}, u32[]{:S(2)}) collective-permute-start(f32[2,2,3,2,64,128]{5,4,3,2,1,0:T(8,128)S(1)} %add.26), channel_id=1, source_target_pairs={{0,1},{1,0},{2,3},{3,2},{4,5},{5,4},{6,7},{7,6},{8,9},{9,8},{10,11... | collective-permute-start | bytes 2359304 | tf_op jit(solution)/shard_map/ppermute | solution.py:234
  35.8 1.6 %terms00.1 = (f32[2,2,3,2,64,128]{5,4,3,2,1,0:T(8,128)S(1)}, f32[2,2,3,2,64,128]{5,4,3,2,1,0:T(8,128)S(1)}) custom-call(s32[1]{0:T(128)} %bitcast.place_ref, bf16[384,512]{1,0:T(8,128)(2,1)S(1)} %get-tuple-element.13.in_ref, bf16[1,256,2,4096]{3,2,1,0:T(2,128)(2,1)S(1)} %copy-done), custom_call_target="tpu_custom_call" | custom-call | tf_op jit(solution)/shard_map/terms00/pallas_call | solution.py:138
  37.4 2.0 %collective-permute-start = (f32[2,2,3,2,64,128]{5,4,3,2,1,0:T(8,128)S(1)}, f32[2,2,3,2,64,128]{5,4,3,2,1,0:T(8,128)S(1)}, u32[]{:S(2)}, u32[]{:S(2)}) collective-permute-start(f32[2,2,3,2,64,128]{5,4,3,2,1,0:T(8,128)S(1)} %get-tuple-element.15), channel_id=1, source_target_pairs={{0,1},{1,0},{2,3},{3,2},{4,5},{5,4},{6,7},{7,6},{8,9},{9,8},{10,11... | collective-permute-start | bytes 2359304 | tf_op jit(solution)/shard_map/ppermute | solution.py:233
  39.4 0.1 add.23
  39.5 4.6 %collective-permute-start.2 = (f32[2,2,3,2,64,128]{5,4,3,2,1,0:T(8,128)S(1)}, f32[2,2,3,2,64,128]{5,4,3,2,1,0:T(8,128)S(1)}, u32[]{:S(2)}, u32[]{:S(2)}) collective-permute-start(f32[2,2,3,2,64,128]{5,4,3,2,1,0:T(8,128)S(1)} %add.23), channel_id=1, source_target_pairs={{0,16},{1,17},{2,18},{3,19},{4,20},{5,21},{6,22},{7,23},{8,24},{9,... | collective-permute-start | bytes 2359304 | tf_op jit(solution)/shard_map/ppermute | solution.py:233
  44.1 1.1 collective-permute-done.5
  45.1 0.2 add_add_fusion
  45.3 8.2 %collective-permute-done = f32[2,2,3,2,64,128]{5,4,3,2,1,0:T(8,128)S(1)} collective-permute-done((f32[2,2,3,2,64,128]{5,4,3,2,1,0:T(8,128)S(1)}, f32[2,2,3,2,64,128]{5,4,3,2,1,0:T(8,128)S(1)}, u32[]{:S(2)}, u32[]{:S(2)}) %collective-permute-start) | collective-permute-done | bytes 786464 | tf_op jit(solution)/shard_map/ppermute | solution.py:233
  53.6 0.2 add_add_fusion.1
  53.8 0.1 pad_maximum_fusion
  53.9 34.6 %all_to_all.15 = f32[8,6,64,128]{3,2,1,0:T(8,128)S(1)} all-to-all(f32[8,6,64,128]{3,2,1,0:T(8,128)S(1)} %bitcast.6), channel_id=1, replica_groups={{0,2,32,34,8,10,40,42},{4,6,36,38,12,14,44,46},{64,66,96,98,72,74,104,1..., dimensions={0} | all-to-all | bytes 3145728 | tf_op jit(solution)/shard_map/all_to_all | solution.py:236
  88.6 21.7 %all_to_all.16.parts_ref = f32[6,64,128]{2,1,0:T(8,128)S(1)} all-to-all(f32[6,64,128]{2,1,0:T(8,128)S(1)} %reduce_sum.9), channel_id=1, replica_groups={{0,4,64,68,128,132},{1,5,65,69,129,133},{2,6,66,70,130,134},{3,7,67,71,..., dimensions={0} | all-to-all | bytes 393216 | tf_op jit(solution)/shard_map/all_to_all | solution.py:238
  110.3 1.6 %encode.1 = (f32[1,1,64,128]{3,2,1,0:T(8,128)}, f32[4,64,128]{2,1,0:T(8,128)S(1)}) custom-call(f32[6,64,128]{2,1,0:T(8,128)S(1)} %all_to_all.16.parts_ref, f32[1,1,64,128]{3,2,1,0:T(8,128)S(1)} %copy-done.4, s32[1,2,32]{2,1,0:T(2,128)S(1)} %copy-done.5, f32[64,64]{1,0:T(8,128)S(1)} %copy-done.3, f32[128,128]{1,0:T(8,128)S(1)} %copy-done.1), custom_call_target="tpu_custom_call" | custom-call | tf_op jit(solution)/shard_map/encode/pallas_call | solution.py:199
  111.9 7.2 %all_to_all.17.every_ref = f32[4,64,128]{2,1,0:T(8,128)S(1)} all-to-all(f32[4,64,128]{2,1,0:T(8,128)S(1)} %get-tuple-element.23), channel_id=1, replica_groups=mesh['replica'=4,'shard'=192] {'replica'}, dimensions={0} | all-to-all | bytes 262144 | tf_op jit(solution)/shard_map/all_to_all | solution.py:240
  119.1 1.0 decode.1
  (15 shorter events, 0.1 us)
Async XLA Ops:
  0.6 0.9 copy-start.2
  1.6 2.7 %copy-start = (bf16[1,256,2,4096]{3,2,1,0:T(2,128)(2,1)S(1)}, bf16[1,256,2,4096]{3,2,1,0:T(2,128)(2,1)}, u32[]{:S(2)}) copy-start(bf16[1,256,2,4096]{3,2,1,0:T(2,128)(2,1)} %grad_ref.7) | copy-start | bytes 12582916
  5.9 24.5 %collective-permute-start.4 = (f32[2,2,3,2,64,128]{5,4,3,2,1,0:T(8,128)S(1)}, f32[2,2,3,2,64,128]{5,4,3,2,1,0:T(8,128)S(1)}, u32[]{:S(2)}, u32[]{:S(2)}) collective-permute-start(f32[2,2,3,2,64,128]{5,4,3,2,1,0:T(8,128)S(1)} %get-tuple-element.21), channel_id=1, source_target_pairs={{0,16},{1,17},{2,18},{3,19},{4,20},{5,21},{6,22},{7,23},{8,24},{9,... | collective-permute-start | bytes 2359304 | tf_op jit(solution)/shard_map/ppermute | solution.py:232
  21.0 18.3 %collective-permute-start.1 = (f32[2,2,3,2,64,128]{5,4,3,2,1,0:T(8,128)S(1)}, f32[2,2,3,2,64,128]{5,4,3,2,1,0:T(8,128)S(1)}, u32[]{:S(2)}, u32[]{:S(2)}) collective-permute-start(f32[2,2,3,2,64,128]{5,4,3,2,1,0:T(8,128)S(1)} %get-tuple-element.17), channel_id=1, source_target_pairs={{0,1},{1,0},{2,3},{3,2},{4,5},{5,4},{6,7},{7,6},{8,9},{9,8},{10,11... | collective-permute-start | bytes 2359304 | tf_op jit(solution)/shard_map/ppermute | solution.py:231
  26.3 17.8 %collective-permute-start.3 = (f32[2,2,3,2,64,128]{5,4,3,2,1,0:T(8,128)S(1)}, f32[2,2,3,2,64,128]{5,4,3,2,1,0:T(8,128)S(1)}, u32[]{:S(2)}, u32[]{:S(2)}) collective-permute-start(f32[2,2,3,2,64,128]{5,4,3,2,1,0:T(8,128)S(1)} %get-tuple-element.19), channel_id=1, source_target_pairs={{0,16},{1,17},{2,18},{3,19},{4,20},{5,21},{6,22},{7,23},{8,24},{9,... | collective-permute-start | bytes 2359304 | tf_op jit(solution)/shard_map/ppermute | solution.py:234
  30.5 14.6 %collective-permute-start.5 = (f32[2,2,3,2,64,128]{5,4,3,2,1,0:T(8,128)S(1)}, f32[2,2,3,2,64,128]{5,4,3,2,1,0:T(8,128)S(1)}, u32[]{:S(2)}, u32[]{:S(2)}) collective-permute-start(f32[2,2,3,2,64,128]{5,4,3,2,1,0:T(8,128)S(1)} %add.26), channel_id=1, source_target_pairs={{0,1},{1,0},{2,3},{3,2},{4,5},{5,4},{6,7},{7,6},{8,9},{9,8},{10,11... | collective-permute-start | bytes 2359304 | tf_op jit(solution)/shard_map/ppermute | solution.py:234
  37.4 16.2 %collective-permute-start = (f32[2,2,3,2,64,128]{5,4,3,2,1,0:T(8,128)S(1)}, f32[2,2,3,2,64,128]{5,4,3,2,1,0:T(8,128)S(1)}, u32[]{:S(2)}, u32[]{:S(2)}) collective-permute-start(f32[2,2,3,2,64,128]{5,4,3,2,1,0:T(8,128)S(1)} %get-tuple-element.15), channel_id=1, source_target_pairs={{0,1},{1,0},{2,3},{3,2},{4,5},{5,4},{6,7},{7,6},{8,9},{9,8},{10,11... | collective-permute-start | bytes 2359304 | tf_op jit(solution)/shard_map/ppermute | solution.py:233
  39.5 14.1 %collective-permute-start.2 = (f32[2,2,3,2,64,128]{5,4,3,2,1,0:T(8,128)S(1)}, f32[2,2,3,2,64,128]{5,4,3,2,1,0:T(8,128)S(1)}, u32[]{:S(2)}, u32[]{:S(2)}) collective-permute-start(f32[2,2,3,2,64,128]{5,4,3,2,1,0:T(8,128)S(1)} %add.23), channel_id=1, source_target_pairs={{0,16},{1,17},{2,18},{3,19},{4,20},{5,21},{6,22},{7,23},{8,24},{9,... | collective-permute-start | bytes 2359304 | tf_op jit(solution)/shard_map/ppermute | solution.py:233
  88.5 21.8 %copy-start.1 = (f32[128,128]{1,0:T(8,128)S(1)}, f32[128,128]{1,0:T(8,128)}, u32[]{:S(2)}) copy-start(f32[128,128]{1,0:T(8,128)} %constant.15.clone.wide_ref) | copy-start | bytes 196612
  88.5 21.8 %copy-start.3 = (f32[64,64]{1,0:T(8,128)S(1)}, f32[64,64]{1,0:T(8,128)}, u32[]{:S(2)}) copy-start(f32[64,64]{1,0:T(8,128)} %constant.14.clone.left_ref) | copy-start | bytes 49156
  88.5 21.8 %copy-start.4 = (f32[1,1,64,128]{3,2,1,0:T(8,128)S(1)}, f32[1,1,64,128]{3,2,1,0:T(8,128)}, u32[]{:S(2)}) copy-start(f32[1,1,64,128]{3,2,1,0:T(8,128)} %mom_ref.1) | copy-start | bytes 98308
  88.5 21.8 %copy-start.5 = (s32[1,2,32]{2,1,0:T(2,128)S(1)}, s32[1,2,32]{2,1,0:T(2,128)}, u32[]{:S(2)}) copy-start(s32[1,2,32]{2,1,0:T(2,128)} %idx_ref.1) | copy-start | bytes 772

commit v5 on v4

--- a/solution.py
+++ b/solution.py
@@ -31,7 +31,7 @@
     return (((at + size - core) ^ 1) + core) % size
 
 
-def pairs(across_z, across_y):
+def pairs(across_z, across_y, across_x=False):
     return [
         (
             flat(x_lo, core, z, x_hi, y),
@@ -39,7 +39,7 @@
                 x_lo,
                 core,
                 partner(z, core, Z) if across_z else z,
-                x_hi,
+                1 - x_hi if across_x else x_hi,
                 partner(y, core, Y) if across_y else y,
             ),
         )
@@ -52,30 +52,20 @@
 
 
 def stage_groups():
-    second, third = [], []
-    for x_lo in range(2):
-        for core in range(2):
-            for z0 in range(2):
-                for y0 in range(2):
-                    for m in range(core, 6 + core, 2):
-                        for n in range(core, 4 + core, 2):
-                            pz = sorted((m % 6, (m + 1) % 6), key=lambda v: v % 2)
-                            py = sorted((n % 4, (n + 1) % 4), key=lambda v: v % 2)
-                            second.append(
-                                [
-                                    flat(x_lo, core, 2 * a + z0, h, 2 * b + y0)
-                                    for h in range(2)
-                                    for a in pz
-                                    for b in py
-                                ]
-                            )
-            for x_hi in range(2):
-                for z in range(4):
-                    for y in range(4):
-                        third.append(
-                            [flat(x_lo, core, 4 * a + z, x_hi, 4 * b + y) for a in range(3) for b in range(2)]
-                        )
-    return second, third
+    return [
+        [
+            flat(x_lo, core, 4 * a + 2 * z1 + z0, x_hi, 4 * b + 2 * y1 + y0)
+            for z1 in range(2)
+            for y1 in range(2)
+            for a in range(Z // 4)
+            for b in range(Y // 4)
+        ]
+        for x_lo in range(2)
+        for core in range(2)
+        for x_hi in range(2)
+        for z0 in range(2)
+        for y0 in range(2)
+    ]
 
 
 def dct_matrix():
@@ -86,7 +76,7 @@
 
 
 def parities(place_ref):
-    return (place_ref[0] >> 4) & 1, place_ref[0] & 1
+    return (place_ref[0] >> 4) & 1, place_ref[0] & 1, (place_ref[0] >> 3) & 1
 
 
 def left_kernel_part(act_ref, left_ref):
@@ -121,7 +111,7 @@
                 even_ref[0, pair % 2, a, pair // 2] = jnp.where(low, one, pltpu.roll(two, SIDE, 1))
                 odd_ref[0, pair % 2, a, pair // 2] = jnp.where(low, pltpu.roll(one, SIDE, 1), two)
 
-    _, y_own = parities(place_ref)
+    _, y_own, _ = parities(place_ref)
     pl.when(y_own == 0)(lambda: write(own_ref, other_ref))
     pl.when(y_own == 1)(lambda: write(other_ref, own_ref))
 
@@ -144,7 +134,12 @@
                 pl.BlockSpec(acts_or_left.shape, lambda k, place: (0, 0, 0)) if first else left_spec,
                 pl.BlockSpec(
                     (1, tokens, LAYERS, CHUNK),
-                    lambda k, place: (0, 0, 0, k * 4 + (parities(place)[0] ^ far) * 2 + colour),
+                    lambda k, place: (
+                        0,
+                        0,
+                        0,
+                        k * 4 + (parities(place)[0] ^ far) * 2 + (parities(place)[2] ^ colour),
+                    ),
                 ),
             ],
             out_specs=[out_spec, out_spec] + [left_spec] * first,
@@ -217,13 +212,12 @@
 
 
 def local(acts, grads, momentum, band_idx):
-    second, third = stage_groups()
     axes = ("replica", "shard")
     exchange = functools.partial(lax.all_to_all, axis_name=axes, split_axis=0, concat_axis=0, tiled=True)
     place = lax.axis_index(axes)[None]
     acts = acts[0].transpose(1, 2, 0)
     hop = functools.partial(lax.ppermute, axis_name=axes)
-    across_z, across_y = pairs(True, False), pairs(False, True)
+    across_z, across_y, across_x = pairs(True, False), pairs(False, True), pairs(False, False, True)
     far0_other, far0_own, left = gradient_terms(place, acts, grads, 0, 1)
     far1_other, far1_own = gradient_terms(place, left, grads, 1, 1)
     near0_other, near0_own = gradient_terms(place, left, grads, 0, 0)
@@ -232,10 +226,8 @@
     other1 = near1_other + hop(far1_other, perm=across_z)
     sum0 = near0_own + hop(near0_other, perm=across_y) + hop(far0, perm=across_z)
     sum1 = near1_own + hop(far1_own, perm=across_z) + hop(other1, perm=across_y)
-    terms = jnp.concatenate([sum0, sum1]).reshape(8, 6, SIDE, WIDE)
-    terms = exchange(terms, axis_index_groups=second)
-    terms = jnp.sum(terms, axis=0)
-    terms = exchange(terms, axis_index_groups=third)
+    terms = (sum0 + hop(sum1, perm=across_x)).reshape(24, SIDE, WIDE)
+    terms = exchange(terms, axis_index_groups=stage_groups())
     new_momentum, sent = encode(terms, momentum, band_idx)
     every = lax.all_to_all(sent, "replica", split_axis=0, concat_axis=0, tiled=True)
     update = decode(every)

time: 121 us -> 122 us (level)
  the two profiles are of different devices: /device:TPU:1 before, /device:TPU:16 now
where the time goes in v5:
time: 122 us; the launch traced here: 121 us
  blocking collectives  67.6 us (55%)
  starting transfers between devices  24.6 us (20%)
  waiting for transfers between devices  16.5 us (14%)
  Pallas kernels  10.2 us (8%)
    all_to_all x1, blocking collectives, local(): terms = exchange(terms, axis_index_groups=stage_groups())  60.5 us
    ppermute x1, waiting for transfers between devices, local(): terms = (sum0 + hop(sum1, perm=across_x)).reshape(24, SIDE, WIDE)  8.09 us
    pallas_call x4, Pallas kernels, gradient_terms(): pl.pallas_call(functools.partial(terms_kernel, first), grid_spec=pltpu.Pr...  7.56 us
    all_to_all x1, blocking collectives, local(): lax.all_to_all(sent, 'replica', split_axis=0, concat_axis=0, tiled=True)  7.16 us
    ppermute x2, starting transfers between devices, local(): sum1 = near1_own + hop(far1_own, perm=across_z) + hop(other1, perm=across_y)  5.55 us
    ppermute x1, starting transfers between devices, local(): terms = (sum0 + hop(sum1, perm=across_x)).reshape(24, SIDE, WIDE)  4.93 us
    ppermute x1, starting transfers between devices, local(): other1 = near1_other + hop(far1_other, perm=across_z)  4.28 us
    ppermute x1, starting transfers between devices, local(): hop(far0, perm=across_z)  3.92 us
  transfers between devices with their start and end apart: 7, of which 4 were waited for; matrix products, arithmetic and copies ran while one was open for 0% of the time, Pallas kernels for 3%

profile of v5, /device:TPU:16, one launch (start us, length us, event | category | flops | bytes accessed | tf_op | source)
XLA Modules:
  0.0 121.5 jit_solution(12469387513239494387)
XLA Ops:
  0.7 1.1 copy-done.2
  1.7 2.9 %terms01.1 = (f32[2,2,3,2,64,128]{5,4,3,2,1,0:T(8,128)S(1)}, f32[2,2,3,2,64,128]{5,4,3,2,1,0:T(8,128)S(1)}, bf16[384,512]{1,0:T(8,128)(2,1)S(1)}) custom-call(s32[1]{0:T(128)} %bitcast.place_ref, bf16[2,192,256]{2,1,0:T(8,128)(2,1)S(1)} %bitcast.5, bf16[1,256,2,4096]{3,2,1,0:T(2,128)(2,1)} %grad_ref.7), custom_call_target="tpu_custom_call" | custom-call | tf_op jit(solution)/shard_map/terms01/pallas_call | solution.py:128
  4.6 1.6 %terms11.1 = (f32[2,2,3,2,64,128]{5,4,3,2,1,0:T(8,128)S(1)}, f32[2,2,3,2,64,128]{5,4,3,2,1,0:T(8,128)S(1)}) custom-call(s32[1]{0:T(128)} %bitcast.place_ref, bf16[384,512]{1,0:T(8,128)(2,1)S(1)} %get-tuple-element.13.in_ref, bf16[1,256,2,4096]{3,2,1,0:T(2,128)(2,1)S(1)} %copy-done), custom_call_target="tpu_custom_call" | custom-call | tf_op jit(solution)/shard_map/terms11/pallas_call | solution.py:128
  6.2 4.3 %collective-permute-start.4 = (f32[2,2,3,2,64,128]{5,4,3,2,1,0:T(8,128)S(1)}, f32[2,2,3,2,64,128]{5,4,3,2,1,0:T(8,128)S(1)}, u32[]{:S(2)}, u32[]{:S(2)}) collective-permute-start(f32[2,2,3,2,64,128]{5,4,3,2,1,0:T(8,128)S(1)} %get-tuple-element.21), channel_id=1, source_target_pairs={{0,16},{1,17},{2,18},{3,19},{4,20},{5,21},{6,22},{7,23},{8,24},{9,... | collective-permute-start | bytes 2359304 | tf_op jit(solution)/shard_map/ppermute | solution.py:226
  10.5 3.6 %collective-permute-start.1 = (f32[2,2,3,2,64,128]{5,4,3,2,1,0:T(8,128)S(1)}, f32[2,2,3,2,64,128]{5,4,3,2,1,0:T(8,128)S(1)}, u32[]{:S(2)}, u32[]{:S(2)}) collective-permute-start(f32[2,2,3,2,64,128]{5,4,3,2,1,0:T(8,128)S(1)} %get-tuple-element.17), channel_id=1, source_target_pairs={{0,1},{1,0},{2,3},{3,2},{4,5},{5,4},{6,7},{7,6},{8,9},{9,8},{10,11... | collective-permute-start | bytes 2359304 | tf_op jit(solution)/shard_map/ppermute | solution.py:225
  14.1 1.9 %collective-permute-start.3 = (f32[2,2,3,2,64,128]{5,4,3,2,1,0:T(8,128)S(1)}, f32[2,2,3,2,64,128]{5,4,3,2,1,0:T(8,128)S(1)}, u32[]{:S(2)}, u32[]{:S(2)}) collective-permute-start(f32[2,2,3,2,64,128]{5,4,3,2,1,0:T(8,128)S(1)} %get-tuple-element.19), channel_id=1, source_target_pairs={{0,16},{1,17},{2,18},{3,19},{4,20},{5,21},{6,22},{7,23},{8,24},{9,... | collective-permute-start | bytes 2359304 | tf_op jit(solution)/shard_map/ppermute | solution.py:228
  16.0 1.6 %terms10.1 = (f32[2,2,3,2,64,128]{5,4,3,2,1,0:T(8,128)S(1)}, f32[2,2,3,2,64,128]{5,4,3,2,1,0:T(8,128)S(1)}) custom-call(s32[1]{0:T(128)} %bitcast.place_ref, bf16[384,512]{1,0:T(8,128)(2,1)S(1)} %get-tuple-element.13.in_ref, bf16[1,256,2,4096]{3,2,1,0:T(2,128)(2,1)S(1)} %copy-done), custom_call_target="tpu_custom_call" | custom-call | tf_op jit(solution)/shard_map/terms10/pallas_call | solution.py:128
  17.6 2.8 %collective-permute-done.4 = f32[2,2,3,2,64,128]{5,4,3,2,1,0:T(8,128)S(1)} collective-permute-done((f32[2,2,3,2,64,128]{5,4,3,2,1,0:T(8,128)S(1)}, f32[2,2,3,2,64,128]{5,4,3,2,1,0:T(8,128)S(1)}, u32[]{:S(2)}, u32[]{:S(2)}) %collective-permute-start.4) | collective-permute-done | bytes 786464 | tf_op jit(solution)/shard_map/ppermute | solution.py:226
  20.4 0.1 add.29
  20.5 3.6 %collective-permute-start.5 = (f32[2,2,3,2,64,128]{5,4,3,2,1,0:T(8,128)S(1)}, f32[2,2,3,2,64,128]{5,4,3,2,1,0:T(8,128)S(1)}, u32[]{:S(2)}, u32[]{:S(2)}) collective-permute-start(f32[2,2,3,2,64,128]{5,4,3,2,1,0:T(8,128)S(1)} %add.29), channel_id=1, source_target_pairs={{0,1},{1,0},{2,3},{3,2},{4,5},{5,4},{6,7},{7,6},{8,9},{9,8},{10,11... | collective-permute-start | bytes 2359304 | tf_op jit(solution)/shard_map/ppermute | solution.py:228
  24.2 1.6 %terms00.1 = (f32[2,2,3,2,64,128]{5,4,3,2,1,0:T(8,128)S(1)}, f32[2,2,3,2,64,128]{5,4,3,2,1,0:T(8,128)S(1)}) custom-call(s32[1]{0:T(128)} %bitcast.place_ref, bf16[384,512]{1,0:T(8,128)(2,1)S(1)} %get-tuple-element.13.in_ref, bf16[1,256,2,4096]{3,2,1,0:T(2,128)(2,1)S(1)} %copy-done), custom_call_target="tpu_custom_call" | custom-call | tf_op jit(solution)/shard_map/terms00/pallas_call | solution.py:128
  25.8 2.3 %collective-permute-start = (f32[2,2,3,2,64,128]{5,4,3,2,1,0:T(8,128)S(1)}, f32[2,2,3,2,64,128]{5,4,3,2,1,0:T(8,128)S(1)}, u32[]{:S(2)}, u32[]{:S(2)}) collective-permute-start(f32[2,2,3,2,64,128]{5,4,3,2,1,0:T(8,128)S(1)} %get-tuple-element.15), channel_id=1, source_target_pairs={{0,1},{1,0},{2,3},{3,2},{4,5},{5,4},{6,7},{7,6},{8,9},{9,8},{10,11... | collective-permute-start | bytes 2359304 | tf_op jit(solution)/shard_map/ppermute | solution.py:227
  28.1 0.1 add.26
  28.2 3.9 %collective-permute-start.2 = (f32[2,2,3,2,64,128]{5,4,3,2,1,0:T(8,128)S(1)}, f32[2,2,3,2,64,128]{5,4,3,2,1,0:T(8,128)S(1)}, u32[]{:S(2)}, u32[]{:S(2)}) collective-permute-start(f32[2,2,3,2,64,128]{5,4,3,2,1,0:T(8,128)S(1)} %add.26), channel_id=1, source_target_pairs={{0,16},{1,17},{2,18},{3,19},{4,20},{5,21},{6,22},{7,23},{8,24},{9,... | collective-permute-start | bytes 2359304 | tf_op jit(solution)/shard_map/ppermute | solution.py:227
  32.1 2.3 %collective-permute-done.5 = f32[2,2,3,2,64,128]{5,4,3,2,1,0:T(8,128)S(1)} collective-permute-done((f32[2,2,3,2,64,128]{5,4,3,2,1,0:T(8,128)S(1)}, f32[2,2,3,2,64,128]{5,4,3,2,1,0:T(8,128)S(1)}, u32[]{:S(2)}, u32[]{:S(2)}) %collective-permute-start.5) | collective-permute-done | bytes 786464 | tf_op jit(solution)/shard_map/ppermute | solution.py:228
  34.4 0.2 add_add_fusion
  34.6 4.9 %collective-permute-start.6 = (f32[2,2,3,2,64,128]{5,4,3,2,1,0:T(8,128)S(1)}, f32[2,2,3,2,64,128]{5,4,3,2,1,0:T(8,128)S(1)}, u32[]{:S(2)}, u32[]{:S(2)}) collective-permute-start(f32[2,2,3,2,64,128]{5,4,3,2,1,0:T(8,128)S(1)} %add_add_fusion), channel_id=1, source_target_pairs={{0,8},{1,9},{2,10},{3,11},{4,12},{5,13},{6,14},{7,15},{8,0},{9,1},... | collective-permute-start | bytes 2359304 | tf_op jit(solution)/shard_map/ppermute | solution.py:229
  39.6 3.3 %collective-permute-done = f32[2,2,3,2,64,128]{5,4,3,2,1,0:T(8,128)S(1)} collective-permute-done((f32[2,2,3,2,64,128]{5,4,3,2,1,0:T(8,128)S(1)}, f32[2,2,3,2,64,128]{5,4,3,2,1,0:T(8,128)S(1)}, u32[]{:S(2)}, u32[]{:S(2)}) %collective-permute-start) | collective-permute-done | bytes 786464 | tf_op jit(solution)/shard_map/ppermute | solution.py:227
  42.9 8.1 %collective-permute-done.6 = f32[2,2,3,2,64,128]{5,4,3,2,1,0:T(8,128)S(1)} collective-permute-done((f32[2,2,3,2,64,128]{5,4,3,2,1,0:T(8,128)S(1)}, f32[2,2,3,2,64,128]{5,4,3,2,1,0:T(8,128)S(1)}, u32[]{:S(2)}, u32[]{:S(2)}) %collective-permute-start.6) | collective-permute-done | bytes 786464 | tf_op jit(solution)/shard_map/ppermute | solution.py:229
  50.9 0.3 add_add_fusion.1
  51.2 60.5 %all_to_all.10.parts_ref = f32[24,64,128]{2,1,0:T(8,128)S(1)} all-to-all(f32[24,64,128]{2,1,0:T(8,128)S(1)} %bitcast.6), channel_id=1, replica_groups={{0,4,64,68,128,132,2,6,66,70,130,134,32,36,96,100,160,164,34,38,98,102,..., dimensions={0} | all-to-all | bytes 1572864 | tf_op jit(solution)/shard_map/all_to_all | solution.py:230
  111.7 1.6 %encode.1 = (f32[1,1,64,128]{3,2,1,0:T(8,128)}, f32[4,64,128]{2,1,0:T(8,128)S(1)}) custom-call(f32[24,64,128]{2,1,0:T(8,128)S(1)} %all_to_all.10.parts_ref, f32[1,1,64,128]{3,2,1,0:T(8,128)S(1)} %copy-done.4, s32[1,2,32]{2,1,0:T(2,128)S(1)} %copy-done.5, f32[64,64]{1,0:T(8,128)S(1)} %copy-done.3, f32[128,128]{1,0:T(8,128)S(1)} %copy-done.1), custom_call_target="tpu_custom_call" | custom-call | tf_op jit(solution)/shard_map/encode/pallas_call | solution.py:194
  113.3 7.2 %all_to_all.11.every_ref = f32[4,64,128]{2,1,0:T(8,128)S(1)} all-to-all(f32[4,64,128]{2,1,0:T(8,128)S(1)} %get-tuple-element.23), channel_id=1, replica_groups=mesh['replica'=4,'shard'=192] {'replica'}, dimensions={0} | all-to-all | bytes 262144 | tf_op jit(solution)/shard_map/all_to_all | solution.py:232
  120.4 1.0 decode.1
  (14 shorter events, 0.0 us)
Async XLA Ops:
  0.6 3.9 %copy-start = (bf16[1,256,2,4096]{3,2,1,0:T(2,128)(2,1)S(1)}, bf16[1,256,2,4096]{3,2,1,0:T(2,128)(2,1)}, u32[]{:S(2)}) copy-start(bf16[1,256,2,4096]{3,2,1,0:T(2,128)(2,1)} %grad_ref.7) | copy-start | bytes 12582916
  0.7 1.1 copy-start.2
  6.2 14.2 %collective-permute-start.4 = (f32[2,2,3,2,64,128]{5,4,3,2,1,0:T(8,128)S(1)}, f32[2,2,3,2,64,128]{5,4,3,2,1,0:T(8,128)S(1)}, u32[]{:S(2)}, u32[]{:S(2)}) collective-permute-start(f32[2,2,3,2,64,128]{5,4,3,2,1,0:T(8,128)S(1)} %get-tuple-element.21), channel_id=1, source_target_pairs={{0,16},{1,17},{2,18},{3,19},{4,20},{5,21},{6,22},{7,23},{8,24},{9,... | collective-permute-start | bytes 2359304 | tf_op jit(solution)/shard_map/ppermute | solution.py:226
  10.5 17.6 %collective-permute-start.1 = (f32[2,2,3,2,64,128]{5,4,3,2,1,0:T(8,128)S(1)}, f32[2,2,3,2,64,128]{5,4,3,2,1,0:T(8,128)S(1)}, u32[]{:S(2)}, u32[]{:S(2)}) collective-permute-start(f32[2,2,3,2,64,128]{5,4,3,2,1,0:T(8,128)S(1)} %get-tuple-element.17), channel_id=1, source_target_pairs={{0,1},{1,0},{2,3},{3,2},{4,5},{5,4},{6,7},{7,6},{8,9},{9,8},{10,11... | collective-permute-start | bytes 2359304 | tf_op jit(solution)/shard_map/ppermute | solution.py:225
  14.1 18.0 %collective-permute-start.3 = (f32[2,2,3,2,64,128]{5,4,3,2,1,0:T(8,128)S(1)}, f32[2,2,3,2,64,128]{5,4,3,2,1,0:T(8,128)S(1)}, u32[]{:S(2)}, u32[]{:S(2)}) collective-permute-start(f32[2,2,3,2,64,128]{5,4,3,2,1,0:T(8,128)S(1)} %get-tuple-element.19), channel_id=1, source_target_pairs={{0,16},{1,17},{2,18},{3,19},{4,20},{5,21},{6,22},{7,23},{8,24},{9,... | collective-permute-start | bytes 2359304 | tf_op jit(solution)/shard_map/ppermute | solution.py:228
  20.5 13.9 %collective-permute-start.5 = (f32[2,2,3,2,64,128]{5,4,3,2,1,0:T(8,128)S(1)}, f32[2,2,3,2,64,128]{5,4,3,2,1,0:T(8,128)S(1)}, u32[]{:S(2)}, u32[]{:S(2)}) collective-permute-start(f32[2,2,3,2,64,128]{5,4,3,2,1,0:T(8,128)S(1)} %add.29), channel_id=1, source_target_pairs={{0,1},{1,0},{2,3},{3,2},{4,5},{5,4},{6,7},{7,6},{8,9},{9,8},{10,11... | collective-permute-start | bytes 2359304 | tf_op jit(solution)/shard_map/ppermute | solution.py:228
  25.8 17.1 %collective-permute-start = (f32[2,2,3,2,64,128]{5,4,3,2,1,0:T(8,128)S(1)}, f32[2,2,3,2,64,128]{5,4,3,2,1,0:T(8,128)S(1)}, u32[]{:S(2)}, u32[]{:S(2)}) collective-permute-start(f32[2,2,3,2,64,128]{5,4,3,2,1,0:T(8,128)S(1)} %get-tuple-element.15), channel_id=1, source_target_pairs={{0,1},{1,0},{2,3},{3,2},{4,5},{5,4},{6,7},{7,6},{8,9},{9,8},{10,11... | collective-permute-start | bytes 2359304 | tf_op jit(solution)/shard_map/ppermute | solution.py:227
  28.2 14.7 %collective-permute-start.2 = (f32[2,2,3,2,64,128]{5,4,3,2,1,0:T(8,128)S(1)}, f32[2,2,3,2,64,128]{5,4,3,2,1,0:T(8,128)S(1)}, u32[]{:S(2)}, u32[]{:S(2)}) collective-permute-start(f32[2,2,3,2,64,128]{5,4,3,2,1,0:T(8,128)S(1)} %add.26), channel_id=1, source_target_pairs={{0,16},{1,17},{2,18},{3,19},{4,20},{5,21},{6,22},{7,23},{8,24},{9,... | collective-permute-start | bytes 2359304 | tf_op jit(solution)/shard_map/ppermute | solution.py:227
  34.4 77.3 %copy-start.1 = (f32[128,128]{1,0:T(8,128)S(1)}, f32[128,128]{1,0:T(8,128)}, u32[]{:S(2)}) copy-start(f32[128,128]{1,0:T(8,128)} %constant.13.clone.wide_ref) | copy-start | bytes 196612
  34.4 77.3 %copy-start.3 = (f32[64,64]{1,0:T(8,128)S(1)}, f32[64,64]{1,0:T(8,128)}, u32[]{:S(2)}) copy-start(f32[64,64]{1,0:T(8,128)} %constant.12.clone.left_ref) | copy-start | bytes 49156
  34.4 77.3 %copy-start.4 = (f32[1,1,64,128]{3,2,1,0:T(8,128)S(1)}, f32[1,1,64,128]{3,2,1,0:T(8,128)}, u32[]{:S(2)}) copy-start(f32[1,1,64,128]{3,2,1,0:T(8,128)} %mom_ref.1) | copy-start | bytes 98308
  34.4 77.3 %copy-start.5 = (s32[1,2,32]{2,1,0:T(2,128)S(1)}, s32[1,2,32]{2,1,0:T(2,128)}, u32[]{:S(2)}) copy-start(s32[1,2,32]{2,1,0:T(2,128)} %idx_ref.1) | copy-start | bytes 772
  34.6 16.3 %collective-permute-start.6 = (f32[2,2,3,2,64,128]{5,4,3,2,1,0:T(8,128)S(1)}, f32[2,2,3,2,64,128]{5,4,3,2,1,0:T(8,128)S(1)}, u32[]{:S(2)}, u32[]{:S(2)}) collective-permute-start(f32[2,2,3,2,64,128]{5,4,3,2,1,0:T(8,128)S(1)} %add_add_fusion), channel_id=1, source_target_pairs={{0,8},{1,9},{2,10},{3,11},{4,12},{5,13},{6,14},{7,15},{8,0},{9,1},... | collective-permute-start | bytes 2359304 | tf_op jit(solution)/shard_map/ppermute | solution.py:229

commit v6 on v5

--- a/solution.py
+++ b/solution.py
@@ -31,17 +31,14 @@
     return (((at + size - core) ^ 1) + core) % size
 
 
-def pairs(across_z, across_y, across_x=False):
+def pairs(across_x, across_z, across_y, stride=1):
+    def target(at, core, size, crossed):
+        return stride * partner(at // stride, core, size // stride) + at % stride if crossed else at
+
     return [
         (
             flat(x_lo, core, z, x_hi, y),
-            flat(
-                x_lo,
-                core,
-                partner(z, core, Z) if across_z else z,
-                1 - x_hi if across_x else x_hi,
-                partner(y, core, Y) if across_y else y,
-            ),
+            flat(x_lo, core, target(z, core, Z, across_z), x_hi ^ across_x, target(y, core, Y, across_y)),
         )
         for x_lo in range(2)
         for core in range(2)
@@ -53,18 +50,12 @@
 
 def stage_groups():
     return [
-        [
-            flat(x_lo, core, 4 * a + 2 * z1 + z0, x_hi, 4 * b + 2 * y1 + y0)
-            for z1 in range(2)
-            for y1 in range(2)
-            for a in range(Z // 4)
-            for b in range(Y // 4)
-        ]
+        [flat(x_lo, core, 4 * a + z, x_hi, 4 * b + y) for a in range(Z // 4) for b in range(Y // 4)]
         for x_lo in range(2)
         for core in range(2)
         for x_hi in range(2)
-        for z0 in range(2)
-        for y0 in range(2)
+        for z in range(4)
+        for y in range(4)
     ]
 
 
@@ -75,8 +66,10 @@
     return (scale * np.cos(np.pi * (2.0 * x + 1.0) * u / (2.0 * SIDE))).astype(np.float32)
 
 
-def parities(place_ref):
-    return (place_ref[0] >> 4) & 1, place_ref[0] & 1, (place_ref[0] >> 3) & 1
+def coordinates(place_ref):
+    place = place_ref[0]
+    core = lax.div(place, 192) & 1
+    return core, lax.div(lax.rem(place, 192), 16), (place >> 3) & 1, place & 7
 
 
 def left_kernel_part(act_ref, left_ref):
@@ -102,22 +95,33 @@
     both = jnp.dot(left_ref[...], rhs, preferred_element_type=jnp.float32)
     low = lax.broadcasted_iota(jnp.int32, (SIDE, WIDE), 1) < SIDE
 
-    def write(even_ref, odd_ref):
+    core, _, _, y = coordinates(place_ref)
+    other_bit = 1 ^ ((partner(y, core, Y) >> 1) & 1)
+    own_bit = 1 ^ ((y >> 1) & 1)
+
+    def write(even_ref, odd_ref, even_bit, odd_bit):
         for a in range(rows // SIDE):
             for pair in range(CHUNK // WIDE):
                 cols = slice(pair * WIDE, (pair + 1) * WIDE)
                 one = both[a * SIDE : (a + 1) * SIDE, cols]
                 two = both[rows + a * SIDE : rows + (a + 1) * SIDE, cols]
-                even_ref[0, pair % 2, a, pair // 2] = jnp.where(low, one, pltpu.roll(two, SIDE, 1))
-                odd_ref[0, pair % 2, a, pair // 2] = jnp.where(low, pltpu.roll(one, SIDE, 1), two)
-
-    _, y_own, _ = parities(place_ref)
-    pl.when(y_own == 0)(lambda: write(own_ref, other_ref))
-    pl.when(y_own == 1)(lambda: write(other_ref, own_ref))
+                even = jnp.where(low, one, pltpu.roll(two, SIDE, 1))
+                odd = jnp.where(low, pltpu.roll(one, SIDE, 1), two)
+                even_ref[0, even_bit ^ (pair % 2), a, pair // 2] = even
+                odd_ref[0, odd_bit ^ (pair % 2), a, pair // 2] = odd
+
+    pl.when(y & 1 == 0)(lambda: write(own_ref, other_ref, own_bit, other_bit))
+    pl.when(y & 1 == 1)(lambda: write(other_ref, own_ref, other_bit, own_bit))
 
 
 def gradient_terms(place, acts_or_left, grads, colour, far):
     first = acts_or_left.ndim == 3
+
+    def column_block(k, place):
+        core, z, x, _ = coordinates(place)
+        holder = partner(z, core, Z) if far else z
+        return (0, 0, 0, (k ^ 1 ^ ((holder >> 1) & 1)) * 4 + (holder & 1) * 2 + (x ^ colour))
+
     tokens = grads.shape[1]
     rows = acts_or_left.shape[1] if first else acts_or_left.shape[0] // LAYERS
     blocks = (2, 2, rows // SIDE, 2, SIDE, WIDE)
@@ -134,12 +138,7 @@
                 pl.BlockSpec(acts_or_left.shape, lambda k, place: (0, 0, 0)) if first else left_spec,
                 pl.BlockSpec(
                     (1, tokens, LAYERS, CHUNK),
-                    lambda k, place: (
-                        0,
-                        0,
-                        0,
-                        k * 4 + (parities(place)[0] ^ far) * 2 + (parities(place)[2] ^ colour),
-                    ),
+                    column_block,
                 ),
             ],
             out_specs=[out_spec, out_spec] + [left_spec] * first,
@@ -217,17 +216,22 @@
     place = lax.axis_index(axes)[None]
     acts = acts[0].transpose(1, 2, 0)
     hop = functools.partial(lax.ppermute, axis_name=axes)
-    across_z, across_y, across_x = pairs(True, False), pairs(False, True), pairs(False, False, True)
-    far0_other, far0_own, left = gradient_terms(place, acts, grads, 0, 1)
-    far1_other, far1_own = gradient_terms(place, left, grads, 1, 1)
+    across_z, across_y = pairs(0, 1, 0), pairs(0, 0, 1)
+    far1_other, far1_own, left = gradient_terms(place, acts, grads, 1, 1)
+    far0_other, far0_own = gradient_terms(place, left, grads, 0, 1)
     near0_other, near0_own = gradient_terms(place, left, grads, 0, 0)
     near1_other, near1_own = gradient_terms(place, left, grads, 1, 0)
+    near0_other, near1_other = lax.optimization_barrier((near0_other, near1_other))
     far0 = far0_own + hop(far0_other, perm=across_y)
     other1 = near1_other + hop(far1_other, perm=across_z)
     sum0 = near0_own + hop(near0_other, perm=across_y) + hop(far0, perm=across_z)
     sum1 = near1_own + hop(far1_own, perm=across_z) + hop(other1, perm=across_y)
-    terms = (sum0 + hop(sum1, perm=across_x)).reshape(24, SIDE, WIDE)
-    terms = exchange(terms, axis_index_groups=stage_groups())
+    terms = sum0[1, 1]
+    for other_x, piece in ((1, sum1), (0, sum0)):
+        for z_like, y_like in ((0, 0), (0, 1), (1, 0), (1, 1)):
+            if other_x or not (z_like and y_like):
+                terms += hop(piece[z_like, y_like], perm=pairs(other_x, 1 - z_like, 1 - y_like, 2))
+    terms = exchange(terms.reshape(6, SIDE, WIDE), axis_index_groups=stage_groups())
     new_momentum, sent = encode(terms, momentum, band_idx)
     every = lax.all_to_all(sent, "replica", split_axis=0, concat_axis=0, tiled=True)
     update = decode(every)

time: 122 us -> 117 us (0.959)
  the two profiles are of different devices: /device:TPU:16 before, /device:TPU:1 now
where the time goes in v6:
time: 117 us
  starting transfers between devices  66.2 us (57%)
  blocking collectives  28.5 us (24%)
  Pallas kernels  10.5 us (9%)
  waiting for transfers between devices  8.71 us (7%)
  local copies, waits for them, and re-layouts  1.2 us (1%)
    ppermute x7, starting transfers between devices, local(): hop(piece[z_like, y_like], perm=pairs(other_x, 1 - z_like, 1 - y_like, 2))  32.8 us
    all_to_all x1, blocking collectives, local(): exchange(terms.reshape(6, SIDE, WIDE), axis_index_groups=stage_groups())  21.9 us
    ppermute x1, starting transfers between devices, local(): other1 = near1_other + hop(far1_other, perm=across_z)  15.1 us
    pallas_call x4, Pallas kernels, gradient_terms(): pl.pallas_call(functools.partial(terms_kernel, first), grid_spec=pltpu.Pr...  7.86 us
    all_to_all x1, blocking collectives, local(): lax.all_to_all(sent, 'replica', split_axis=0, concat_axis=0, tiled=True)  6.66 us
    ppermute x7, waiting for transfers between devices, local(): hop(piece[z_like, y_like], perm=pairs(other_x, 1 - z_like, 1 - y_like, 2))  5.98 us
    ppermute x1, starting transfers between devices, local(): far0 = far0_own + hop(far0_other, perm=across_y)  5.25 us
    ppermute x1, starting transfers between devices, local(): hop(far0, perm=across_z)  4.57 us
  transfers between devices with their start and end apart: 13, of which 4 were waited for; matrix products, arithmetic and copies ran while one was open for 1% of the time, Pallas kernels for 4%

profile of v6, /device:TPU:1, one launch (start us, length us, event | category | flops | bytes accessed | tf_op | source)
XLA Modules:
  0.0 116.7 jit_solution(9907360249536281205)
XLA Ops:
  0.7 1.1 copy-done.2
  1.7 2.9 %terms11.1 = (f32[2,2,3,2,64,128]{5,4,3,2,1,0:T(8,128)S(1)}, f32[2,2,3,2,64,128]{5,4,3,2,1,0:T(8,128)S(1)}, bf16[384,512]{1,0:T(8,128)(2,1)S(1)}) custom-call(s32[1]{0:T(128)} %bitcast.place_ref, bf16[2,192,256]{2,1,0:T(8,128)(2,1)S(1)} %bitcast.35, bf16[1,256,2,4096]{3,2,1,0:T(2,128)(2,1)} %grad_ref.7), custom_call_target="tpu_custom_call" | custom-call | tf_op jit(solution)/shard_map/terms11/pallas_call | solution.py:132
  4.6 15.1 %collective-permute-start.4 = (f32[2,2,3,2,64,128]{5,4,3,2,1,0:T(8,128)S(1)}, f32[2,2,3,2,64,128]{5,4,3,2,1,0:T(8,128)S(1)}, u32[]{:S(2)}, u32[]{:S(2)}) collective-permute-start(f32[2,2,3,2,64,128]{5,4,3,2,1,0:T(8,128)S(1)} %get-tuple-element.25), channel_id=1, source_target_pairs={{0,16},{1,17},{2,18},{3,19},{4,20},{5,21},{6,22},{7,23},{8,24},{9,... | collective-permute-start | bytes 2359304 | tf_op jit(solution)/shard_map/ppermute | solution.py:226
  19.8 1.7 %terms01.1 = (f32[2,2,3,2,64,128]{5,4,3,2,1,0:T(8,128)S(1)}, f32[2,2,3,2,64,128]{5,4,3,2,1,0:T(8,128)S(1)}) custom-call(s32[1]{0:T(128)} %bitcast.place_ref, bf16[384,512]{1,0:T(8,128)(2,1)S(1)} %get-tuple-element.15.in_ref, bf16[1,256,2,4096]{3,2,1,0:T(2,128)(2,1)S(1)} %copy-done), custom_call_target="tpu_custom_call" | custom-call | tf_op jit(solution)/shard_map/terms01/pallas_call | solution.py:132
  21.5 5.3 %collective-permute-start.1 = (f32[2,2,3,2,64,128]{5,4,3,2,1,0:T(8,128)S(1)}, f32[2,2,3,2,64,128]{5,4,3,2,1,0:T(8,128)S(1)}, u32[]{:S(2)}, u32[]{:S(2)}) collective-permute-start(f32[2,2,3,2,64,128]{5,4,3,2,1,0:T(8,128)S(1)} %get-tuple-element.21), channel_id=1, source_target_pairs={{0,1},{1,0},{2,3},{3,2},{4,5},{5,4},{6,7},{7,6},{8,9},{9,8},{10,11... | collective-permute-start | bytes 2359304 | tf_op jit(solution)/shard_map/ppermute | solution.py:225
  26.8 1.9 %collective-permute-start.3 = (f32[2,2,3,2,64,128]{5,4,3,2,1,0:T(8,128)S(1)}, f32[2,2,3,2,64,128]{5,4,3,2,1,0:T(8,128)S(1)}, u32[]{:S(2)}, u32[]{:S(2)}) collective-permute-start(f32[2,2,3,2,64,128]{5,4,3,2,1,0:T(8,128)S(1)} %get-tuple-element.23), channel_id=1, source_target_pairs={{0,16},{1,17},{2,18},{3,19},{4,20},{5,21},{6,22},{7,23},{8,24},{9,... | collective-permute-start | bytes 2359304 | tf_op jit(solution)/shard_map/ppermute | solution.py:228
  28.7 1.6 %terms10.1 = (f32[2,2,3,2,64,128]{5,4,3,2,1,0:T(8,128)S(1)}, f32[2,2,3,2,64,128]{5,4,3,2,1,0:T(8,128)S(1)}) custom-call(s32[1]{0:T(128)} %bitcast.place_ref, bf16[384,512]{1,0:T(8,128)(2,1)S(1)} %get-tuple-element.15.in_ref, bf16[1,256,2,4096]{3,2,1,0:T(2,128)(2,1)S(1)} %copy-done), custom_call_target="tpu_custom_call" | custom-call | tf_op jit(solution)/shard_map/terms10/pallas_call | solution.py:132
  30.3 1.6 %terms00.1 = (f32[2,2,3,2,64,128]{5,4,3,2,1,0:T(8,128)S(1)}, f32[2,2,3,2,64,128]{5,4,3,2,1,0:T(8,128)S(1)}) custom-call(s32[1]{0:T(128)} %bitcast.place_ref, bf16[384,512]{1,0:T(8,128)(2,1)S(1)} %get-tuple-element.15.in_ref, bf16[1,256,2,4096]{3,2,1,0:T(2,128)(2,1)S(1)} %copy-done), custom_call_target="tpu_custom_call" | custom-call | tf_op jit(solution)/shard_map/terms00/pallas_call | solution.py:132
  32.1 2.3 %collective-permute-start.5 = (f32[2,2,3,2,64,128]{5,4,3,2,1,0:T(8,128)S(1)}, f32[2,2,3,2,64,128]{5,4,3,2,1,0:T(8,128)S(1)}, u32[]{:S(2)}, u32[]{:S(2)}) collective-permute-start(f32[2,2,3,2,64,128]{5,4,3,2,1,0:T(8,128)S(1)} %add.47), channel_id=1, source_target_pairs={{0,1},{1,0},{2,3},{3,2},{4,5},{5,4},{6,7},{7,6},{8,9},{9,8},{10,11... | collective-permute-start | bytes 2359304 | tf_op jit(solution)/shard_map/ppermute | solution.py:228
  34.4 4.2 %collective-permute-start = (f32[2,2,3,2,64,128]{5,4,3,2,1,0:T(8,128)S(1)}, f32[2,2,3,2,64,128]{5,4,3,2,1,0:T(8,128)S(1)}, u32[]{:S(2)}, u32[]{:S(2)}) collective-permute-start(f32[2,2,3,2,64,128]{5,4,3,2,1,0:T(8,128)S(1)} %get-tuple-element.19), channel_id=1, source_target_pairs={{0,1},{1,0},{2,3},{3,2},{4,5},{5,4},{6,7},{7,6},{8,9},{9,8},{10,11... | collective-permute-start | bytes 2359304 | tf_op jit(solution)/shard_map/ppermute | solution.py:227
  38.7 4.6 %collective-permute-start.2 = (f32[2,2,3,2,64,128]{5,4,3,2,1,0:T(8,128)S(1)}, f32[2,2,3,2,64,128]{5,4,3,2,1,0:T(8,128)S(1)}, u32[]{:S(2)}, u32[]{:S(2)}) collective-permute-start(f32[2,2,3,2,64,128]{5,4,3,2,1,0:T(8,128)S(1)} %add.44), channel_id=1, source_target_pairs={{0,16},{1,17},{2,18},{3,19},{4,20},{5,21},{6,22},{7,23},{8,24},{9,... | collective-permute-start | bytes 2359304 | tf_op jit(solution)/shard_map/ppermute | solution.py:227
  43.3 2.7 %collective-permute-done.5 = f32[2,2,3,2,64,128]{5,4,3,2,1,0:T(8,128)S(1)} collective-permute-done((f32[2,2,3,2,64,128]{5,4,3,2,1,0:T(8,128)S(1)}, f32[2,2,3,2,64,128]{5,4,3,2,1,0:T(8,128)S(1)}, u32[]{:S(2)}, u32[]{:S(2)}) %collective-permute-start.5) | collective-permute-done | bytes 786464 | tf_op jit(solution)/shard_map/ppermute | solution.py:228
  46.4 6.5 %collective-permute-start.6 = (f32[3,2,64,128]{3,2,1,0:T(8,128)S(1)}, f32[3,2,64,128]{3,2,1,0:T(8,128)S(1)}, u32[]{:S(2)}, u32[]{:S(2)}) collective-permute-start(f32[3,2,64,128]{3,2,1,0:T(8,128)S(1)} %get-tuple-element.28), channel_id=1, source_target_pairs={{0,42},{1,43},{2,40},{3,41},{4,46},{5,47},{6,44},{7,45},{8,34},{9,... | collective-permute-start | bytes 589832 | tf_op jit(solution)/shard_map/ppermute | solution.py:233
  52.8 2.1 %collective-permute-start.9 = (f32[3,2,64,128]{3,2,1,0:T(8,128)S(1)}, f32[3,2,64,128]{3,2,1,0:T(8,128)S(1)}, u32[]{:S(2)}, u32[]{:S(2)}) collective-permute-start(f32[3,2,64,128]{3,2,1,0:T(8,128)S(1)} %get-tuple-element.29), channel_id=1, source_target_pairs={{0,8},{1,9},{2,10},{3,11},{4,12},{5,13},{6,14},{7,15},{8,0},{9,1},... | collective-permute-start | bytes 589832 | tf_op jit(solution)/shard_map/ppermute | solution.py:233
  55.0 7.0 %collective-permute-start.8 = (f32[3,2,64,128]{3,2,1,0:T(8,128)S(1)}, f32[3,2,64,128]{3,2,1,0:T(8,128)S(1)}, u32[]{:S(2)}, u32[]{:S(2)}) collective-permute-start(f32[3,2,64,128]{3,2,1,0:T(8,128)S(1)} %get-tuple-element.30), channel_id=1, source_target_pairs={{0,10},{1,11},{2,8},{3,9},{4,14},{5,15},{6,12},{7,13},{8,2},{9,3},... | collective-permute-start | bytes 589832 | tf_op jit(solution)/shard_map/ppermute | solution.py:233
  62.0 4.6 %collective-permute-start.7 = (f32[3,2,64,128]{3,2,1,0:T(8,128)S(1)}, f32[3,2,64,128]{3,2,1,0:T(8,128)S(1)}, u32[]{:S(2)}, u32[]{:S(2)}) collective-permute-start(f32[3,2,64,128]{3,2,1,0:T(8,128)S(1)} %get-tuple-element.31), channel_id=1, source_target_pairs={{0,40},{1,41},{2,42},{3,43},{4,44},{5,45},{6,46},{7,47},{8,32},{9,... | collective-permute-start | bytes 589832 | tf_op jit(solution)/shard_map/ppermute | solution.py:233
  66.8 6.8 %collective-permute-start.10 = (f32[3,2,64,128]{3,2,1,0:T(8,128)S(1)}, f32[3,2,64,128]{3,2,1,0:T(8,128)S(1)}, u32[]{:S(2)}, u32[]{:S(2)}) collective-permute-start(f32[3,2,64,128]{3,2,1,0:T(8,128)S(1)} %get-tuple-element.32), channel_id=1, source_target_pairs={{0,34},{1,35},{2,32},{3,33},{4,38},{5,39},{6,36},{7,37},{8,42},{9,... | collective-permute-start | bytes 589832 | tf_op jit(solution)/shard_map/ppermute | solution.py:233
  73.6 1.9 %collective-permute-start.12 = (f32[3,2,64,128]{3,2,1,0:T(8,128)S(1)}, f32[3,2,64,128]{3,2,1,0:T(8,128)S(1)}, u32[]{:S(2)}, u32[]{:S(2)}) collective-permute-start(f32[3,2,64,128]{3,2,1,0:T(8,128)S(1)} %get-tuple-element.33), channel_id=1, source_target_pairs={{0,2},{1,3},{2,0},{3,1},{4,6},{5,7},{6,4},{7,5},{8,10},{9,11},{10,... | collective-permute-start | bytes 589832 | tf_op jit(solution)/shard_map/ppermute | solution.py:233
  75.6 3.9 %collective-permute-start.11 = (f32[3,2,64,128]{3,2,1,0:T(8,128)S(1)}, f32[3,2,64,128]{3,2,1,0:T(8,128)S(1)}, u32[]{:S(2)}, u32[]{:S(2)}) collective-permute-start(f32[3,2,64,128]{3,2,1,0:T(8,128)S(1)} %get-tuple-element.34), channel_id=1, source_target_pairs={{0,32},{1,33},{2,34},{3,35},{4,36},{5,37},{6,38},{7,39},{8,40},{9,... | collective-permute-start | bytes 589832 | tf_op jit(solution)/shard_map/ppermute | solution.py:233
  80.4 2.6 %collective-permute-done.12 = f32[3,2,64,128]{3,2,1,0:T(8,128)S(1)} collective-permute-done((f32[3,2,64,128]{3,2,1,0:T(8,128)S(1)}, f32[3,2,64,128]{3,2,1,0:T(8,128)S(1)}, u32[]{:S(2)}, u32[]{:S(2)}) %collective-permute-start.12) | collective-permute-done | bytes 196640 | tf_op jit(solution)/shard_map/ppermute | solution.py:233
  83.0 2.5 %collective-permute-done.11 = f32[3,2,64,128]{3,2,1,0:T(8,128)S(1)} collective-permute-done((f32[3,2,64,128]{3,2,1,0:T(8,128)S(1)}, f32[3,2,64,128]{3,2,1,0:T(8,128)S(1)}, u32[]{:S(2)}, u32[]{:S(2)}) %collective-permute-start.11) | collective-permute-done | bytes 196640 | tf_op jit(solution)/shard_map/ppermute | solution.py:233
  85.6 21.9 %all_to_all.10.parts_ref = f32[6,64,128]{2,1,0:T(8,128)S(1)} all-to-all(f32[6,64,128]{2,1,0:T(8,128)S(1)} %bitcast.36), channel_id=1, replica_groups={{0,4,64,68,128,132},{1,5,65,69,129,133},{2,6,66,70,130,134},{3,7,67,71,..., dimensions={0} | all-to-all | bytes 393216 | tf_op jit(solution)/shard_map/all_to_all | solution.py:234
  107.4 1.6 %encode.1 = (f32[1,1,64,128]{3,2,1,0:T(8,128)}, f32[4,64,128]{2,1,0:T(8,128)S(1)}) custom-call(f32[6,64,128]{2,1,0:T(8,128)S(1)} %all_to_all.10.parts_ref, f32[1,1,64,128]{3,2,1,0:T(8,128)S(1)} %copy-done.4, s32[1,2,32]{2,1,0:T(2,128)S(1)} %copy-done.5, f32[64,64]{1,0:T(8,128)S(1)} %copy-done.3, f32[128,128]{1,0:T(8,128)S(1)} %copy-done.1), custom_call_target="tpu_custom_call" | custom-call | tf_op jit(solution)/shard_map/encode/pallas_call | solution.py:193
  109.0 6.7 %all_to_all.11.every_ref = f32[4,64,128]{2,1,0:T(8,128)S(1)} all-to-all(f32[4,64,128]{2,1,0:T(8,128)S(1)} %get-tuple-element.27), channel_id=1, replica_groups=mesh['replica'=4,'shard'=192] {'replica'}, dimensions={0} | all-to-all | bytes 262144 | tf_op jit(solution)/shard_map/all_to_all | solution.py:236
  (29 shorter events, 2.8 us)
Async XLA Ops:
  0.6 19.1 %copy-start = (bf16[1,256,2,4096]{3,2,1,0:T(2,128)(2,1)S(1)}, bf16[1,256,2,4096]{3,2,1,0:T(2,128)(2,1)}, u32[]{:S(2)}) copy-start(bf16[1,256,2,4096]{3,2,1,0:T(2,128)(2,1)} %grad_ref.7) | copy-start | bytes 12582916
  0.7 1.1 copy-start.2
  4.6 27.3 %collective-permute-start.4 = (f32[2,2,3,2,64,128]{5,4,3,2,1,0:T(8,128)S(1)}, f32[2,2,3,2,64,128]{5,4,3,2,1,0:T(8,128)S(1)}, u32[]{:S(2)}, u32[]{:S(2)}) collective-permute-start(f32[2,2,3,2,64,128]{5,4,3,2,1,0:T(8,128)S(1)} %get-tuple-element.25), channel_id=1, source_target_pairs={{0,16},{1,17},{2,18},{3,19},{4,20},{5,21},{6,22},{7,23},{8,24},{9,... | collective-permute-start | bytes 2359304 | tf_op jit(solution)/shard_map/ppermute | solution.py:226
  21.5 17.1 %collective-permute-start.1 = (f32[2,2,3,2,64,128]{5,4,3,2,1,0:T(8,128)S(1)}, f32[2,2,3,2,64,128]{5,4,3,2,1,0:T(8,128)S(1)}, u32[]{:S(2)}, u32[]{:S(2)}) collective-permute-start(f32[2,2,3,2,64,128]{5,4,3,2,1,0:T(8,128)S(1)} %get-tuple-element.21), channel_id=1, source_target_pairs={{0,1},{1,0},{2,3},{3,2},{4,5},{5,4},{6,7},{7,6},{8,9},{9,8},{10,11... | collective-permute-start | bytes 2359304 | tf_op jit(solution)/shard_map/ppermute | solution.py:225
  26.8 16.6 %collective-permute-start.3 = (f32[2,2,3,2,64,128]{5,4,3,2,1,0:T(8,128)S(1)}, f32[2,2,3,2,64,128]{5,4,3,2,1,0:T(8,128)S(1)}, u32[]{:S(2)}, u32[]{:S(2)}) collective-permute-start(f32[2,2,3,2,64,128]{5,4,3,2,1,0:T(8,128)S(1)} %get-tuple-element.23), channel_id=1, source_target_pairs={{0,16},{1,17},{2,18},{3,19},{4,20},{5,21},{6,22},{7,23},{8,24},{9,... | collective-permute-start | bytes 2359304 | tf_op jit(solution)/shard_map/ppermute | solution.py:228
  32.1 13.9 %collective-permute-start.5 = (f32[2,2,3,2,64,128]{5,4,3,2,1,0:T(8,128)S(1)}, f32[2,2,3,2,64,128]{5,4,3,2,1,0:T(8,128)S(1)}, u32[]{:S(2)}, u32[]{:S(2)}) collective-permute-start(f32[2,2,3,2,64,128]{5,4,3,2,1,0:T(8,128)S(1)} %add.47), channel_id=1, source_target_pairs={{0,1},{1,0},{2,3},{3,2},{4,5},{5,4},{6,7},{7,6},{8,9},{9,8},{10,11... | collective-permute-start | bytes 2359304 | tf_op jit(solution)/shard_map/ppermute | solution.py:228
  34.4 27.5 %collective-permute-start = (f32[2,2,3,2,64,128]{5,4,3,2,1,0:T(8,128)S(1)}, f32[2,2,3,2,64,128]{5,4,3,2,1,0:T(8,128)S(1)}, u32[]{:S(2)}, u32[]{:S(2)}) collective-permute-start(f32[2,2,3,2,64,128]{5,4,3,2,1,0:T(8,128)S(1)} %get-tuple-element.19), channel_id=1, source_target_pairs={{0,1},{1,0},{2,3},{3,2},{4,5},{5,4},{6,7},{7,6},{8,9},{9,8},{10,11... | collective-permute-start | bytes 2359304 | tf_op jit(solution)/shard_map/ppermute | solution.py:227
  38.7 27.9 %collective-permute-start.2 = (f32[2,2,3,2,64,128]{5,4,3,2,1,0:T(8,128)S(1)}, f32[2,2,3,2,64,128]{5,4,3,2,1,0:T(8,128)S(1)}, u32[]{:S(2)}, u32[]{:S(2)}) collective-permute-start(f32[2,2,3,2,64,128]{5,4,3,2,1,0:T(8,128)S(1)} %add.44), channel_id=1, source_target_pairs={{0,16},{1,17},{2,18},{3,19},{4,20},{5,21},{6,22},{7,23},{8,24},{9,... | collective-permute-start | bytes 2359304 | tf_op jit(solution)/shard_map/ppermute | solution.py:227
  46.2 61.2 %copy-start.1 = (f32[128,128]{1,0:T(8,128)S(1)}, f32[128,128]{1,0:T(8,128)}, u32[]{:S(2)}) copy-start(f32[128,128]{1,0:T(8,128)} %constant.13.clone.wide_ref) | copy-start | bytes 196612
  46.3 61.2 %copy-start.3 = (f32[64,64]{1,0:T(8,128)S(1)}, f32[64,64]{1,0:T(8,128)}, u32[]{:S(2)}) copy-start(f32[64,64]{1,0:T(8,128)} %constant.12.clone.left_ref) | copy-start | bytes 49156
  46.3 61.2 %copy-start.4 = (f32[1,1,64,128]{3,2,1,0:T(8,128)S(1)}, f32[1,1,64,128]{3,2,1,0:T(8,128)}, u32[]{:S(2)}) copy-start(f32[1,1,64,128]{3,2,1,0:T(8,128)} %mom_ref.1) | copy-start | bytes 98308
  46.3 61.2 %copy-start.5 = (s32[1,2,32]{2,1,0:T(2,128)S(1)}, s32[1,2,32]{2,1,0:T(2,128)}, u32[]{:S(2)}) copy-start(s32[1,2,32]{2,1,0:T(2,128)} %idx_ref.1) | copy-start | bytes 772
  46.4 27.3 %collective-permute-start.6 = (f32[3,2,64,128]{3,2,1,0:T(8,128)S(1)}, f32[3,2,64,128]{3,2,1,0:T(8,128)S(1)}, u32[]{:S(2)}, u32[]{:S(2)}) collective-permute-start(f32[3,2,64,128]{3,2,1,0:T(8,128)S(1)} %get-tuple-element.28), channel_id=1, source_target_pairs={{0,42},{1,43},{2,40},{3,41},{4,46},{5,47},{6,44},{7,45},{8,34},{9,... | collective-permute-start | bytes 589832 | tf_op jit(solution)/shard_map/ppermute | solution.py:233
  52.8 22.8 %collective-permute-start.9 = (f32[3,2,64,128]{3,2,1,0:T(8,128)S(1)}, f32[3,2,64,128]{3,2,1,0:T(8,128)S(1)}, u32[]{:S(2)}, u32[]{:S(2)}) collective-permute-start(f32[3,2,64,128]{3,2,1,0:T(8,128)S(1)} %get-tuple-element.29), channel_id=1, source_target_pairs={{0,8},{1,9},{2,10},{3,11},{4,12},{5,13},{6,14},{7,15},{8,0},{9,1},... | collective-permute-start | bytes 589832 | tf_op jit(solution)/shard_map/ppermute | solution.py:233
  55.0 24.5 %collective-permute-start.8 = (f32[3,2,64,128]{3,2,1,0:T(8,128)S(1)}, f32[3,2,64,128]{3,2,1,0:T(8,128)S(1)}, u32[]{:S(2)}, u32[]{:S(2)}) collective-permute-start(f32[3,2,64,128]{3,2,1,0:T(8,128)S(1)} %get-tuple-element.30), channel_id=1, source_target_pairs={{0,10},{1,11},{2,8},{3,9},{4,14},{5,15},{6,12},{7,13},{8,2},{9,3},... | collective-permute-start | bytes 589832 | tf_op jit(solution)/shard_map/ppermute | solution.py:233
  62.0 17.5 %collective-permute-start.7 = (f32[3,2,64,128]{3,2,1,0:T(8,128)S(1)}, f32[3,2,64,128]{3,2,1,0:T(8,128)S(1)}, u32[]{:S(2)}, u32[]{:S(2)}) collective-permute-start(f32[3,2,64,128]{3,2,1,0:T(8,128)S(1)} %get-tuple-element.31), channel_id=1, source_target_pairs={{0,40},{1,41},{2,42},{3,43},{4,44},{5,45},{6,46},{7,47},{8,32},{9,... | collective-permute-start | bytes 589832 | tf_op jit(solution)/shard_map/ppermute | solution.py:233
  66.8 13.5 %collective-permute-start.10 = (f32[3,2,64,128]{3,2,1,0:T(8,128)S(1)}, f32[3,2,64,128]{3,2,1,0:T(8,128)S(1)}, u32[]{:S(2)}, u32[]{:S(2)}) collective-permute-start(f32[3,2,64,128]{3,2,1,0:T(8,128)S(1)} %get-tuple-element.32), channel_id=1, source_target_pairs={{0,34},{1,35},{2,32},{3,33},{4,38},{5,39},{6,36},{7,37},{8,42},{9,... | collective-permute-start | bytes 589832 | tf_op jit(solution)/shard_map/ppermute | solution.py:233
  73.6 9.3 %collective-permute-start.12 = (f32[3,2,64,128]{3,2,1,0:T(8,128)S(1)}, f32[3,2,64,128]{3,2,1,0:T(8,128)S(1)}, u32[]{:S(2)}, u32[]{:S(2)}) collective-permute-start(f32[3,2,64,128]{3,2,1,0:T(8,128)S(1)} %get-tuple-element.33), channel_id=1, source_target_pairs={{0,2},{1,3},{2,0},{3,1},{4,6},{5,7},{6,4},{7,5},{8,10},{9,11},{10,... | collective-permute-start | bytes 589832 | tf_op jit(solution)/shard_map/ppermute | solution.py:233
  75.6 9.9 %collective-permute-start.11 = (f32[3,2,64,128]{3,2,1,0:T(8,128)S(1)}, f32[3,2,64,128]{3,2,1,0:T(8,128)S(1)}, u32[]{:S(2)}, u32[]{:S(2)}) collective-permute-start(f32[3,2,64,128]{3,2,1,0:T(8,128)S(1)} %get-tuple-element.34), channel_id=1, source_target_pairs={{0,32},{1,33},{2,34},{3,35},{4,36},{5,37},{6,38},{7,39},{8,40},{9,... | collective-permute-start | bytes 589832 | tf_op jit(solution)/shard_map/ppermute | solution.py:233

commit v7 on v4

--- a/solution.py
+++ b/solution.py
@@ -224,10 +224,11 @@
     acts = acts[0].transpose(1, 2, 0)
     hop = functools.partial(lax.ppermute, axis_name=axes)
     across_z, across_y = pairs(True, False), pairs(False, True)
-    far0_other, far0_own, left = gradient_terms(place, acts, grads, 0, 1)
-    far1_other, far1_own = gradient_terms(place, left, grads, 1, 1)
+    far1_other, far1_own, left = gradient_terms(place, acts, grads, 1, 1)
+    far0_other, far0_own = gradient_terms(place, left, grads, 0, 1)
     near0_other, near0_own = gradient_terms(place, left, grads, 0, 0)
     near1_other, near1_own = gradient_terms(place, left, grads, 1, 0)
+    near0_other, near1_other = lax.optimization_barrier((near0_other, near1_other))
     far0 = far0_own + hop(far0_other, perm=across_y)
     other1 = near1_other + hop(far1_other, perm=across_z)
     sum0 = near0_own + hop(near0_other, perm=across_y) + hop(far0, perm=across_z)

time: 121 us -> 119 us (0.983)
  blocking collectives: 63.5 us -> 61.5 us
    ppermute x2, starting transfers between devices: 7.16 us -> 4.53 us  [local(): sum1 = near1_own + hop(far1_own, perm=across_z) + hop(other1, perm=across_y)]
    ppermute x1, starting transfers between devices: 1.99 us -> 3.89 us  [local(): hop(near0_other, perm=across_y)]
    ppermute x2, waiting for transfers between devices: 1.07 us -> 2.72 us  [local(): sum1 = near1_own + hop(far1_own, perm=across_z) + hop(other1, perm=across_y)]
    all_to_all x1, blocking collectives: 34.6 us -> 33.2 us  [local(): terms = exchange(terms, axis_index_groups=second)]
  transfers between devices with their start and end apart: 6 -> 6, of which waited for: 3 -> 2; matrix products, arithmetic and copies ran while one was open for 0% -> 0% of each run, Pallas kernels for 3% -> 4%
where the time goes in v7:
time: 119 us; the launch traced here: 118 us
  blocking collectives  61.5 us (52%)
  starting transfers between devices  33.4 us (28%)
  waiting for transfers between devices  10.9 us (9%)
  Pallas kernels  10 us (8%)
    all_to_all x1, blocking collectives, local(): terms = exchange(terms, axis_index_groups=second)  33.2 us
    all_to_all x1, blocking collectives, local(): terms = exchange(terms, axis_index_groups=third)  21.7 us
    ppermute x1, starting transfers between devices, local(): other1 = near1_other + hop(far1_other, perm=across_z)  15.1 us
    ppermute x1, waiting for transfers between devices, local(): hop(near0_other, perm=across_y)  8.22 us
    pallas_call x4, Pallas kernels, gradient_terms(): pl.pallas_call(functools.partial(terms_kernel, first), grid_spec=pltpu.Pr...  7.44 us
    all_to_all x1, blocking collectives, local(): lax.all_to_all(sent, 'replica', split_axis=0, concat_axis=0, tiled=True)  6.52 us
    ppermute x1, starting transfers between devices, local(): far0 = far0_own + hop(far0_other, perm=across_y)  5.24 us
    ppermute x1, starting transfers between devices, local(): hop(far0, perm=across_z)  4.57 us
  transfers between devices with their start and end apart: 6, of which 2 were waited for; matrix products, arithmetic and copies ran while one was open for 0% of the time, Pallas kernels for 4%

profile of v7, /device:TPU:1, one launch (start us, length us, event | category | flops | bytes accessed | tf_op | source)
XLA Modules:
  0.0 118.4 jit_solution(5822757254807851855)
XLA Ops:
  0.7 0.9 copy-done.2
  1.6 2.7 %terms11.1 = (f32[2,2,3,2,64,128]{5,4,3,2,1,0:T(8,128)S(1)}, f32[2,2,3,2,64,128]{5,4,3,2,1,0:T(8,128)S(1)}, bf16[384,512]{1,0:T(8,128)(2,1)S(1)}) custom-call(s32[1]{0:T(128)} %bitcast.place_ref, bf16[2,192,256]{2,1,0:T(8,128)(2,1)S(1)} %bitcast.5, bf16[1,256,2,4096]{3,2,1,0:T(2,128)(2,1)} %grad_ref.7), custom_call_target="tpu_custom_call" | custom-call | tf_op jit(solution)/shard_map/terms11/pallas_call | solution.py:138
  4.3 15.1 %collective-permute-start.4 = (f32[2,2,3,2,64,128]{5,4,3,2,1,0:T(8,128)S(1)}, f32[2,2,3,2,64,128]{5,4,3,2,1,0:T(8,128)S(1)}, u32[]{:S(2)}, u32[]{:S(2)}) collective-permute-start(f32[2,2,3,2,64,128]{5,4,3,2,1,0:T(8,128)S(1)} %get-tuple-element.25), channel_id=1, source_target_pairs={{0,16},{1,17},{2,18},{3,19},{4,20},{5,21},{6,22},{7,23},{8,24},{9,... | collective-permute-start | bytes 2359304 | tf_op jit(solution)/shard_map/ppermute | solution.py:233
  19.5 1.6 %terms01.1 = (f32[2,2,3,2,64,128]{5,4,3,2,1,0:T(8,128)S(1)}, f32[2,2,3,2,64,128]{5,4,3,2,1,0:T(8,128)S(1)}) custom-call(s32[1]{0:T(128)} %bitcast.place_ref, bf16[384,512]{1,0:T(8,128)(2,1)S(1)} %get-tuple-element.15.in_ref, bf16[1,256,2,4096]{3,2,1,0:T(2,128)(2,1)S(1)} %copy-done), custom_call_target="tpu_custom_call" | custom-call | tf_op jit(solution)/shard_map/terms01/pallas_call | solution.py:138
  21.0 5.2 %collective-permute-start.1 = (f32[2,2,3,2,64,128]{5,4,3,2,1,0:T(8,128)S(1)}, f32[2,2,3,2,64,128]{5,4,3,2,1,0:T(8,128)S(1)}, u32[]{:S(2)}, u32[]{:S(2)}) collective-permute-start(f32[2,2,3,2,64,128]{5,4,3,2,1,0:T(8,128)S(1)} %get-tuple-element.21), channel_id=1, source_target_pairs={{0,1},{1,0},{2,3},{3,2},{4,5},{5,4},{6,7},{7,6},{8,9},{9,8},{10,11... | collective-permute-start | bytes 2359304 | tf_op jit(solution)/shard_map/ppermute | solution.py:232
  26.3 1.9 %collective-permute-start.3 = (f32[2,2,3,2,64,128]{5,4,3,2,1,0:T(8,128)S(1)}, f32[2,2,3,2,64,128]{5,4,3,2,1,0:T(8,128)S(1)}, u32[]{:S(2)}, u32[]{:S(2)}) collective-permute-start(f32[2,2,3,2,64,128]{5,4,3,2,1,0:T(8,128)S(1)} %get-tuple-element.23), channel_id=1, source_target_pairs={{0,16},{1,17},{2,18},{3,19},{4,20},{5,21},{6,22},{7,23},{8,24},{9,... | collective-permute-start | bytes 2359304 | tf_op jit(solution)/shard_map/ppermute | solution.py:235
  28.2 1.6 %terms00.1 = (f32[2,2,3,2,64,128]{5,4,3,2,1,0:T(8,128)S(1)}, f32[2,2,3,2,64,128]{5,4,3,2,1,0:T(8,128)S(1)}) custom-call(s32[1]{0:T(128)} %bitcast.place_ref, bf16[384,512]{1,0:T(8,128)(2,1)S(1)} %get-tuple-element.15.in_ref, bf16[1,256,2,4096]{3,2,1,0:T(2,128)(2,1)S(1)} %copy-done), custom_call_target="tpu_custom_call" | custom-call | tf_op jit(solution)/shard_map/terms00/pallas_call | solution.py:138
  29.8 1.6 %terms10.1 = (f32[2,2,3,2,64,128]{5,4,3,2,1,0:T(8,128)S(1)}, f32[2,2,3,2,64,128]{5,4,3,2,1,0:T(8,128)S(1)}) custom-call(s32[1]{0:T(128)} %bitcast.place_ref, bf16[384,512]{1,0:T(8,128)(2,1)S(1)} %get-tuple-element.15.in_ref, bf16[1,256,2,4096]{3,2,1,0:T(2,128)(2,1)S(1)} %copy-done), custom_call_target="tpu_custom_call" | custom-call | tf_op jit(solution)/shard_map/terms10/pallas_call | solution.py:138
  31.4 0.1 add.26
  31.5 2.6 %collective-permute-start.5 = (f32[2,2,3,2,64,128]{5,4,3,2,1,0:T(8,128)S(1)}, f32[2,2,3,2,64,128]{5,4,3,2,1,0:T(8,128)S(1)}, u32[]{:S(2)}, u32[]{:S(2)}) collective-permute-start(f32[2,2,3,2,64,128]{5,4,3,2,1,0:T(8,128)S(1)} %add.26), channel_id=1, source_target_pairs={{0,1},{1,0},{2,3},{3,2},{4,5},{5,4},{6,7},{7,6},{8,9},{9,8},{10,11... | collective-permute-start | bytes 2359304 | tf_op jit(solution)/shard_map/ppermute | solution.py:235
  34.1 3.9 %collective-permute-start = (f32[2,2,3,2,64,128]{5,4,3,2,1,0:T(8,128)S(1)}, f32[2,2,3,2,64,128]{5,4,3,2,1,0:T(8,128)S(1)}, u32[]{:S(2)}, u32[]{:S(2)}) collective-permute-start(f32[2,2,3,2,64,128]{5,4,3,2,1,0:T(8,128)S(1)} %get-tuple-element.19), channel_id=1, source_target_pairs={{0,1},{1,0},{2,3},{3,2},{4,5},{5,4},{6,7},{7,6},{8,9},{9,8},{10,11... | collective-permute-start | bytes 2359304 | tf_op jit(solution)/shard_map/ppermute | solution.py:234
  38.0 0.1 add.23
  38.1 4.6 %collective-permute-start.2 = (f32[2,2,3,2,64,128]{5,4,3,2,1,0:T(8,128)S(1)}, f32[2,2,3,2,64,128]{5,4,3,2,1,0:T(8,128)S(1)}, u32[]{:S(2)}, u32[]{:S(2)}) collective-permute-start(f32[2,2,3,2,64,128]{5,4,3,2,1,0:T(8,128)S(1)} %add.23), channel_id=1, source_target_pairs={{0,16},{1,17},{2,18},{3,19},{4,20},{5,21},{6,22},{7,23},{8,24},{9,... | collective-permute-start | bytes 2359304 | tf_op jit(solution)/shard_map/ppermute | solution.py:234
  42.7 2.7 %collective-permute-done.5 = f32[2,2,3,2,64,128]{5,4,3,2,1,0:T(8,128)S(1)} collective-permute-done((f32[2,2,3,2,64,128]{5,4,3,2,1,0:T(8,128)S(1)}, f32[2,2,3,2,64,128]{5,4,3,2,1,0:T(8,128)S(1)}, u32[]{:S(2)}, u32[]{:S(2)}) %collective-permute-start.5) | collective-permute-done | bytes 786464 | tf_op jit(solution)/shard_map/ppermute | solution.py:235
  45.5 0.2 add_add_fusion
  45.7 8.2 %collective-permute-done = f32[2,2,3,2,64,128]{5,4,3,2,1,0:T(8,128)S(1)} collective-permute-done((f32[2,2,3,2,64,128]{5,4,3,2,1,0:T(8,128)S(1)}, f32[2,2,3,2,64,128]{5,4,3,2,1,0:T(8,128)S(1)}, u32[]{:S(2)}, u32[]{:S(2)}) %collective-permute-start) | collective-permute-done | bytes 786464 | tf_op jit(solution)/shard_map/ppermute | solution.py:234
  53.9 0.2 add_add_fusion.1
  54.1 0.1 pad_maximum_fusion
  54.2 33.2 %all_to_all.15 = f32[8,6,64,128]{3,2,1,0:T(8,128)S(1)} all-to-all(f32[8,6,64,128]{3,2,1,0:T(8,128)S(1)} %bitcast.6), channel_id=1, replica_groups={{0,2,32,34,8,10,40,42},{4,6,36,38,12,14,44,46},{64,66,96,98,72,74,104,1..., dimensions={0} | all-to-all | bytes 3145728 | tf_op jit(solution)/shard_map/all_to_all | solution.py:237
  87.4 0.1 reduce_sum.9
  87.5 21.7 %all_to_all.16.parts_ref = f32[6,64,128]{2,1,0:T(8,128)S(1)} all-to-all(f32[6,64,128]{2,1,0:T(8,128)S(1)} %reduce_sum.9), channel_id=1, replica_groups={{0,4,64,68,128,132},{1,5,65,69,129,133},{2,6,66,70,130,134},{3,7,67,71,..., dimensions={0} | all-to-all | bytes 393216 | tf_op jit(solution)/shard_map/all_to_all | solution.py:239
  109.3 1.6 %encode.1 = (f32[1,1,64,128]{3,2,1,0:T(8,128)}, f32[4,64,128]{2,1,0:T(8,128)S(1)}) custom-call(f32[6,64,128]{2,1,0:T(8,128)S(1)} %all_to_all.16.parts_ref, f32[1,1,64,128]{3,2,1,0:T(8,128)S(1)} %copy-done.4, s32[1,2,32]{2,1,0:T(2,128)S(1)} %copy-done.5, f32[64,64]{1,0:T(8,128)S(1)} %copy-done.3, f32[128,128]{1,0:T(8,128)S(1)} %copy-done.1), custom_call_target="tpu_custom_call" | custom-call | tf_op jit(solution)/shard_map/encode/pallas_call | solution.py:199
  110.9 6.5 %all_to_all.17.every_ref = f32[4,64,128]{2,1,0:T(8,128)S(1)} all-to-all(f32[4,64,128]{2,1,0:T(8,128)S(1)} %get-tuple-element.27), channel_id=1, replica_groups=mesh['replica'=4,'shard'=192] {'replica'}, dimensions={0} | all-to-all | bytes 262144 | tf_op jit(solution)/shard_map/all_to_all | solution.py:241
  117.4 1.0 decode.1
  (15 shorter events, 0.0 us)
Async XLA Ops:
  0.6 0.9 copy-start.2
  1.6 17.9 %copy-start = (bf16[1,256,2,4096]{3,2,1,0:T(2,128)(2,1)S(1)}, bf16[1,256,2,4096]{3,2,1,0:T(2,128)(2,1)}, u32[]{:S(2)}) copy-start(bf16[1,256,2,4096]{3,2,1,0:T(2,128)(2,1)} %grad_ref.7) | copy-start | bytes 12582916
  4.3 27.1 %collective-permute-start.4 = (f32[2,2,3,2,64,128]{5,4,3,2,1,0:T(8,128)S(1)}, f32[2,2,3,2,64,128]{5,4,3,2,1,0:T(8,128)S(1)}, u32[]{:S(2)}, u32[]{:S(2)}) collective-permute-start(f32[2,2,3,2,64,128]{5,4,3,2,1,0:T(8,128)S(1)} %get-tuple-element.25), channel_id=1, source_target_pairs={{0,16},{1,17},{2,18},{3,19},{4,20},{5,21},{6,22},{7,23},{8,24},{9,... | collective-permute-start | bytes 2359304 | tf_op jit(solution)/shard_map/ppermute | solution.py:233
  21.0 17.0 %collective-permute-start.1 = (f32[2,2,3,2,64,128]{5,4,3,2,1,0:T(8,128)S(1)}, f32[2,2,3,2,64,128]{5,4,3,2,1,0:T(8,128)S(1)}, u32[]{:S(2)}, u32[]{:S(2)}) collective-permute-start(f32[2,2,3,2,64,128]{5,4,3,2,1,0:T(8,128)S(1)} %get-tuple-element.21), channel_id=1, source_target_pairs={{0,1},{1,0},{2,3},{3,2},{4,5},{5,4},{6,7},{7,6},{8,9},{9,8},{10,11... | collective-permute-start | bytes 2359304 | tf_op jit(solution)/shard_map/ppermute | solution.py:232
  26.3 16.4 %collective-permute-start.3 = (f32[2,2,3,2,64,128]{5,4,3,2,1,0:T(8,128)S(1)}, f32[2,2,3,2,64,128]{5,4,3,2,1,0:T(8,128)S(1)}, u32[]{:S(2)}, u32[]{:S(2)}) collective-permute-start(f32[2,2,3,2,64,128]{5,4,3,2,1,0:T(8,128)S(1)} %get-tuple-element.23), channel_id=1, source_target_pairs={{0,16},{1,17},{2,18},{3,19},{4,20},{5,21},{6,22},{7,23},{8,24},{9,... | collective-permute-start | bytes 2359304 | tf_op jit(solution)/shard_map/ppermute | solution.py:235
  31.5 13.9 %collective-permute-start.5 = (f32[2,2,3,2,64,128]{5,4,3,2,1,0:T(8,128)S(1)}, f32[2,2,3,2,64,128]{5,4,3,2,1,0:T(8,128)S(1)}, u32[]{:S(2)}, u32[]{:S(2)}) collective-permute-start(f32[2,2,3,2,64,128]{5,4,3,2,1,0:T(8,128)S(1)} %add.26), channel_id=1, source_target_pairs={{0,1},{1,0},{2,3},{3,2},{4,5},{5,4},{6,7},{7,6},{8,9},{9,8},{10,11... | collective-permute-start | bytes 2359304 | tf_op jit(solution)/shard_map/ppermute | solution.py:235
  34.1 19.8 %collective-permute-start = (f32[2,2,3,2,64,128]{5,4,3,2,1,0:T(8,128)S(1)}, f32[2,2,3,2,64,128]{5,4,3,2,1,0:T(8,128)S(1)}, u32[]{:S(2)}, u32[]{:S(2)}) collective-permute-start(f32[2,2,3,2,64,128]{5,4,3,2,1,0:T(8,128)S(1)} %get-tuple-element.19), channel_id=1, source_target_pairs={{0,1},{1,0},{2,3},{3,2},{4,5},{5,4},{6,7},{7,6},{8,9},{9,8},{10,11... | collective-permute-start | bytes 2359304 | tf_op jit(solution)/shard_map/ppermute | solution.py:234
  38.1 15.7 %collective-permute-start.2 = (f32[2,2,3,2,64,128]{5,4,3,2,1,0:T(8,128)S(1)}, f32[2,2,3,2,64,128]{5,4,3,2,1,0:T(8,128)S(1)}, u32[]{:S(2)}, u32[]{:S(2)}) collective-permute-start(f32[2,2,3,2,64,128]{5,4,3,2,1,0:T(8,128)S(1)} %add.23), channel_id=1, source_target_pairs={{0,16},{1,17},{2,18},{3,19},{4,20},{5,21},{6,22},{7,23},{8,24},{9,... | collective-permute-start | bytes 2359304 | tf_op jit(solution)/shard_map/ppermute | solution.py:234
  87.4 21.9 %copy-start.1 = (f32[128,128]{1,0:T(8,128)S(1)}, f32[128,128]{1,0:T(8,128)}, u32[]{:S(2)}) copy-start(f32[128,128]{1,0:T(8,128)} %constant.15.clone.wide_ref) | copy-start | bytes 196612
  87.4 21.9 %copy-start.3 = (f32[64,64]{1,0:T(8,128)S(1)}, f32[64,64]{1,0:T(8,128)}, u32[]{:S(2)}) copy-start(f32[64,64]{1,0:T(8,128)} %constant.14.clone.left_ref) | copy-start | bytes 49156
  87.4 21.9 %copy-start.4 = (f32[1,1,64,128]{3,2,1,0:T(8,128)S(1)}, f32[1,1,64,128]{3,2,1,0:T(8,128)}, u32[]{:S(2)}) copy-start(f32[1,1,64,128]{3,2,1,0:T(8,128)} %mom_ref.1) | copy-start | bytes 98308
  87.4 21.9 %copy-start.5 = (s32[1,2,32]{2,1,0:T(2,128)S(1)}, s32[1,2,32]{2,1,0:T(2,128)}, u32[]{:S(2)}) copy-start(s32[1,2,32]{2,1,0:T(2,128)} %idx_ref.1) | copy-start | bytes 772

commit v8 on v6

--- a/solution.py
+++ b/solution.py
@@ -221,8 +221,8 @@
     far0_other, far0_own = gradient_terms(place, left, grads, 0, 1)
     near0_other, near0_own = gradient_terms(place, left, grads, 0, 0)
     near1_other, near1_own = gradient_terms(place, left, grads, 1, 0)
-    near0_other, near1_other = lax.optimization_barrier((near0_other, near1_other))
     far0 = far0_own + hop(far0_other, perm=across_y)
+    near0_other, far0 = lax.optimization_barrier((near0_other, far0))
     other1 = near1_other + hop(far1_other, perm=across_z)
     sum0 = near0_own + hop(near0_other, perm=across_y) + hop(far0, perm=across_z)
     sum1 = near1_own + hop(far1_own, perm=across_z) + hop(other1, perm=across_y)

time: 117 us -> 117 us (level)
  waiting for transfers between devices: 8.71 us -> 6.22 us
  starting transfers between devices: 66.2 us -> 67.7 us
    all_to_all x1, blocking collectives: 6.66 us -> 9.36 us  [local(): lax.all_to_all(sent, 'replica', split_axis=0, concat_axis=0, tiled=True)]
    ppermute x1, starting transfers between devices: 4.57 us -> 2.56 us  [local(): hop(far0, perm=across_z)]
    all_to_all x1, blocking collectives: 21.9 us -> 20.1 us  [local(): exchange(terms.reshape(6, SIDE, WIDE), axis_index_groups=stage_groups())]
    ppermute x2, starting transfers between devices: 4.26 us -> 5.9 us  [local(): sum1 = near1_own + hop(far1_own, perm=across_z) + hop(other1, perm=across_y)]
    ppermute x2, waiting for transfers between devices: 2.72 us -> 1.15 us  [local(): sum1 = near1_own + hop(far1_own, perm=across_z) + hop(other1, perm=across_y)]
    ppermute x7, starting transfers between devices: 32.8 us -> 34.3 us  [local(): hop(piece[z_like, y_like], perm=pairs(other_x, 1 - z_like, 1 - y_like, 2))]
where the time goes in v8:
time: 117 us
  starting transfers between devices  67.7 us (58%)
  blocking collectives  29.5 us (25%)
  Pallas kernels  10.5 us (9%)
  waiting for transfers between devices  6.22 us (5%)
  local copies, waits for them, and re-layouts  1.2 us (1%)
    ppermute x7, starting transfers between devices, local(): hop(piece[z_like, y_like], perm=pairs(other_x, 1 - z_like, 1 - y_like, 2))  34.3 us
    all_to_all x1, blocking collectives, local(): exchange(terms.reshape(6, SIDE, WIDE), axis_index_groups=stage_groups())  20.1 us
    ppermute x1, starting transfers between devices, local(): other1 = near1_other + hop(far1_other, perm=across_z)  15.1 us
    all_to_all x1, blocking collectives, local(): lax.all_to_all(sent, 'replica', split_axis=0, concat_axis=0, tiled=True)  9.36 us
    pallas_call x4, Pallas kernels, gradient_terms(): pl.pallas_call(functools.partial(terms_kernel, first), grid_spec=pltpu.Pr...  7.86 us
    ppermute x2, starting transfers between devices, local(): sum1 = near1_own + hop(far1_own, perm=across_z) + hop(other1, perm=across_y)  5.9 us
    ppermute x1, starting transfers between devices, local(): far0 = far0_own + hop(far0_other, perm=across_y)  5.25 us
    ppermute x7, waiting for transfers between devices, local(): hop(piece[z_like, y_like], perm=pairs(other_x, 1 - z_like, 1 - y_like, 2))  5.03 us
  transfers between devices with their start and end apart: 13, of which 4 were waited for; matrix products, arithmetic and copies ran while one was open for 1% of the time, Pallas kernels for 4%

profile of v8, /device:TPU:1, one launch (start us, length us, event | category | flops | bytes accessed | tf_op | source)
XLA Modules:
  0.0 116.7 jit_solution(6983349328336118773)
XLA Ops:
  0.7 1.1 copy-done.2
  1.7 2.9 %terms11.1 = (f32[2,2,3,2,64,128]{5,4,3,2,1,0:T(8,128)S(1)}, f32[2,2,3,2,64,128]{5,4,3,2,1,0:T(8,128)S(1)}, bf16[384,512]{1,0:T(8,128)(2,1)S(1)}) custom-call(s32[1]{0:T(128)} %bitcast.place_ref, bf16[2,192,256]{2,1,0:T(8,128)(2,1)S(1)} %bitcast.35, bf16[1,256,2,4096]{3,2,1,0:T(2,128)(2,1)} %grad_ref.7), custom_call_target="tpu_custom_call" | custom-call | tf_op jit(solution)/shard_map/terms11/pallas_call | solution.py:132
  4.6 15.1 %collective-permute-start.4 = (f32[2,2,3,2,64,128]{5,4,3,2,1,0:T(8,128)S(1)}, f32[2,2,3,2,64,128]{5,4,3,2,1,0:T(8,128)S(1)}, u32[]{:S(2)}, u32[]{:S(2)}) collective-permute-start(f32[2,2,3,2,64,128]{5,4,3,2,1,0:T(8,128)S(1)} %get-tuple-element.25), channel_id=1, source_target_pairs={{0,16},{1,17},{2,18},{3,19},{4,20},{5,21},{6,22},{7,23},{8,24},{9,... | collective-permute-start | bytes 2359304 | tf_op jit(solution)/shard_map/ppermute | solution.py:226
  19.8 1.7 %terms01.1 = (f32[2,2,3,2,64,128]{5,4,3,2,1,0:T(8,128)S(1)}, f32[2,2,3,2,64,128]{5,4,3,2,1,0:T(8,128)S(1)}) custom-call(s32[1]{0:T(128)} %bitcast.place_ref, bf16[384,512]{1,0:T(8,128)(2,1)S(1)} %get-tuple-element.15.in_ref, bf16[1,256,2,4096]{3,2,1,0:T(2,128)(2,1)S(1)} %copy-done), custom_call_target="tpu_custom_call" | custom-call | tf_op jit(solution)/shard_map/terms01/pallas_call | solution.py:132
  21.5 5.3 %collective-permute-start = (f32[2,2,3,2,64,128]{5,4,3,2,1,0:T(8,128)S(1)}, f32[2,2,3,2,64,128]{5,4,3,2,1,0:T(8,128)S(1)}, u32[]{:S(2)}, u32[]{:S(2)}) collective-permute-start(f32[2,2,3,2,64,128]{5,4,3,2,1,0:T(8,128)S(1)} %get-tuple-element.19), channel_id=1, source_target_pairs={{0,1},{1,0},{2,3},{3,2},{4,5},{5,4},{6,7},{7,6},{8,9},{9,8},{10,11... | collective-permute-start | bytes 2359304 | tf_op jit(solution)/shard_map/ppermute | solution.py:224
  26.8 1.9 %collective-permute-start.3 = (f32[2,2,3,2,64,128]{5,4,3,2,1,0:T(8,128)S(1)}, f32[2,2,3,2,64,128]{5,4,3,2,1,0:T(8,128)S(1)}, u32[]{:S(2)}, u32[]{:S(2)}) collective-permute-start(f32[2,2,3,2,64,128]{5,4,3,2,1,0:T(8,128)S(1)} %get-tuple-element.23), channel_id=1, source_target_pairs={{0,16},{1,17},{2,18},{3,19},{4,20},{5,21},{6,22},{7,23},{8,24},{9,... | collective-permute-start | bytes 2359304 | tf_op jit(solution)/shard_map/ppermute | solution.py:228
  28.7 1.6 %terms10.1 = (f32[2,2,3,2,64,128]{5,4,3,2,1,0:T(8,128)S(1)}, f32[2,2,3,2,64,128]{5,4,3,2,1,0:T(8,128)S(1)}) custom-call(s32[1]{0:T(128)} %bitcast.place_ref, bf16[384,512]{1,0:T(8,128)(2,1)S(1)} %get-tuple-element.15.in_ref, bf16[1,256,2,4096]{3,2,1,0:T(2,128)(2,1)S(1)} %copy-done), custom_call_target="tpu_custom_call" | custom-call | tf_op jit(solution)/shard_map/terms10/pallas_call | solution.py:132
  30.5 4.0 %collective-permute-start.5 = (f32[2,2,3,2,64,128]{5,4,3,2,1,0:T(8,128)S(1)}, f32[2,2,3,2,64,128]{5,4,3,2,1,0:T(8,128)S(1)}, u32[]{:S(2)}, u32[]{:S(2)}) collective-permute-start(f32[2,2,3,2,64,128]{5,4,3,2,1,0:T(8,128)S(1)} %add.47), channel_id=1, source_target_pairs={{0,1},{1,0},{2,3},{3,2},{4,5},{5,4},{6,7},{7,6},{8,9},{9,8},{10,11... | collective-permute-start | bytes 2359304 | tf_op jit(solution)/shard_map/ppermute | solution.py:228
  34.4 1.6 %terms00.1 = (f32[2,2,3,2,64,128]{5,4,3,2,1,0:T(8,128)S(1)}, f32[2,2,3,2,64,128]{5,4,3,2,1,0:T(8,128)S(1)}) custom-call(s32[1]{0:T(128)} %bitcast.place_ref, bf16[384,512]{1,0:T(8,128)(2,1)S(1)} %get-tuple-element.15.in_ref, bf16[1,256,2,4096]{3,2,1,0:T(2,128)(2,1)S(1)} %copy-done), custom_call_target="tpu_custom_call" | custom-call | tf_op jit(solution)/shard_map/terms00/pallas_call | solution.py:132
  36.2 4.6 %collective-permute-start.1 = (f32[2,2,3,2,64,128]{5,4,3,2,1,0:T(8,128)S(1)}, f32[2,2,3,2,64,128]{5,4,3,2,1,0:T(8,128)S(1)}, u32[]{:S(2)}, u32[]{:S(2)}) collective-permute-start(f32[2,2,3,2,64,128]{5,4,3,2,1,0:T(8,128)S(1)} %get-tuple-element.20), channel_id=1, source_target_pairs={{0,1},{1,0},{2,3},{3,2},{4,5},{5,4},{6,7},{7,6},{8,9},{9,8},{10,11... | collective-permute-start | bytes 2359304 | tf_op jit(solution)/shard_map/ppermute | solution.py:227
  40.8 2.6 %collective-permute-start.2 = (f32[2,2,3,2,64,128]{5,4,3,2,1,0:T(8,128)S(1)}, f32[2,2,3,2,64,128]{5,4,3,2,1,0:T(8,128)S(1)}, u32[]{:S(2)}, u32[]{:S(2)}) collective-permute-start(f32[2,2,3,2,64,128]{5,4,3,2,1,0:T(8,128)S(1)} %add.43), channel_id=1, source_target_pairs={{0,16},{1,17},{2,18},{3,19},{4,20},{5,21},{6,22},{7,23},{8,24},{9,... | collective-permute-start | bytes 2359304 | tf_op jit(solution)/shard_map/ppermute | solution.py:227
  43.4 1.1 collective-permute-done.5
  44.9 7.5 %collective-permute-start.6 = (f32[3,2,64,128]{3,2,1,0:T(8,128)S(1)}, f32[3,2,64,128]{3,2,1,0:T(8,128)S(1)}, u32[]{:S(2)}, u32[]{:S(2)}) collective-permute-start(f32[3,2,64,128]{3,2,1,0:T(8,128)S(1)} %get-tuple-element.28), channel_id=1, source_target_pairs={{0,42},{1,43},{2,40},{3,41},{4,46},{5,47},{6,44},{7,45},{8,34},{9,... | collective-permute-start | bytes 589832 | tf_op jit(solution)/shard_map/ppermute | solution.py:233
  52.4 2.1 %collective-permute-start.9 = (f32[3,2,64,128]{3,2,1,0:T(8,128)S(1)}, f32[3,2,64,128]{3,2,1,0:T(8,128)S(1)}, u32[]{:S(2)}, u32[]{:S(2)}) collective-permute-start(f32[3,2,64,128]{3,2,1,0:T(8,128)S(1)} %get-tuple-element.29), channel_id=1, source_target_pairs={{0,8},{1,9},{2,10},{3,11},{4,12},{5,13},{6,14},{7,15},{8,0},{9,1},... | collective-permute-start | bytes 589832 | tf_op jit(solution)/shard_map/ppermute | solution.py:233
  54.6 5.8 %collective-permute-start.8 = (f32[3,2,64,128]{3,2,1,0:T(8,128)S(1)}, f32[3,2,64,128]{3,2,1,0:T(8,128)S(1)}, u32[]{:S(2)}, u32[]{:S(2)}) collective-permute-start(f32[3,2,64,128]{3,2,1,0:T(8,128)S(1)} %get-tuple-element.30), channel_id=1, source_target_pairs={{0,10},{1,11},{2,8},{3,9},{4,14},{5,15},{6,12},{7,13},{8,2},{9,3},... | collective-permute-start | bytes 589832 | tf_op jit(solution)/shard_map/ppermute | solution.py:233
  60.4 6.2 %collective-permute-start.7 = (f32[3,2,64,128]{3,2,1,0:T(8,128)S(1)}, f32[3,2,64,128]{3,2,1,0:T(8,128)S(1)}, u32[]{:S(2)}, u32[]{:S(2)}) collective-permute-start(f32[3,2,64,128]{3,2,1,0:T(8,128)S(1)} %get-tuple-element.31), channel_id=1, source_target_pairs={{0,40},{1,41},{2,42},{3,43},{4,44},{5,45},{6,46},{7,47},{8,32},{9,... | collective-permute-start | bytes 589832 | tf_op jit(solution)/shard_map/ppermute | solution.py:233
  66.8 6.7 %collective-permute-start.10 = (f32[3,2,64,128]{3,2,1,0:T(8,128)S(1)}, f32[3,2,64,128]{3,2,1,0:T(8,128)S(1)}, u32[]{:S(2)}, u32[]{:S(2)}) collective-permute-start(f32[3,2,64,128]{3,2,1,0:T(8,128)S(1)} %get-tuple-element.32), channel_id=1, source_target_pairs={{0,34},{1,35},{2,32},{3,33},{4,38},{5,39},{6,36},{7,37},{8,42},{9,... | collective-permute-start | bytes 589832 | tf_op jit(solution)/shard_map/ppermute | solution.py:233
  73.6 1.9 %collective-permute-start.12 = (f32[3,2,64,128]{3,2,1,0:T(8,128)S(1)}, f32[3,2,64,128]{3,2,1,0:T(8,128)S(1)}, u32[]{:S(2)}, u32[]{:S(2)}) collective-permute-start(f32[3,2,64,128]{3,2,1,0:T(8,128)S(1)} %get-tuple-element.33), channel_id=1, source_target_pairs={{0,2},{1,3},{2,0},{3,1},{4,6},{5,7},{6,4},{7,5},{8,10},{9,11},{10,... | collective-permute-start | bytes 589832 | tf_op jit(solution)/shard_map/ppermute | solution.py:233
  75.5 3.9 %collective-permute-start.11 = (f32[3,2,64,128]{3,2,1,0:T(8,128)S(1)}, f32[3,2,64,128]{3,2,1,0:T(8,128)S(1)}, u32[]{:S(2)}, u32[]{:S(2)}) collective-permute-start(f32[3,2,64,128]{3,2,1,0:T(8,128)S(1)} %get-tuple-element.34), channel_id=1, source_target_pairs={{0,32},{1,33},{2,34},{3,35},{4,36},{5,37},{6,38},{7,39},{8,40},{9,... | collective-permute-start | bytes 589832 | tf_op jit(solution)/shard_map/ppermute | solution.py:233
  80.3 2.9 %collective-permute-done.12 = f32[3,2,64,128]{3,2,1,0:T(8,128)S(1)} collective-permute-done((f32[3,2,64,128]{3,2,1,0:T(8,128)S(1)}, f32[3,2,64,128]{3,2,1,0:T(8,128)S(1)}, u32[]{:S(2)}, u32[]{:S(2)}) %collective-permute-start.12) | collective-permute-done | bytes 196640 | tf_op jit(solution)/shard_map/ppermute | solution.py:233
  83.2 1.3 %collective-permute-done.11 = f32[3,2,64,128]{3,2,1,0:T(8,128)S(1)} collective-permute-done((f32[3,2,64,128]{3,2,1,0:T(8,128)S(1)}, f32[3,2,64,128]{3,2,1,0:T(8,128)S(1)}, u32[]{:S(2)}, u32[]{:S(2)}) %collective-permute-start.11) | collective-permute-done | bytes 196640 | tf_op jit(solution)/shard_map/ppermute | solution.py:233
  84.6 20.1 %all_to_all.10.parts_ref = f32[6,64,128]{2,1,0:T(8,128)S(1)} all-to-all(f32[6,64,128]{2,1,0:T(8,128)S(1)} %bitcast.36), channel_id=1, replica_groups={{0,4,64,68,128,132},{1,5,65,69,129,133},{2,6,66,70,130,134},{3,7,67,71,..., dimensions={0} | all-to-all | bytes 393216 | tf_op jit(solution)/shard_map/all_to_all | solution.py:234
  104.8 1.6 %encode.1 = (f32[1,1,64,128]{3,2,1,0:T(8,128)}, f32[4,64,128]{2,1,0:T(8,128)S(1)}) custom-call(f32[6,64,128]{2,1,0:T(8,128)S(1)} %all_to_all.10.parts_ref, f32[1,1,64,128]{3,2,1,0:T(8,128)S(1)} %copy-done.4, s32[1,2,32]{2,1,0:T(2,128)S(1)} %copy-done.5, f32[64,64]{1,0:T(8,128)S(1)} %copy-done.3, f32[128,128]{1,0:T(8,128)S(1)} %copy-done.1), custom_call_target="tpu_custom_call" | custom-call | tf_op jit(solution)/shard_map/encode/pallas_call | solution.py:193
  106.3 9.4 %all_to_all.11.every_ref = f32[4,64,128]{2,1,0:T(8,128)S(1)} all-to-all(f32[4,64,128]{2,1,0:T(8,128)S(1)} %get-tuple-element.27), channel_id=1, replica_groups=mesh['replica'=4,'shard'=192] {'replica'}, dimensions={0} | all-to-all | bytes 262144 | tf_op jit(solution)/shard_map/all_to_all | solution.py:236
  (29 shorter events, 2.7 us)
Async XLA Ops:
  0.6 19.1 %copy-start = (bf16[1,256,2,4096]{3,2,1,0:T(2,128)(2,1)S(1)}, bf16[1,256,2,4096]{3,2,1,0:T(2,128)(2,1)}, u32[]{:S(2)}) copy-start(bf16[1,256,2,4096]{3,2,1,0:T(2,128)(2,1)} %grad_ref.7) | copy-start | bytes 12582916
  0.7 1.1 copy-start.2
  4.6 25.7 %collective-permute-start.4 = (f32[2,2,3,2,64,128]{5,4,3,2,1,0:T(8,128)S(1)}, f32[2,2,3,2,64,128]{5,4,3,2,1,0:T(8,128)S(1)}, u32[]{:S(2)}, u32[]{:S(2)}) collective-permute-start(f32[2,2,3,2,64,128]{5,4,3,2,1,0:T(8,128)S(1)} %get-tuple-element.25), channel_id=1, source_target_pairs={{0,16},{1,17},{2,18},{3,19},{4,20},{5,21},{6,22},{7,23},{8,24},{9,... | collective-permute-start | bytes 2359304 | tf_op jit(solution)/shard_map/ppermute | solution.py:226
  21.5 14.6 %collective-permute-start = (f32[2,2,3,2,64,128]{5,4,3,2,1,0:T(8,128)S(1)}, f32[2,2,3,2,64,128]{5,4,3,2,1,0:T(8,128)S(1)}, u32[]{:S(2)}, u32[]{:S(2)}) collective-permute-start(f32[2,2,3,2,64,128]{5,4,3,2,1,0:T(8,128)S(1)} %get-tuple-element.19), channel_id=1, source_target_pairs={{0,1},{1,0},{2,3},{3,2},{4,5},{5,4},{6,7},{7,6},{8,9},{9,8},{10,11... | collective-permute-start | bytes 2359304 | tf_op jit(solution)/shard_map/ppermute | solution.py:224
  26.8 16.6 %collective-permute-start.3 = (f32[2,2,3,2,64,128]{5,4,3,2,1,0:T(8,128)S(1)}, f32[2,2,3,2,64,128]{5,4,3,2,1,0:T(8,128)S(1)}, u32[]{:S(2)}, u32[]{:S(2)}) collective-permute-start(f32[2,2,3,2,64,128]{5,4,3,2,1,0:T(8,128)S(1)} %get-tuple-element.23), channel_id=1, source_target_pairs={{0,16},{1,17},{2,18},{3,19},{4,20},{5,21},{6,22},{7,23},{8,24},{9,... | collective-permute-start | bytes 2359304 | tf_op jit(solution)/shard_map/ppermute | solution.py:228
  30.5 14.1 %collective-permute-start.5 = (f32[2,2,3,2,64,128]{5,4,3,2,1,0:T(8,128)S(1)}, f32[2,2,3,2,64,128]{5,4,3,2,1,0:T(8,128)S(1)}, u32[]{:S(2)}, u32[]{:S(2)}) collective-permute-start(f32[2,2,3,2,64,128]{5,4,3,2,1,0:T(8,128)S(1)} %add.47), channel_id=1, source_target_pairs={{0,1},{1,0},{2,3},{3,2},{4,5},{5,4},{6,7},{7,6},{8,9},{9,8},{10,11... | collective-permute-start | bytes 2359304 | tf_op jit(solution)/shard_map/ppermute | solution.py:228
  36.2 24.1 %collective-permute-start.1 = (f32[2,2,3,2,64,128]{5,4,3,2,1,0:T(8,128)S(1)}, f32[2,2,3,2,64,128]{5,4,3,2,1,0:T(8,128)S(1)}, u32[]{:S(2)}, u32[]{:S(2)}) collective-permute-start(f32[2,2,3,2,64,128]{5,4,3,2,1,0:T(8,128)S(1)} %get-tuple-element.20), channel_id=1, source_target_pairs={{0,1},{1,0},{2,3},{3,2},{4,5},{5,4},{6,7},{7,6},{8,9},{9,8},{10,11... | collective-permute-start | bytes 2359304 | tf_op jit(solution)/shard_map/ppermute | solution.py:227
  40.8 25.8 %collective-permute-start.2 = (f32[2,2,3,2,64,128]{5,4,3,2,1,0:T(8,128)S(1)}, f32[2,2,3,2,64,128]{5,4,3,2,1,0:T(8,128)S(1)}, u32[]{:S(2)}, u32[]{:S(2)}) collective-permute-start(f32[2,2,3,2,64,128]{5,4,3,2,1,0:T(8,128)S(1)} %add.43), channel_id=1, source_target_pairs={{0,16},{1,17},{2,18},{3,19},{4,20},{5,21},{6,22},{7,23},{8,24},{9,... | collective-permute-start | bytes 2359304 | tf_op jit(solution)/shard_map/ppermute | solution.py:227
  44.7 60.0 %copy-start.1 = (f32[128,128]{1,0:T(8,128)S(1)}, f32[128,128]{1,0:T(8,128)}, u32[]{:S(2)}) copy-start(f32[128,128]{1,0:T(8,128)} %constant.13.clone.wide_ref) | copy-start | bytes 196612
  44.8 60.0 %copy-start.3 = (f32[64,64]{1,0:T(8,128)S(1)}, f32[64,64]{1,0:T(8,128)}, u32[]{:S(2)}) copy-start(f32[64,64]{1,0:T(8,128)} %constant.12.clone.left_ref) | copy-start | bytes 49156
  44.8 60.0 %copy-start.4 = (f32[1,1,64,128]{3,2,1,0:T(8,128)S(1)}, f32[1,1,64,128]{3,2,1,0:T(8,128)}, u32[]{:S(2)}) copy-start(f32[1,1,64,128]{3,2,1,0:T(8,128)} %mom_ref.1) | copy-start | bytes 98308
  44.8 60.0 %copy-start.5 = (s32[1,2,32]{2,1,0:T(2,128)S(1)}, s32[1,2,32]{2,1,0:T(2,128)}, u32[]{:S(2)}) copy-start(s32[1,2,32]{2,1,0:T(2,128)} %idx_ref.1) | copy-start | bytes 772
  44.9 28.7 %collective-permute-start.6 = (f32[3,2,64,128]{3,2,1,0:T(8,128)S(1)}, f32[3,2,64,128]{3,2,1,0:T(8,128)S(1)}, u32[]{:S(2)}, u32[]{:S(2)}) collective-permute-start(f32[3,2,64,128]{3,2,1,0:T(8,128)S(1)} %get-tuple-element.28), channel_id=1, source_target_pairs={{0,42},{1,43},{2,40},{3,41},{4,46},{5,47},{6,44},{7,45},{8,34},{9,... | collective-permute-start | bytes 589832 | tf_op jit(solution)/shard_map/ppermute | solution.py:233
  52.4 23.1 %collective-permute-start.9 = (f32[3,2,64,128]{3,2,1,0:T(8,128)S(1)}, f32[3,2,64,128]{3,2,1,0:T(8,128)S(1)}, u32[]{:S(2)}, u32[]{:S(2)}) collective-permute-start(f32[3,2,64,128]{3,2,1,0:T(8,128)S(1)} %get-tuple-element.29), channel_id=1, source_target_pairs={{0,8},{1,9},{2,10},{3,11},{4,12},{5,13},{6,14},{7,15},{8,0},{9,1},... | collective-permute-start | bytes 589832 | tf_op jit(solution)/shard_map/ppermute | solution.py:233
  54.6 24.9 %collective-permute-start.8 = (f32[3,2,64,128]{3,2,1,0:T(8,128)S(1)}, f32[3,2,64,128]{3,2,1,0:T(8,128)S(1)}, u32[]{:S(2)}, u32[]{:S(2)}) collective-permute-start(f32[3,2,64,128]{3,2,1,0:T(8,128)S(1)} %get-tuple-element.30), channel_id=1, source_target_pairs={{0,10},{1,11},{2,8},{3,9},{4,14},{5,15},{6,12},{7,13},{8,2},{9,3},... | collective-permute-start | bytes 589832 | tf_op jit(solution)/shard_map/ppermute | solution.py:233
  60.4 19.1 %collective-permute-start.7 = (f32[3,2,64,128]{3,2,1,0:T(8,128)S(1)}, f32[3,2,64,128]{3,2,1,0:T(8,128)S(1)}, u32[]{:S(2)}, u32[]{:S(2)}) collective-permute-start(f32[3,2,64,128]{3,2,1,0:T(8,128)S(1)} %get-tuple-element.31), channel_id=1, source_target_pairs={{0,40},{1,41},{2,42},{3,43},{4,44},{5,45},{6,46},{7,47},{8,32},{9,... | collective-permute-start | bytes 589832 | tf_op jit(solution)/shard_map/ppermute | solution.py:233
  66.8 13.4 %collective-permute-start.10 = (f32[3,2,64,128]{3,2,1,0:T(8,128)S(1)}, f32[3,2,64,128]{3,2,1,0:T(8,128)S(1)}, u32[]{:S(2)}, u32[]{:S(2)}) collective-permute-start(f32[3,2,64,128]{3,2,1,0:T(8,128)S(1)} %get-tuple-element.32), channel_id=1, source_target_pairs={{0,34},{1,35},{2,32},{3,33},{4,38},{5,39},{6,36},{7,37},{8,42},{9,... | collective-permute-start | bytes 589832 | tf_op jit(solution)/shard_map/ppermute | solution.py:233
  73.6 9.6 %collective-permute-start.12 = (f32[3,2,64,128]{3,2,1,0:T(8,128)S(1)}, f32[3,2,64,128]{3,2,1,0:T(8,128)S(1)}, u32[]{:S(2)}, u32[]{:S(2)}) collective-permute-start(f32[3,2,64,128]{3,2,1,0:T(8,128)S(1)} %get-tuple-element.33), channel_id=1, source_target_pairs={{0,2},{1,3},{2,0},{3,1},{4,6},{5,7},{6,4},{7,5},{8,10},{9,11},{10,... | collective-permute-start | bytes 589832 | tf_op jit(solution)/shard_map/ppermute | solution.py:233
  75.5 9.0 %collective-permute-start.11 = (f32[3,2,64,128]{3,2,1,0:T(8,128)S(1)}, f32[3,2,64,128]{3,2,1,0:T(8,128)S(1)}, u32[]{:S(2)}, u32[]{:S(2)}) collective-permute-start(f32[3,2,64,128]{3,2,1,0:T(8,128)S(1)} %get-tuple-element.34), channel_id=1, source_target_pairs={{0,32},{1,33},{2,34},{3,35},{4,36},{5,37},{6,38},{7,39},{8,40},{9,... | collective-permute-start | bytes 589832 | tf_op jit(solution)/shard_map/ppermute | solution.py:233

commit v9 on v8

--- a/solution.py
+++ b/solution.py
@@ -164,18 +164,25 @@
     return jnp.concatenate(masks, axis=1)
 
 
-def encode_kernel(parts_ref, mom_ref, idx_ref, left_ref, wide_ref, new_ref, sent_ref):
+def mask_kernel(idx_ref, mask_ref):
+    mask_ref[...] = one_hots(idx_ref)
+
+
+def encode_kernel(parts_ref, mom_ref, mask_ref, left_ref, wide_ref, pre_ref, sent_ref):
     gradient = parts_ref[0]
     for k in range(1, parts_ref.shape[0]):
         gradient = gradient + parts_ref[k]
     pre = MOMENTUM_DECAY * mom_ref[0, 0] + gradient
-    mask = one_hots(idx_ref)
     coeffs = dot(dot(left_ref[...], pre, ((1,), (0,))), wide_ref[...], ((1,), (1,)))
-    kept = coeffs * mask
+    kept = coeffs * mask_ref[...]
+    pre_ref[...] = pre
     for k in range(REPLICAS):
         sent_ref[k] = kept
-    back = dot(dot(left_ref[...], kept, ((0,), (0,))), wide_ref[...], ((1,), (0,)))
-    new_ref[0, 0] = pre - back
+
+
+def residual_kernel(pre_ref, sent_ref, left_ref, wide_ref, new_ref):
+    back = dot(dot(left_ref[...], sent_ref[0], ((0,), (0,))), wide_ref[...], ((1,), (0,)))
+    new_ref[0, 0] = pre_ref[...] - back
 
 
 def decode_kernel(every_ref, left_ref, wide_ref, out_ref):
@@ -189,16 +196,25 @@
     return jnp.asarray(side), jnp.asarray(np.kron(np.eye(LAYERS, dtype=np.float32), side))
 
 
+def small_call(kernel, shape, name):
+    return pl.pallas_call(
+        kernel,
+        out_shape=shape,
+        compiler_params=pltpu.CompilerParams(vmem_limit_bytes=4 * 2**20),
+        name=name,
+    )
+
+
 def encode(parts, momentum, band_idx):
-    return pl.pallas_call(
-        encode_kernel,
-        out_shape=(
-            jax.ShapeDtypeStruct((1, 1, SIDE, WIDE), jnp.float32),
-            jax.ShapeDtypeStruct((REPLICAS, SIDE, WIDE), jnp.float32),
-        ),
-        compiler_params=pltpu.CompilerParams(vmem_limit_bytes=4 * 2**20),
-        name="encode",
-    )(parts, momentum, band_idx, *matrices())
+    tile = jax.ShapeDtypeStruct((SIDE, WIDE), jnp.float32)
+    every = jax.ShapeDtypeStruct((REPLICAS, SIDE, WIDE), jnp.float32)
+    mask = small_call(mask_kernel, tile, "mask")(band_idx)
+    return small_call(encode_kernel, (tile, every), "encode")(parts, momentum, mask, *matrices())
+
+
+def residual(pre, sent):
+    shape = jax.ShapeDtypeStruct((1, 1, SIDE, WIDE), jnp.float32)
+    return small_call(residual_kernel, shape, "residual")(pre, sent, *matrices())
 
 
 def decode(every):
@@ -232,8 +248,9 @@
             if other_x or not (z_like and y_like):
                 terms += hop(piece[z_like, y_like], perm=pairs(other_x, 1 - z_like, 1 - y_like, 2))
     terms = exchange(terms.reshape(6, SIDE, WIDE), axis_index_groups=stage_groups())
-    new_momentum, sent = encode(terms, momentum, band_idx)
+    pre, sent = encode(terms, momentum, band_idx)
     every = lax.all_to_all(sent, "replica", split_axis=0, concat_axis=0, tiled=True)
+    new_momentum = residual(pre, sent)
     update = decode(every)
     return (new_momentum, update)
 

time: 117 us -> 119 us (1.017)
  blocking collectives: 29.5 us -> 0 us
  waiting for transfers between devices: 6.22 us -> 21.7 us
  starting transfers between devices: 67.7 us -> 80.5 us
  Pallas kernels: 10.5 us -> 12.2 us
    all_to_all x2 -> x0, blocking collectives: 29.5 us -> none  [the longest x1 20.1 us: local(): exchange(terms.reshape(6, SIDE, WIDE), axis_index_groups=stage_groups())]
    all_to_all x0 -> x2, waiting for transfers between devices: none -> 15.6 us  [the longest x1 14 us: local(): exchange(terms.reshape(6, SIDE, WIDE), axis_index_groups=stage_groups())]
    all_to_all x0 -> x2, starting transfers between devices: none -> 12.8 us  [the longest x1 6.72 us: local(): lax.all_to_all(sent, 'replica', split_axis=0, concat_axis=0, tiled=True)]
    pallas_call x1 -> x3, Pallas kernels: 1.56 us -> 3.29 us  [the longest x1 1.98 us: residual(): small_call(residual_kernel, shape, 'residual')(pre, sent, *matrices())]
  transfers between devices with their start and end apart: 13 -> 15, of which waited for: 4 -> 5; matrix products, arithmetic and copies ran while one was open for 1% -> 1% of each run, Pallas kernels for 4% -> 6%
where the time goes in v9:
time: 119 us; the launch traced here: 118 us
  starting transfers between devices  80.5 us (68%)
  waiting for transfers between devices  21.7 us (18%)
  Pallas kernels  12.2 us (10%)
  other arithmetic  1.39 us (1%)
  local copies, waits for them, and re-layouts  1.22 us (1%)
    ppermute x7, starting transfers between devices, local(): hop(piece[z_like, y_like], perm=pairs(other_x, 1 - z_like, 1 - y_like, 2))  34.3 us
    ppermute x1, starting transfers between devices, local(): other1 = near1_other + hop(far1_other, perm=across_z)  15.1 us
    all_to_all x1, waiting for transfers between devices, local(): exchange(terms.reshape(6, SIDE, WIDE), axis_index_groups=stage_groups())  14 us
    pallas_call x4, Pallas kernels, gradient_terms(): pl.pallas_call(functools.partial(terms_kernel, first), grid_spec=pltpu.Pr...  7.86 us
    all_to_all x1, starting transfers between devices, local(): lax.all_to_all(sent, 'replica', split_axis=0, concat_axis=0, tiled=True)  6.72 us
    all_to_all x1, starting transfers between devices, local(): exchange(terms.reshape(6, SIDE, WIDE), axis_index_groups=stage_groups())  6.05 us
    ppermute x2, starting transfers between devices, local(): sum1 = near1_own + hop(far1_own, perm=across_z) + hop(other1, perm=across_y)  5.9 us
    ppermute x1, starting transfers between devices, local(): far0 = far0_own + hop(far0_other, perm=across_y)  5.25 us
  transfers between devices with their start and end apart: 15, of which 5 were waited for; matrix products, arithmetic and copies ran while one was open for 1% of the time, Pallas kernels for 6%

profile of v9, /device:TPU:1, one launch (start us, length us, event | category | flops | bytes accessed | tf_op | source)
XLA Modules:
  0.0 118.0 jit_solution(1336978743426956004)
XLA Ops:
  1.7 2.9 %terms11.1 = (f32[2,2,3,2,64,128]{5,4,3,2,1,0:T(8,128)S(1)}, f32[2,2,3,2,64,128]{5,4,3,2,1,0:T(8,128)S(1)}, bf16[384,512]{1,0:T(8,128)(2,1)S(1)}) custom-call(s32[1]{0:T(128)} %bitcast.place_ref, bf16[2,192,256]{2,1,0:T(8,128)(2,1)S(1)} %bitcast.35, bf16[1,256,2,4096]{3,2,1,0:T(2,128)(2,1)} %grad_ref.7), custom_call_target="tpu_custom_call" | custom-call | tf_op jit(solution)/shard_map/terms11/pallas_call | solution.py:132
  4.6 15.1 %collective-permute-start.4 = (f32[2,2,3,2,64,128]{5,4,3,2,1,0:T(8,128)S(1)}, f32[2,2,3,2,64,128]{5,4,3,2,1,0:T(8,128)S(1)}, u32[]{:S(2)}, u32[]{:S(2)}) collective-permute-start(f32[2,2,3,2,64,128]{5,4,3,2,1,0:T(8,128)S(1)} %get-tuple-element.25), channel_id=1, source_target_pairs={{0,16},{1,17},{2,18},{3,19},{4,20},{5,21},{6,22},{7,23},{8,24},{9,... | collective-permute-start | bytes 2359304 | tf_op jit(solution)/shard_map/ppermute | solution.py:242
  19.8 1.7 %terms01.1 = (f32[2,2,3,2,64,128]{5,4,3,2,1,0:T(8,128)S(1)}, f32[2,2,3,2,64,128]{5,4,3,2,1,0:T(8,128)S(1)}) custom-call(s32[1]{0:T(128)} %bitcast.place_ref, bf16[384,512]{1,0:T(8,128)(2,1)S(1)} %get-tuple-element.15.in_ref, bf16[1,256,2,4096]{3,2,1,0:T(2,128)(2,1)S(1)} %copy-done), custom_call_target="tpu_custom_call" | custom-call | tf_op jit(solution)/shard_map/terms01/pallas_call | solution.py:132
  21.5 5.3 %collective-permute-start = (f32[2,2,3,2,64,128]{5,4,3,2,1,0:T(8,128)S(1)}, f32[2,2,3,2,64,128]{5,4,3,2,1,0:T(8,128)S(1)}, u32[]{:S(2)}, u32[]{:S(2)}) collective-permute-start(f32[2,2,3,2,64,128]{5,4,3,2,1,0:T(8,128)S(1)} %get-tuple-element.19), channel_id=1, source_target_pairs={{0,1},{1,0},{2,3},{3,2},{4,5},{5,4},{6,7},{7,6},{8,9},{9,8},{10,11... | collective-permute-start | bytes 2359304 | tf_op jit(solution)/shard_map/ppermute | solution.py:240
  26.8 1.9 %collective-permute-start.3 = (f32[2,2,3,2,64,128]{5,4,3,2,1,0:T(8,128)S(1)}, f32[2,2,3,2,64,128]{5,4,3,2,1,0:T(8,128)S(1)}, u32[]{:S(2)}, u32[]{:S(2)}) collective-permute-start(f32[2,2,3,2,64,128]{5,4,3,2,1,0:T(8,128)S(1)} %get-tuple-element.23), channel_id=1, source_target_pairs={{0,16},{1,17},{2,18},{3,19},{4,20},{5,21},{6,22},{7,23},{8,24},{9,... | collective-permute-start | bytes 2359304 | tf_op jit(solution)/shard_map/ppermute | solution.py:244
  28.7 1.6 %terms10.1 = (f32[2,2,3,2,64,128]{5,4,3,2,1,0:T(8,128)S(1)}, f32[2,2,3,2,64,128]{5,4,3,2,1,0:T(8,128)S(1)}) custom-call(s32[1]{0:T(128)} %bitcast.place_ref, bf16[384,512]{1,0:T(8,128)(2,1)S(1)} %get-tuple-element.15.in_ref, bf16[1,256,2,4096]{3,2,1,0:T(2,128)(2,1)S(1)} %copy-done), custom_call_target="tpu_custom_call" | custom-call | tf_op jit(solution)/shard_map/terms10/pallas_call | solution.py:132
  30.5 4.0 %collective-permute-start.5 = (f32[2,2,3,2,64,128]{5,4,3,2,1,0:T(8,128)S(1)}, f32[2,2,3,2,64,128]{5,4,3,2,1,0:T(8,128)S(1)}, u32[]{:S(2)}, u32[]{:S(2)}) collective-permute-start(f32[2,2,3,2,64,128]{5,4,3,2,1,0:T(8,128)S(1)} %add.47), channel_id=1, source_target_pairs={{0,1},{1,0},{2,3},{3,2},{4,5},{5,4},{6,7},{7,6},{8,9},{9,8},{10,11... | collective-permute-start | bytes 2359304 | tf_op jit(solution)/shard_map/ppermute | solution.py:244
  34.4 1.6 %terms00.1 = (f32[2,2,3,2,64,128]{5,4,3,2,1,0:T(8,128)S(1)}, f32[2,2,3,2,64,128]{5,4,3,2,1,0:T(8,128)S(1)}) custom-call(s32[1]{0:T(128)} %bitcast.place_ref, bf16[384,512]{1,0:T(8,128)(2,1)S(1)} %get-tuple-element.15.in_ref, bf16[1,256,2,4096]{3,2,1,0:T(2,128)(2,1)S(1)} %copy-done), custom_call_target="tpu_custom_call" | custom-call | tf_op jit(solution)/shard_map/terms00/pallas_call | solution.py:132
  36.2 4.6 %collective-permute-start.1 = (f32[2,2,3,2,64,128]{5,4,3,2,1,0:T(8,128)S(1)}, f32[2,2,3,2,64,128]{5,4,3,2,1,0:T(8,128)S(1)}, u32[]{:S(2)}, u32[]{:S(2)}) collective-permute-start(f32[2,2,3,2,64,128]{5,4,3,2,1,0:T(8,128)S(1)} %get-tuple-element.20), channel_id=1, source_target_pairs={{0,1},{1,0},{2,3},{3,2},{4,5},{5,4},{6,7},{7,6},{8,9},{9,8},{10,11... | collective-permute-start | bytes 2359304 | tf_op jit(solution)/shard_map/ppermute | solution.py:243
  40.8 2.6 %collective-permute-start.2 = (f32[2,2,3,2,64,128]{5,4,3,2,1,0:T(8,128)S(1)}, f32[2,2,3,2,64,128]{5,4,3,2,1,0:T(8,128)S(1)}, u32[]{:S(2)}, u32[]{:S(2)}) collective-permute-start(f32[2,2,3,2,64,128]{5,4,3,2,1,0:T(8,128)S(1)} %add.43), channel_id=1, source_target_pairs={{0,16},{1,17},{2,18},{3,19},{4,20},{5,21},{6,22},{7,23},{8,24},{9,... | collective-permute-start | bytes 2359304 | tf_op jit(solution)/shard_map/ppermute | solution.py:243
  44.9 7.5 %collective-permute-start.6 = (f32[3,2,64,128]{3,2,1,0:T(8,128)S(1)}, f32[3,2,64,128]{3,2,1,0:T(8,128)S(1)}, u32[]{:S(2)}, u32[]{:S(2)}) collective-permute-start(f32[3,2,64,128]{3,2,1,0:T(8,128)S(1)} %get-tuple-element.28), channel_id=1, source_target_pairs={{0,42},{1,43},{2,40},{3,41},{4,46},{5,47},{6,44},{7,45},{8,34},{9,... | collective-permute-start | bytes 589832 | tf_op jit(solution)/shard_map/ppermute | solution.py:249
  52.4 2.1 %collective-permute-start.9 = (f32[3,2,64,128]{3,2,1,0:T(8,128)S(1)}, f32[3,2,64,128]{3,2,1,0:T(8,128)S(1)}, u32[]{:S(2)}, u32[]{:S(2)}) collective-permute-start(f32[3,2,64,128]{3,2,1,0:T(8,128)S(1)} %get-tuple-element.29), channel_id=1, source_target_pairs={{0,8},{1,9},{2,10},{3,11},{4,12},{5,13},{6,14},{7,15},{8,0},{9,1},... | collective-permute-start | bytes 589832 | tf_op jit(solution)/shard_map/ppermute | solution.py:249
  54.6 5.8 %collective-permute-start.8 = (f32[3,2,64,128]{3,2,1,0:T(8,128)S(1)}, f32[3,2,64,128]{3,2,1,0:T(8,128)S(1)}, u32[]{:S(2)}, u32[]{:S(2)}) collective-permute-start(f32[3,2,64,128]{3,2,1,0:T(8,128)S(1)} %get-tuple-element.30), channel_id=1, source_target_pairs={{0,10},{1,11},{2,8},{3,9},{4,14},{5,15},{6,12},{7,13},{8,2},{9,3},... | collective-permute-start | bytes 589832 | tf_op jit(solution)/shard_map/ppermute | solution.py:249
  60.4 6.2 %collective-permute-start.7 = (f32[3,2,64,128]{3,2,1,0:T(8,128)S(1)}, f32[3,2,64,128]{3,2,1,0:T(8,128)S(1)}, u32[]{:S(2)}, u32[]{:S(2)}) collective-permute-start(f32[3,2,64,128]{3,2,1,0:T(8,128)S(1)} %get-tuple-element.31), channel_id=1, source_target_pairs={{0,40},{1,41},{2,42},{3,43},{4,44},{5,45},{6,46},{7,47},{8,32},{9,... | collective-permute-start | bytes 589832 | tf_op jit(solution)/shard_map/ppermute | solution.py:249
  66.9 6.7 %collective-permute-start.10 = (f32[3,2,64,128]{3,2,1,0:T(8,128)S(1)}, f32[3,2,64,128]{3,2,1,0:T(8,128)S(1)}, u32[]{:S(2)}, u32[]{:S(2)}) collective-permute-start(f32[3,2,64,128]{3,2,1,0:T(8,128)S(1)} %get-tuple-element.32), channel_id=1, source_target_pairs={{0,34},{1,35},{2,32},{3,33},{4,38},{5,39},{6,36},{7,37},{8,42},{9,... | collective-permute-start | bytes 589832 | tf_op jit(solution)/shard_map/ppermute | solution.py:249
  73.6 1.9 %collective-permute-start.12 = (f32[3,2,64,128]{3,2,1,0:T(8,128)S(1)}, f32[3,2,64,128]{3,2,1,0:T(8,128)S(1)}, u32[]{:S(2)}, u32[]{:S(2)}) collective-permute-start(f32[3,2,64,128]{3,2,1,0:T(8,128)S(1)} %get-tuple-element.33), channel_id=1, source_target_pairs={{0,2},{1,3},{2,0},{3,1},{4,6},{5,7},{6,4},{7,5},{8,10},{9,11},{10,... | collective-permute-start | bytes 589832 | tf_op jit(solution)/shard_map/ppermute | solution.py:249
  75.6 3.9 %collective-permute-start.11 = (f32[3,2,64,128]{3,2,1,0:T(8,128)S(1)}, f32[3,2,64,128]{3,2,1,0:T(8,128)S(1)}, u32[]{:S(2)}, u32[]{:S(2)}) collective-permute-start(f32[3,2,64,128]{3,2,1,0:T(8,128)S(1)} %get-tuple-element.34), channel_id=1, source_target_pairs={{0,32},{1,33},{2,34},{3,35},{4,36},{5,37},{6,38},{7,39},{8,40},{9,... | collective-permute-start | bytes 589832 | tf_op jit(solution)/shard_map/ppermute | solution.py:249
  79.6 3.7 %collective-permute-done.12 = f32[3,2,64,128]{3,2,1,0:T(8,128)S(1)} collective-permute-done((f32[3,2,64,128]{3,2,1,0:T(8,128)S(1)}, f32[3,2,64,128]{3,2,1,0:T(8,128)S(1)}, u32[]{:S(2)}, u32[]{:S(2)}) %collective-permute-start.12) | collective-permute-done | bytes 196640 | tf_op jit(solution)/shard_map/ppermute | solution.py:249
  83.2 1.3 %collective-permute-done.11 = f32[3,2,64,128]{3,2,1,0:T(8,128)S(1)} collective-permute-done((f32[3,2,64,128]{3,2,1,0:T(8,128)S(1)}, f32[3,2,64,128]{3,2,1,0:T(8,128)S(1)}, u32[]{:S(2)}, u32[]{:S(2)}) %collective-permute-start.11) | collective-permute-done | bytes 196640 | tf_op jit(solution)/shard_map/ppermute | solution.py:249
  85.3 6.0 %all-to-all-start = ((f32[6,64,128]{2,1,0:T(8,128)}), f32[6,64,128]{2,1,0:T(8,128)S(1)}, u32[]{:S(2)}, u32[]{:S(2)}) async-start(f32[6,64,128]{2,1,0:T(8,128)} %bitcast.11), calls=%async_computation | async-start | bytes 393216 | tf_op jit(solution)/shard_map/all_to_all | solution.py:250
  91.6 14.0 %all-to-all-done.parts_ref = f32[6,64,128]{2,1,0:T(8,128)S(1)} async-done(((f32[6,64,128]{2,1,0:T(8,128)}), f32[6,64,128]{2,1,0:T(8,128)S(1)}, u32[]{:S(2)}, u32[]{:S(2)}) %all-to-all-start) | async-done | bytes 196640 | tf_op jit(solution)/shard_map/all_to_all | solution.py:250
  106.6 6.7 %all-to-all-start.1 = ((f32[4,64,128]{2,1,0:T(8,128)}), f32[4,64,128]{2,1,0:T(8,128)S(1)}, u32[]{:S(2)}, u32[]{:S(2)}) async-start(f32[4,64,128]{2,1,0:T(8,128)} %get-tuple-element.27.sent_ref), calls=%async_computation.1 | async-start | bytes 262144 | tf_op jit(solution)/shard_map/all_to_all | solution.py:252
  113.3 2.0 %residual.1 = f32[1,1,64,128]{3,2,1,0:T(8,128)} custom-call(f32[64,128]{1,0:T(8,128)S(1)} %get-tuple-element.26.pre_ref, f32[4,64,128]{2,1,0:T(8,128)} %get-tuple-element.27.sent_ref, f32[64,64]{1,0:T(8,128)S(1)} %copy-done.2, f32[128,128]{1,0:T(8,128)S(1)} %copy-done.1), custom_call_target="tpu_custom_call" | custom-call | tf_op jit(solution)/shard_map/residual/pallas_call | solution.py:217
  115.3 1.6 %all-to-all-done.1.every_ref = f32[4,64,128]{2,1,0:T(8,128)S(1)} async-done(((f32[4,64,128]{2,1,0:T(8,128)}), f32[4,64,128]{2,1,0:T(8,128)S(1)}, u32[]{:S(2)}, u32[]{:S(2)}) %all-to-all-start.1) | async-done | bytes 131104 | tf_op jit(solution)/shard_map/all_to_all | solution.py:252
  (33 shorter events, 6.2 us)
Async XLA Ops:
  0.6 19.1 %copy-start = (bf16[1,256,2,4096]{3,2,1,0:T(2,128)(2,1)S(1)}, bf16[1,256,2,4096]{3,2,1,0:T(2,128)(2,1)}, u32[]{:S(2)}) copy-start(bf16[1,256,2,4096]{3,2,1,0:T(2,128)(2,1)} %grad_ref.7) | copy-start | bytes 12582916
  0.7 1.1 copy-start.3
  4.6 25.7 %collective-permute-start.4 = (f32[2,2,3,2,64,128]{5,4,3,2,1,0:T(8,128)S(1)}, f32[2,2,3,2,64,128]{5,4,3,2,1,0:T(8,128)S(1)}, u32[]{:S(2)}, u32[]{:S(2)}) collective-permute-start(f32[2,2,3,2,64,128]{5,4,3,2,1,0:T(8,128)S(1)} %get-tuple-element.25), channel_id=1, source_target_pairs={{0,16},{1,17},{2,18},{3,19},{4,20},{5,21},{6,22},{7,23},{8,24},{9,... | collective-permute-start | bytes 2359304 | tf_op jit(solution)/shard_map/ppermute | solution.py:242
  21.5 14.6 %collective-permute-start = (f32[2,2,3,2,64,128]{5,4,3,2,1,0:T(8,128)S(1)}, f32[2,2,3,2,64,128]{5,4,3,2,1,0:T(8,128)S(1)}, u32[]{:S(2)}, u32[]{:S(2)}) collective-permute-start(f32[2,2,3,2,64,128]{5,4,3,2,1,0:T(8,128)S(1)} %get-tuple-element.19), channel_id=1, source_target_pairs={{0,1},{1,0},{2,3},{3,2},{4,5},{5,4},{6,7},{7,6},{8,9},{9,8},{10,11... | collective-permute-start | bytes 2359304 | tf_op jit(solution)/shard_map/ppermute | solution.py:240
  26.8 16.6 %collective-permute-start.3 = (f32[2,2,3,2,64,128]{5,4,3,2,1,0:T(8,128)S(1)}, f32[2,2,3,2,64,128]{5,4,3,2,1,0:T(8,128)S(1)}, u32[]{:S(2)}, u32[]{:S(2)}) collective-permute-start(f32[2,2,3,2,64,128]{5,4,3,2,1,0:T(8,128)S(1)} %get-tuple-element.23), channel_id=1, source_target_pairs={{0,16},{1,17},{2,18},{3,19},{4,20},{5,21},{6,22},{7,23},{8,24},{9,... | collective-permute-start | bytes 2359304 | tf_op jit(solution)/shard_map/ppermute | solution.py:244
  30.5 14.1 %collective-permute-start.5 = (f32[2,2,3,2,64,128]{5,4,3,2,1,0:T(8,128)S(1)}, f32[2,2,3,2,64,128]{5,4,3,2,1,0:T(8,128)S(1)}, u32[]{:S(2)}, u32[]{:S(2)}) collective-permute-start(f32[2,2,3,2,64,128]{5,4,3,2,1,0:T(8,128)S(1)} %add.47), channel_id=1, source_target_pairs={{0,1},{1,0},{2,3},{3,2},{4,5},{5,4},{6,7},{7,6},{8,9},{9,8},{10,11... | collective-permute-start | bytes 2359304 | tf_op jit(solution)/shard_map/ppermute | solution.py:244
  36.2 24.1 %collective-permute-start.1 = (f32[2,2,3,2,64,128]{5,4,3,2,1,0:T(8,128)S(1)}, f32[2,2,3,2,64,128]{5,4,3,2,1,0:T(8,128)S(1)}, u32[]{:S(2)}, u32[]{:S(2)}) collective-permute-start(f32[2,2,3,2,64,128]{5,4,3,2,1,0:T(8,128)S(1)} %get-tuple-element.20), channel_id=1, source_target_pairs={{0,1},{1,0},{2,3},{3,2},{4,5},{5,4},{6,7},{7,6},{8,9},{9,8},{10,11... | collective-permute-start | bytes 2359304 | tf_op jit(solution)/shard_map/ppermute | solution.py:243
  40.8 25.8 %collective-permute-start.2 = (f32[2,2,3,2,64,128]{5,4,3,2,1,0:T(8,128)S(1)}, f32[2,2,3,2,64,128]{5,4,3,2,1,0:T(8,128)S(1)}, u32[]{:S(2)}, u32[]{:S(2)}) collective-permute-start(f32[2,2,3,2,64,128]{5,4,3,2,1,0:T(8,128)S(1)} %add.43), channel_id=1, source_target_pairs={{0,16},{1,17},{2,18},{3,19},{4,20},{5,21},{6,22},{7,23},{8,24},{9,... | collective-permute-start | bytes 2359304 | tf_op jit(solution)/shard_map/ppermute | solution.py:243
  44.7 46.6 %copy-start.5 = (s32[1,2,32]{2,1,0:T(2,128)S(1)}, s32[1,2,32]{2,1,0:T(2,128)}, u32[]{:S(2)}) copy-start(s32[1,2,32]{2,1,0:T(2,128)} %idx_ref.1) | copy-start | bytes 772
  44.8 60.8 %copy-start.1 = (f32[128,128]{1,0:T(8,128)S(1)}, f32[128,128]{1,0:T(8,128)}, u32[]{:S(2)}) copy-start(f32[128,128]{1,0:T(8,128)} %constant.13.clone.wide_ref) | copy-start | bytes 196612
  44.8 60.8 %copy-start.2 = (f32[64,64]{1,0:T(8,128)S(1)}, f32[64,64]{1,0:T(8,128)}, u32[]{:S(2)}) copy-start(f32[64,64]{1,0:T(8,128)} %constant.12.clone.left_ref) | copy-start | bytes 49156
  44.8 60.8 %copy-start.4 = (f32[1,1,64,128]{3,2,1,0:T(8,128)S(1)}, f32[1,1,64,128]{3,2,1,0:T(8,128)}, u32[]{:S(2)}) copy-start(f32[1,1,64,128]{3,2,1,0:T(8,128)} %mom_ref.1) | copy-start | bytes 98308
  44.9 28.8 %collective-permute-start.6 = (f32[3,2,64,128]{3,2,1,0:T(8,128)S(1)}, f32[3,2,64,128]{3,2,1,0:T(8,128)S(1)}, u32[]{:S(2)}, u32[]{:S(2)}) collective-permute-start(f32[3,2,64,128]{3,2,1,0:T(8,128)S(1)} %get-tuple-element.28), channel_id=1, source_target_pairs={{0,42},{1,43},{2,40},{3,41},{4,46},{5,47},{6,44},{7,45},{8,34},{9,... | collective-permute-start | bytes 589832 | tf_op jit(solution)/shard_map/ppermute | solution.py:249
  52.4 23.1 %collective-permute-start.9 = (f32[3,2,64,128]{3,2,1,0:T(8,128)S(1)}, f32[3,2,64,128]{3,2,1,0:T(8,128)S(1)}, u32[]{:S(2)}, u32[]{:S(2)}) collective-permute-start(f32[3,2,64,128]{3,2,1,0:T(8,128)S(1)} %get-tuple-element.29), channel_id=1, source_target_pairs={{0,8},{1,9},{2,10},{3,11},{4,12},{5,13},{6,14},{7,15},{8,0},{9,1},... | collective-permute-start | bytes 589832 | tf_op jit(solution)/shard_map/ppermute | solution.py:249
  54.6 25.0 %collective-permute-start.8 = (f32[3,2,64,128]{3,2,1,0:T(8,128)S(1)}, f32[3,2,64,128]{3,2,1,0:T(8,128)S(1)}, u32[]{:S(2)}, u32[]{:S(2)}) collective-permute-start(f32[3,2,64,128]{3,2,1,0:T(8,128)S(1)} %get-tuple-element.30), channel_id=1, source_target_pairs={{0,10},{1,11},{2,8},{3,9},{4,14},{5,15},{6,12},{7,13},{8,2},{9,3},... | collective-permute-start | bytes 589832 | tf_op jit(solution)/shard_map/ppermute | solution.py:249
  60.4 19.2 %collective-permute-start.7 = (f32[3,2,64,128]{3,2,1,0:T(8,128)S(1)}, f32[3,2,64,128]{3,2,1,0:T(8,128)S(1)}, u32[]{:S(2)}, u32[]{:S(2)}) collective-permute-start(f32[3,2,64,128]{3,2,1,0:T(8,128)S(1)} %get-tuple-element.31), channel_id=1, source_target_pairs={{0,40},{1,41},{2,42},{3,43},{4,44},{5,45},{6,46},{7,47},{8,32},{9,... | collective-permute-start | bytes 589832 | tf_op jit(solution)/shard_map/ppermute | solution.py:249
  66.9 12.7 %collective-permute-start.10 = (f32[3,2,64,128]{3,2,1,0:T(8,128)S(1)}, f32[3,2,64,128]{3,2,1,0:T(8,128)S(1)}, u32[]{:S(2)}, u32[]{:S(2)}) collective-permute-start(f32[3,2,64,128]{3,2,1,0:T(8,128)S(1)} %get-tuple-element.32), channel_id=1, source_target_pairs={{0,34},{1,35},{2,32},{3,33},{4,38},{5,39},{6,36},{7,37},{8,42},{9,... | collective-permute-start | bytes 589832 | tf_op jit(solution)/shard_map/ppermute | solution.py:249
  73.6 9.6 %collective-permute-start.12 = (f32[3,2,64,128]{3,2,1,0:T(8,128)S(1)}, f32[3,2,64,128]{3,2,1,0:T(8,128)S(1)}, u32[]{:S(2)}, u32[]{:S(2)}) collective-permute-start(f32[3,2,64,128]{3,2,1,0:T(8,128)S(1)} %get-tuple-element.33), channel_id=1, source_target_pairs={{0,2},{1,3},{2,0},{3,1},{4,6},{5,7},{6,4},{7,5},{8,10},{9,11},{10,... | collective-permute-start | bytes 589832 | tf_op jit(solution)/shard_map/ppermute | solution.py:249
  75.6 8.9 %collective-permute-start.11 = (f32[3,2,64,128]{3,2,1,0:T(8,128)S(1)}, f32[3,2,64,128]{3,2,1,0:T(8,128)S(1)}, u32[]{:S(2)}, u32[]{:S(2)}) collective-permute-start(f32[3,2,64,128]{3,2,1,0:T(8,128)S(1)} %get-tuple-element.34), channel_id=1, source_target_pairs={{0,32},{1,33},{2,34},{3,35},{4,36},{5,37},{6,38},{7,39},{8,40},{9,... | collective-permute-start | bytes 589832 | tf_op jit(solution)/shard_map/ppermute | solution.py:249
  85.3 20.3 %all-to-all-start = ((f32[6,64,128]{2,1,0:T(8,128)}), f32[6,64,128]{2,1,0:T(8,128)S(1)}, u32[]{:S(2)}, u32[]{:S(2)}) async-start(f32[6,64,128]{2,1,0:T(8,128)} %bitcast.11), calls=%async_computation | async-start | bytes 393216 | tf_op jit(solution)/shard_map/all_to_all | solution.py:250
  106.6 10.3 %all-to-all-start.1 = ((f32[4,64,128]{2,1,0:T(8,128)}), f32[4,64,128]{2,1,0:T(8,128)S(1)}, u32[]{:S(2)}, u32[]{:S(2)}) async-start(f32[4,64,128]{2,1,0:T(8,128)} %get-tuple-element.27.sent_ref), calls=%async_computation.1 | async-start | bytes 262144 | tf_op jit(solution)/shard_map/all_to_all | solution.py:252
